TPU v7x, 256 devices: a whole 4x4x8 slice. The times are simulated.
256 devices in a mesh: dp: 16 (over z, y_hi), seq: 8 (over x, core), mp: 2 (over y_lo).
Axes of the slice: x: 4, y: 4 (y_hi: 2, y_lo: 2; y = y_hi * 2 + y_lo), z: 8, core: 2. Of those that a mesh axis runs over, the one named last changes fastest.
Arguments:
- query: bfloat16 [16, 2048, 4096], P('dp', 'seq', 'mp'), may hold values from -60 to 60
- latents: bfloat16 [16, 48, 64, 1280], P('dp', ('seq', 'mp')), may hold values from -6 to 6
- image_slot: int32 [16, 16], P('dp'), may hold values from 0 to 47, as said below
- block_image: int32 [16, 64], P('dp'), may hold values from 0 to 15, as said below
- key_weight: bfloat16 [1280, 2, 2048], P(None, 'mp', 'seq'), may hold values from -0.15625 to 0.15625
- value_weight: bfloat16 [1280, 2, 2048], P(None, 'mp', 'seq'), may hold values from -0.15625 to 0.15625
- gate: float32 [32], P('mp'), may hold values from 0.2 to 2
- cotangent: bfloat16 [16, 2048, 4096], P('dp', 'seq', 'mp'), may hold values from -6 to 6
Outputs:
- attended: bfloat16 [16, 2048, 4096], P('dp', 'seq', 'mp')
- query_grad: bfloat16 [16, 2048, 4096], P('dp', 'seq', 'mp')
- key_grad: float32 [1280, 2, 2048], P('dp', 'mp', 'seq')
- value_grad: float32 [1280, 2, 2048], P('dp', 'mp', 'seq')
Inputs may be any that keep to these rules, and one draw needn't show every extreme that they name: `image_slot`: within a document the images sit in distinct slots; each vision device (slots k * 3 to (k + 1) * 3 - 1) holds at most 3 of them, and some device holds exactly 3. `block_image`: within a document it never falls from one text block to the next, starts at 0, and names every one of the 16 images.
All inputs are finite; a program needn't handle non-finite values.
Results may differ from a plain program's by a relative error of at most 0.02.
The roundings to bfloat16 on the way count: a program that leaves them out, or rounds other values in their place, can miss the bound.
Values may be sent and summed in bfloat16 or wider, within the bound.
No kernel may reach another device: no remote copies, remote signals or barrier semaphores. Data moves between devices by JAX's collectives and lax.ppermute only.
A program may use at most 128 MiB of HBM per device.

v0:
```python
import math

import jax
import jax.numpy as jnp
from jax import lax
from jax.experimental import pallas as pl
from jax.experimental.pallas import tpu as pltpu
from jax.sharding import PartitionSpec as P

F32, BF16 = jnp.float32, jnp.bfloat16
IMAGES, LAT, HD, TB, UNROLL = 16, 64, 128, 32, 8
PIECES = 8
ROWS = LAT // PIECES
VMEM = pl.BlockSpec(memory_space=pltpu.VMEM)
ANY = pl.BlockSpec(memory_space=pl.ANY)
SMEM = pl.BlockSpec(memory_space=pltpu.SMEM)


def dot(a, b):
    return jnp.dot(a, b, preferred_element_type=F32)


def dot_t(a, b):
    return lax.dot_general(a, b, (((0,), (0,)), ((), ())), preferred_element_type=F32)


def fused_kernel(
    info, blk, gain, wk, wv, *refs
):
    far_parts, far_tok, (oc, send, keep) = refs[:4], refs[4:14], refs[14:17]
    (kz, vz, kzt, vzt, acck, accv, ki, gs), parts, toks, made, sems = refs[17:25], refs[25:29], refs[29:31], *refs[31:33]
    ss, pgs, lows, sgs = refs[33:]
    a0, b0, a1, b1 = parts
    moves = list(zip(far_parts, parts))
    for r in range(8):
        for j in range(2):
            src = far_tok[5 * j + r].at[0] if r < 4 else far_tok[5 * j + 4].at[r - 4]
            moves.append((src, toks[j].at[r]))
    loads = [pltpu.make_async_copy(x, y, sems.at[n]) for n, (x, y) in enumerate(moves)]
    for x in loads:
        x.start()
    scale = 1.0 / math.sqrt(HD)
    c2 = scale * math.log2(math.e)
    me, m, odd = info[0], info[1], info[2]
    span = IMAGES * ROWS
    half = a0.shape[2]
    w_own = pl.ds(pl.multiple_of(m * half, half), half)
    w_other = pl.ds(pl.multiple_of((1 - m) * half, half), half)
    for n, (a, b) in enumerate(((a0, b0), (a1, b1))):
        loads[2 * n].wait()
        loads[2 * n + 1].wait()
        x, y = a[...].reshape(4 * span, half), b[...].reshape(4 * span, half)
        rows = slice(n * 4 * span, (n + 1) * 4 * span)
        acck[rows, :] = dot(x, wk[w_own, :]) + dot(y, wk[w_other, :])
        accv[rows, :] = dot(x, wv[w_own, :]) + dot(y, wv[w_other, :])
    zero = jnp.zeros((LAT, HD), F32)
    for i in range(IMAGES):
        for src, plain, turned in ((acck, kz, kzt), (accv, vz, vzt)):
            x = jnp.concatenate(
                [src[p * span + i * ROWS : p * span + (i + 1) * ROWS, :] for p in range(PIECES)], axis=0
            )
            top = jnp.concatenate([x[:, :HD], zero], axis=1)
            low = jnp.concatenate([zero, x[:, HD:]], axis=1)
            both = jnp.concatenate([top, low], axis=0)
            plain[i] = both.astype(BF16)
            turned[i] = both.T.astype(BF16)
    acck[...] = jnp.zeros_like(acck)
    accv[...] = jnp.zeros_like(accv)
    g = gain[...]
    first = lax.broadcasted_iota(jnp.int32, (TB * UNROLL, 2 * LAT), 1) < LAT
    tokens = TB * UNROLL

    ones = lax.broadcasted_iota(jnp.int32, (2 * LAT, 2 * LAT), 0) // LAT
    ones = (ones == lax.broadcasted_iota(jnp.int32, (2 * LAT, 2 * LAT), 1) // LAT).astype(BF16)

    def half_max(x):
        a = jnp.max(jnp.where(first, x, -jnp.inf), axis=1, keepdims=True)
        b = jnp.max(jnp.where(first, -jnp.inf, x), axis=1, keepdims=True)
        return jnp.where(first, a, b)

    def half_sum(x):
        high = x.astype(BF16)
        low = (x - high.astype(F32)).astype(BF16)
        return dot(high, ones) + dot(low, ones)

    for x in loads[4:]:
        x.wait()

    at = [slice(u * TB, (u + 1) * TB) for u in range(UNROLL)]

    def owner(r):
        return lax.rem(me // 2 + 4 - r % 4, 4) * 2 + lax.rem(me + r // 4, 2)

    def images(r):
        return [blk[owner(r) * UNROLL + u] for u in range(UNROLL)]

    def scores(r):
        img = images(r)
        toks[1][r] = (toks[1][r].astype(F32) * g).astype(BF16)
        for rows, mats, out in ((toks[0], kzt, ss), (toks[1], vzt, pgs)):
            for u in range(0, UNROLL, 2):
                pair = jnp.concatenate([mats[img[u]], mats[img[u + 1]]], axis=1)
                both = dot(rows[r, u * TB : (u + 2) * TB, :], pair)
                out[r, at[u], :] = both[:TB, : 2 * LAT]
                out[r, at[u + 1], :] = both[TB:, 2 * LAT :]

    def weigh(r):
        s, pg = ss[r], pgs[r]
        e = jnp.exp2((s - half_max(s)) * c2)
        prob = e / half_sum(e)
        lows[r] = prob.astype(BF16)
        delta = half_sum(prob * pg)
        sgs[r] = (prob * (pg - delta) * scale).astype(BF16)

    def collect(r):
        img = images(r)
        for u in range(UNROLL):
            lu, su = lows[r, at[u], :], sgs[r, at[u], :]
            made[r, at[u], :] = (dot(lu, vz[img[u]]) * g).astype(BF16)
            made[r, tokens + u * TB : tokens + (u + 1) * TB, :] = dot(su, kz[img[u]]).astype(BF16)
            kt = dot_t(su, toks[0][r, at[u], :])
            vt = dot_t(lu, toks[1][r, at[u], :])
            rows = pl.ds(pl.multiple_of(img[u] * LAT, LAT), LAT)
            acck[rows, :HD] += kt[:LAT, :HD]
            acck[rows, HD:] += kt[LAT:, HD:]
            accv[rows, :HD] += vt[:LAT, :HD]
            accv[rows, HD:] += vt[LAT:, HD:]

    for step in range(10):
        if step < 8:
            scores(step)
        if 1 <= step < 9:
            weigh(step - 1)
        if step >= 2:
            collect(step - 2)
    stores = [pltpu.make_async_copy(made.at[r], oc.at[owner(r)], sems.at[20 + r]) for r in range(8)]
    for x in stores:
        x.start()
    for p in range(PIECES):
        for acc, lo in ((acck, 0), (accv, 2 * HD)):
            x = jnp.concatenate(
                [acc[i * LAT + p * ROWS : i * LAT + (p + 1) * ROWS, :] for i in range(IMAGES)], axis=0
            )
            ki[p * span : (p + 1) * span, lo : lo + 2 * HD] = x.astype(BF16)
    for near, away, rows in ((a0, a1, w_own), (b0, b1, w_other)):
        n = 4 * span
        total = dot_t(near[...].reshape(n, half), ki[:n, :]) + dot_t(away[...].reshape(n, half), ki[n:, :])
        gs[rows, :] = total.astype(BF16)
    n = send.shape[1]
    for k in range(4):
        send[k] = gs[pl.ds(pl.multiple_of((2 * k + 1 - odd) * n, n), n), :]
        keep[k] = gs[pl.ds(pl.multiple_of((2 * k + odd) * n, n), n), :]
    for x in stores:
        x.wait()


def rotate_kernel(info, q, c, *outs):
    cols = outs[0].shape[2]
    me = info[0]
    for d in range(4):
        for j in range(2):
            to = lax.rem(me // 2 + d, 4) * 2 + lax.rem(me + j, 2)
            off = pl.multiple_of(to * cols, cols)
            outs[d][j] = q[:, pl.ds(off, cols)]
            outs[4 + d][j] = c[:, pl.ds(off, cols)]


def spread_kernel(y, a, b):
    cols = y.shape[3]
    for r in range(8):
        a[:, r * cols : (r + 1) * cols] = y[r, 0]
        b[:, r * cols : (r + 1) * cols] = y[r, 1]


def swap(x, axes, pairs):
    return lax.ppermute(x, axes, pairs)


def exchange(x, axes, **kw):
    return lax.all_to_all(x, axes, split_axis=0, concat_axis=0, tiled=True, **kw)


def body(query, latents, image_slot, block_image, key_weight, value_weight, gate, cotangent):
    seq_i, mp_i, dp_i = lax.axis_index("seq"), lax.axis_index("mp"), lax.axis_index("dp")
    tokens, width = query.shape[1], query.shape[2]
    kv = latents.shape[3]
    n_seq = 8
    cols = width // n_seq
    slots = latents.shape[1]
    half = kv // 2
    shape = jax.ShapeDtypeStruct
    info = jnp.stack([seq_i, mp_i, dp_i // 2 % 2]).astype(jnp.int32)
    cut = latents[0].reshape(slots, PIECES, ROWS, 2, half).transpose(1, 3, 0, 2, 4)
    got = exchange(cut.reshape(16, slots * ROWS, half), ("seq", "mp"))

    def along_x(x, d):
        return swap(x, "seq", [(i * 2 + k, (i + d) % 4 * 2 + k) for i in range(4) for k in range(2)])

    def across_y(x):
        return swap(x, "mp", [(0, 1), (1, 0)])

    def sibling(x):
        return swap(x, "seq", [(j, j ^ 1) for j in range(8)])

    turned = pl.pallas_call(
        rotate_kernel,
        out_shape=[shape((2, tokens, cols), BF16)] * 8,
        in_specs=[SMEM, VMEM, VMEM],
        out_specs=[VMEM] * 8,
        name="rotate",
    )(info, query[0], cotangent[0])
    q_in = [turned[0]] + [along_x(turned[d], d) for d in range(1, 4)]
    got, q_in[1], q_in[3] = lax.optimization_barrier((got, q_in[1], q_in[3]))
    mine = jnp.take(got.reshape(16 * slots, ROWS, half), image_slot[0], axis=0)
    mine = mine.reshape(IMAGES * ROWS, half)
    own = [mine] + [along_x(mine, d) for d in (1, -1, 2)]
    other = [across_y(x) for x in own]
    held, c_out = lax.optimization_barrier((own[1:], turned[4:]))
    c_in = [c_out[0]] + [along_x(c_out[d], d) for d in range(1, 4)]
    q_sib = sibling(jnp.stack([x[1] for x in q_in]))
    other, c_in, q_sib = lax.optimization_barrier((other, c_in, q_sib))
    c_sib = sibling(jnp.stack([x[1] for x in c_in]))
    a0, b0 = jnp.stack(own), jnp.stack(other)
    a1, b1 = sibling(a0), sibling(b0)
    wk, wv = key_weight[:, 0, :], value_weight[:, 0, :]
    n_rows = IMAGES * LAT
    gain = jnp.repeat(jnp.tanh(lax.dynamic_slice_in_dim(gate, seq_i * 2, 2)), HD)[None, :]
    rows = kv // 16
    halves = shape((4, 2 * rows, 4 * HD), BF16)
    zs, zt = (IMAGES, 2 * LAT, 2 * HD), (IMAGES, 2 * HD, 2 * LAT)
    oc, send, keep = pl.pallas_call(
        fused_kernel,
        out_shape=(shape((n_seq, 2 * tokens, cols), BF16), halves, halves),
        in_specs=[SMEM, SMEM] + [VMEM] * 3 + [ANY] * 14,
        out_specs=(ANY, VMEM, VMEM),
        scratch_shapes=[pltpu.VMEM(x, BF16) for x in (zs, zs, zt, zt)]
        + [pltpu.VMEM((n_rows, 2 * HD), F32)] * 2
        + [pltpu.VMEM((n_rows, 4 * HD), BF16), pltpu.VMEM((kv, 4 * HD), BF16)]
        + [pltpu.VMEM(a0.shape, BF16)] * 4
        + [pltpu.VMEM((n_seq, tokens, cols), BF16)] * 2
        + [pltpu.VMEM((n_seq, 2 * tokens, cols), BF16), pltpu.SemaphoreType.DMA((28,))]
        + [pltpu.VMEM((n_seq, tokens, 2 * LAT), x) for x in (F32, F32, BF16, BF16)],
        compiler_params=pltpu.CompilerParams(vmem_limit_bytes=26 * 2**20),
        cost_estimate=pl.CostEstimate(
            flops=2**33, bytes_accessed=16 * 2**20, transcendentals=2**19
        ),
        name="fused",
    )(info, block_image[0], gain, wk, wv, a0, b0, a1, b1, *q_in, q_sib, *c_in, c_sib)

    flat_out = shape((tokens, width), BF16)
    attended, query_grad = pl.pallas_call(
        spread_kernel,
        grid=(tokens // 64,),
        out_shape=(flat_out, flat_out),
        in_specs=[pl.BlockSpec((n_seq, 2, 64, cols), lambda t: (0, 0, t, 0))],
        out_specs=[pl.BlockSpec((64, width), lambda t: (t, 0))] * 2,
        name="spread",
    )(exchange(oc, "seq").reshape(n_seq, 2, tokens, cols))

    z_i, h_i = dp_i // 2, dp_i % 2
    pairs = []
    for z in range(8):
        for h in range(2):
            for s in range(8):
                if s % 2 == 0:
                    to = z ^ 1
                else:
                    to = (z + 1) % 8 if z % 2 else (z - 1) % 8
                pairs.append(((z * 2 + h) * 8 + s, (to * 2 + h) * 8 + s))

    def pick(x, i, axis):
        return lax.dynamic_index_in_dim(x, i, axis, keepdims=False)

    def join(x, y):
        return (x.astype(F32) + y.astype(F32)).astype(BF16)

    part = join(keep, swap(send, ("dp", "seq"), pairs)).reshape(4, 2, rows, 4 * HD)
    part = join(pick(part, h_i, 1), swap(pick(part, 1 - h_i, 1), "dp", [(j, j ^ 1) for j in range(16)]))
    k_i = z_i // 2
    more = []
    for r in range(1, 4):
        perm = [(z * 2 + h, (z + 2 * r) % 8 * 2 + h) for z in range(8) for h in range(2)]
        more.append(swap(pick(part, (k_i + r) % 4, 0), "dp", perm))
    (attended, query_grad), more = lax.optimization_barrier(((attended, query_grad), more))
    total = pick(part, k_i, 0).astype(F32)
    for x in more:
        total = total + x.astype(F32)
    key_grad = total[:, : 2 * HD].reshape(rows, 1, 2 * HD)
    value_grad = total[:, 2 * HD :].reshape(rows, 1, 2 * HD)
    return attended[None], query_grad[None], key_grad, value_grad


def solution(mesh):
    in_specs = (
        P("dp", "seq", "mp"),
        P("dp", ("seq", "mp"), None, None),
        P("dp", None),
        P("dp", None),
        P(None, "mp", "seq"),
        P(None, "mp", "seq"),
        P("mp"),
        P("dp", "seq", "mp"),
    )
    out_specs = (
        P("dp", "seq", "mp"),
        P("dp", "seq", "mp"),
        P("dp", "mp", "seq"),
        P("dp", "mp", "seq"),
    )
    return jax.shard_map(body, mesh=mesh, in_specs=in_specs, out_specs=out_specs, check_vma=False)
```

profile of v0, /device:TPU:38, one launch (start us, length us, event | category | flops | bytes accessed | tf_op | source)
XLA Modules:
  0.0 125.2 jit_solution(14347475810213614764)
XLA Ops:
  0.6 1.1 reshape_squeeze.3
  1.8 0.8 copy.14
  2.6 5.8 %all-to-all-start = ((bf16[16,24,640]{2,1,0:T(8,128)(2,1)}), bf16[16,24,640]{2,1,0:T(8,128)(2,1)S(1)}, u32[]{:S(2)}, u32[]{:S(2)}) async-start(bf16[16,24,640]{2,1,0:T(8,128)(2,1)} %bitcast.9), calls=%async_computation | async-start | bytes 983040 | tf_op jit(solution)/shard_map/all_to_all | solution.py:180
  8.5 0.6 pad_add_fusion.info
  9.1 3.2 %rotate.1 = (bf16[2,256,256]{2,1,0:T(8,128)(2,1)}, bf16[2,256,256]{2,1,0:T(8,128)(2,1)}, bf16[2,256,256]{2,1,0:T(8,128)(2,1)}, bf16[2,256,256]{2,1,0:T(8,128)(2,...) custom-call(s32[3]{0:T(128)} %pad_add_fusion.info, ...), custom_call_target="tpu_custom_call" | custom-call | tf_op jit(solution)/shard_map/rotate/pallas_call | solution.py:205
  12.3 1.9 %collective-permute-start.1 = (bf16[2,256,256]{2,1,0:T(8,128)(2,1)}, bf16[2,256,256]{2,1,0:T(8,128)(2,1)S(1)}, u32[]{:S(2)}, u32[]{:S(2)}) collective-permute-start(bf16[2,256,256]{2,1,0:T(8,128)(2,1)} %get-tuple-element.39), channel_id=1, source_target_pairs={{0,12},{2,14},{4,0},{6,2},{8,4},{10,6},{12,8},{14,10},{1,13},{3,15... | collective-permute-start | bytes 786440 | tf_op jit(solution)/shard_map/ppermute | solution.py:176
  14.2 1.5 %collective-permute-start.12 = (bf16[2,256,256]{2,1,0:T(8,128)(2,1)}, bf16[2,256,256]{2,1,0:T(8,128)(2,1)S(1)}, u32[]{:S(2)}, u32[]{:S(2)}) collective-permute-start(bf16[2,256,256]{2,1,0:T(8,128)(2,1)} %get-tuple-element.51), channel_id=1, source_target_pairs={{0,8},{2,10},{4,12},{6,14},{8,0},{10,2},{12,4},{14,6},{1,9},{3,11}... | collective-permute-start | bytes 786440 | tf_op jit(solution)/shard_map/ppermute | solution.py:176
  15.9 5.9 %collective-permute-done.refs_5_ = bf16[2,256,256]{2,1,0:T(8,128)(2,1)S(1)} collective-permute-done((bf16[2,256,256]{2,1,0:T(8,128)(2,1)}, bf16[2,256,256]{2,1,0:T(8,128)(2,1)S(1)}, u32[]{:S(2)}, u32[]{:S(2)}) %collective-permute-start) | collective-permute-done | bytes 262176 | tf_op jit(solution)/shard_map/ppermute | solution.py:176
  21.8 7.6 %collective-permute-done.1.refs_7_ = bf16[2,256,256]{2,1,0:T(8,128)(2,1)S(1)} collective-permute-done((bf16[2,256,256]{2,1,0:T(8,128)(2,1)}, bf16[2,256,256]{2,1,0:T(8,128)(2,1)S(1)}, u32[]{:S(2)}, u32[]{:S(2)}) %collective-permute-start.1) | collective-permute-done | bytes 262176 | tf_op jit(solution)/shard_map/ppermute | solution.py:176
  29.5 0.6 gather_fusion
  30.4 0.9 slice.30
  31.3 2.2 %collective-permute-start.5 = (bf16[128,640]{1,0:T(8,128)(2,1)S(1)}, bf16[128,640]{1,0:T(8,128)(2,1)S(1)}, u32[]{:S(2)}, u32[]{:S(2)}) collective-permute-start(bf16[128,640]{1,0:T(8,128)(2,1)S(1)} %bitcast_select_fusion), channel_id=1, source_target_pairs={{0,1},{1,0},{2,3},{3,2},{4,5},{5,4},{6,7},{7,6},{8,9},{9,8},{10,11... | collective-permute-start | bytes 491528 | tf_op jit(solution)/shard_map/ppermute | solution.py:176
  33.5 2.9 %collective-permute-start.2 = (bf16[128,640]{1,0:T(8,128)(2,1)S(1)}, bf16[128,640]{1,0:T(8,128)(2,1)S(1)}, u32[]{:S(2)}, u32[]{:S(2)}) collective-permute-start(bf16[128,640]{1,0:T(8,128)(2,1)S(1)} %bitcast_select_fusion), channel_id=1, source_target_pairs={{0,4},{2,6},{4,8},{6,10},{8,12},{10,14},{12,0},{14,2},{1,5},{3,7},... | collective-permute-start | bytes 491528 | tf_op jit(solution)/shard_map/ppermute | solution.py:176
  36.4 0.8 collective-permute-done.4
  37.2 1.8 %collective-permute-start.8 = (bf16[128,640]{1,0:T(8,128)(2,1)S(1)}, bf16[128,640]{1,0:T(8,128)(2,1)S(1)}, u32[]{:S(2)}, u32[]{:S(2)}) collective-permute-start(bf16[128,640]{1,0:T(8,128)(2,1)S(1)} %collective-permute-done.4), channel_id=1, source_target_pairs={{0,1},{1,0},{2,3},{3,2},{4,5},{5,4},{6,7},{7,6},{8,9},{9,8},{10,11... | collective-permute-start | bytes 491528 | tf_op jit(solution)/shard_map/ppermute | solution.py:176
  39.0 1.4 %collective-permute-start.7 = (bf16[128,640]{1,0:T(8,128)(2,1)S(1)}, bf16[128,640]{1,0:T(8,128)(2,1)S(1)}, u32[]{:S(2)}, u32[]{:S(2)}) collective-permute-start(bf16[128,640]{1,0:T(8,128)(2,1)S(1)} %collective-permute-done.3), channel_id=1, source_target_pairs={{0,1},{1,0},{2,3},{3,2},{4,5},{5,4},{6,7},{7,6},{8,9},{9,8},{10,11... | collective-permute-start | bytes 491528 | tf_op jit(solution)/shard_map/ppermute | solution.py:176
  40.6 2.3 %collective-permute-start.9 = (bf16[2,256,256]{2,1,0:T(8,128)(2,1)}, bf16[2,256,256]{2,1,0:T(8,128)(2,1)S(1)}, u32[]{:S(2)}, u32[]{:S(2)}) collective-permute-start(bf16[2,256,256]{2,1,0:T(8,128)(2,1)} %get-tuple-element.46), channel_id=1, source_target_pairs={{0,4},{2,6},{4,8},{6,10},{8,12},{10,14},{12,0},{14,2},{1,5},{3,7},... | collective-permute-start | bytes 786440 | tf_op jit(solution)/shard_map/ppermute | solution.py:176
  42.9 1.0 collective-permute-start.10
  44.0 0.3 collective-permute-done.7
  44.3 1.9 %collective-permute-start.6 = (bf16[128,640]{1,0:T(8,128)(2,1)S(1)}, bf16[128,640]{1,0:T(8,128)(2,1)S(1)}, u32[]{:S(2)}, u32[]{:S(2)}) collective-permute-start(bf16[128,640]{1,0:T(8,128)(2,1)S(1)} %collective-permute-done.2), channel_id=1, source_target_pairs={{0,1},{1,0},{2,3},{3,2},{4,5},{5,4},{6,7},{7,6},{8,9},{9,8},{10,11... | collective-permute-start | bytes 491528 | tf_op jit(solution)/shard_map/ppermute | solution.py:176
  46.4 3.2 %collective-permute-done.6 = bf16[128,640]{1,0:T(8,128)(2,1)S(1)} collective-permute-done((bf16[128,640]{1,0:T(8,128)(2,1)S(1)}, bf16[128,640]{1,0:T(8,128)(2,1)S(1)}, u32[]{:S(2)}, u32[]{:S(2)}) %collective-permute-start.6) | collective-permute-done | bytes 163872 | tf_op jit(solution)/shard_map/ppermute | solution.py:176
  49.6 0.4 collective-permute-done.9.refs_10_
  50.0 3.9 %collective-permute-done.10.refs_11_ = bf16[2,256,256]{2,1,0:T(8,128)(2,1)S(1)} collective-permute-done((bf16[2,256,256]{2,1,0:T(8,128)(2,1)}, bf16[2,256,256]{2,1,0:T(8,128)(2,1)S(1)}, u32[]{:S(2)}, u32[]{:S(2)}) %collective-permute-start.10) | collective-permute-done | bytes 262176 | tf_op jit(solution)/shard_map/ppermute | solution.py:176
  53.9 3.3 %collective-permute-done.11.refs_12_ = bf16[2,256,256]{2,1,0:T(8,128)(2,1)S(1)} collective-permute-done((bf16[2,256,256]{2,1,0:T(8,128)(2,1)S(1)}, bf16[2,256,256]{2,1,0:T(8,128)(2,1)S(1)}, u32[]{:S(2)}, u32[]{:S(2)}) %collective-permute-start.11) | collective-permute-done | bytes 262176 | tf_op jit(solution)/shard_map/ppermute | solution.py:176
  57.2 0.8 copy-done.11
  58.3 0.9 pad_maximum_fusion.3
  59.2 0.5 collective-permute-start.16
  59.8 1.8 %collective-permute-done.16.refs_13_ = bf16[4,256,256]{2,1,0:T(8,128)(2,1)} collective-permute-done((bf16[4,256,256]{2,1,0:T(8,128)(2,1)}, bf16[4,256,256]{2,1,0:T(8,128)(2,1)}, u32[]{:S(2)}, u32[]{:S(2)}) %collective-permute-start.16) | collective-permute-done | bytes 524320 | tf_op jit(solution)/shard_map/ppermute | solution.py:176
  61.6 0.9 copy-done.3
  62.6 0.9 copy-done.5
  63.5 1.1 copy-done.7
  64.6 1.1 copy-done.8
  65.7 1.0 copy-done.12
  66.8 12.7 %fused.1 = (bf16[8,512,256]{2,1,0:T(8,128)(2,1)}, bf16[4,160,512]{2,1,0:T(8,128)(2,1)S(1)}, bf16[4,160,512]{2,1,0:T(8,128)(2,1)S(1)}) custom-call(s32[3]{0:T(128)S(1)} %copy-done.6, s32[64]{0:T(128)S(1)} %bitcast.53, f32[1,256]{1,0:T(1,128)S(1)} %bitcast.54, bf16[1280,256]{1,0:T(8,128)(2,1)S(1)} %bitcast.51, bf16[1280,256]{1,0:T(8,128)(2,1)S(1)} %bitcast.52, ...), custom_call_target="tpu_custom_call" | custom-call | flops 8589934592 | bytes 16777216 | tf_op jit(solution)/shard_map/fused/pallas_call | solution.py:231
  79.5 0.8 copy-done.9
  80.3 5.1 %all-to-all-start.1 = ((bf16[8,512,256]{2,1,0:T(8,128)(2,1)}), bf16[8,512,256]{2,1,0:T(8,128)(2,1)}, u32[]{:S(2)}, u32[]{:S(2)}) async-start(bf16[8,512,256]{2,1,0:T(8,128)(2,1)} %get-tuple-element.62), calls=%async_computation.1 | async-start | bytes 4194304 | tf_op jit(solution)/shard_map/all_to_all | solution.py:180
  85.5 10.5 %collective-permute-done.17 = bf16[4,160,512]{2,1,0:T(8,128)(2,1)S(1)} collective-permute-done((bf16[4,160,512]{2,1,0:T(8,128)(2,1)S(1)}, bf16[4,160,512]{2,1,0:T(8,128)(2,1)S(1)}, u32[]{:S(2)}, u32[]{:S(2)}) %collective-permute-start.17) | collective-permute-done | bytes 655392 | tf_op jit(solution)/shard_map/ppermute | solution.py:176
  96.0 0.2 add_convert_fusion
  96.2 3.0 %collective-permute-start.18 = (bf16[4,80,512]{2,1,0:T(8,128)(2,1)S(1)}, bf16[4,80,512]{2,1,0:T(8,128)(2,1)S(1)}, u32[]{:S(2)}, u32[]{:S(2)}) collective-permute-start(bf16[4,80,512]{2,1,0:T(8,128)(2,1)S(1)} %dynamic-slice_bitcast_fusion), channel_id=1, source_target_pairs={{0,16},{16,0},{32,48},{48,32},{64,80},{80,64},{96,112},{112,96},{1... | collective-permute-start | bytes 983048 | tf_op jit(solution)/shard_map/ppermute | solution.py:176
  99.2 7.8 %collective-permute-done.18 = bf16[4,80,512]{2,1,0:T(8,128)(2,1)S(1)} collective-permute-done((bf16[4,80,512]{2,1,0:T(8,128)(2,1)S(1)}, bf16[4,80,512]{2,1,0:T(8,128)(2,1)S(1)}, u32[]{:S(2)}, u32[]{:S(2)}) %collective-permute-start.18) | collective-permute-done | bytes 327712 | tf_op jit(solution)/shard_map/ppermute | solution.py:176
  107.1 6.5 %collective-permute-start.21 = (bf16[80,512]{1,0:T(8,128)(2,1)S(1)}, bf16[80,512]{1,0:T(8,128)(2,1)S(1)}, u32[]{:S(2)}, u32[]{:S(2)}) collective-permute-start(bf16[80,512]{1,0:T(8,128)(2,1)S(1)} %get-tuple-element.72), channel_id=1, source_target_pairs={{0,192},{16,208},{32,224},{48,240},{64,0},{80,16},{96,32},{112,48}... | collective-permute-start | bytes 245768 | tf_op jit(solution)/shard_map/ppermute | solution.py:176
  113.6 1.6 %collective-permute-start.20 = (bf16[80,512]{1,0:T(8,128)(2,1)S(1)}, bf16[80,512]{1,0:T(8,128)(2,1)S(1)}, u32[]{:S(2)}, u32[]{:S(2)}) collective-permute-start(bf16[80,512]{1,0:T(8,128)(2,1)S(1)} %get-tuple-element.73), channel_id=1, source_target_pairs={{0,128},{16,144},{32,160},{48,176},{64,192},{80,208},{96,224},{112... | collective-permute-start | bytes 245768 | tf_op jit(solution)/shard_map/ppermute | solution.py:176
  115.2 1.0 collective-permute-start.19
  116.2 3.8 %spread.1 = (bf16[256,2048]{1,0:T(8,128)(2,1)}, bf16[256,2048]{1,0:T(8,128)(2,1)}) custom-call(bf16[8,2,256,256]{3,2,1,0:T(8,128)(2,1)} %bitcast.24.y), custom_call_target="tpu_custom_call" | custom-call | tf_op jit(solution)/shard_map/spread/pallas_call | solution.py:251
  120.0 3.6 %collective-permute-done.20 = bf16[80,512]{1,0:T(8,128)(2,1)S(1)} collective-permute-done((bf16[80,512]{1,0:T(8,128)(2,1)S(1)}, bf16[80,512]{1,0:T(8,128)(2,1)S(1)}, u32[]{:S(2)}, u32[]{:S(2)}) %collective-permute-start.20) | collective-permute-done | bytes 81952 | tf_op jit(solution)/shard_map/ppermute | solution.py:176
  123.6 0.2 collective-permute-done.19
  123.9 0.7 reshape.104
  124.6 0.7 reshape.103
  (70 shorter events, 1.7 us)
Async XLA Ops:
  2.6 26.9 %all-to-all-start = ((bf16[16,24,640]{2,1,0:T(8,128)(2,1)}), bf16[16,24,640]{2,1,0:T(8,128)(2,1)S(1)}, u32[]{:S(2)}, u32[]{:S(2)}) async-start(bf16[16,24,640]{2,1,0:T(8,128)(2,1)} %bitcast.9), calls=%async_computation | async-start | bytes 983040 | tf_op jit(solution)/shard_map/all_to_all | solution.py:180
  8.4 7.3 %copy-start.15 = (s32[1,16]{1,0:T(1,128)S(1)}, s32[1,16]{1,0:T(1,128)}, u32[]{:S(2)}) copy-start(s32[1,16]{1,0:T(1,128)} %param.10) | copy-start | bytes 196
  12.2 9.6 %collective-permute-start = (bf16[2,256,256]{2,1,0:T(8,128)(2,1)}, bf16[2,256,256]{2,1,0:T(8,128)(2,1)S(1)}, u32[]{:S(2)}, u32[]{:S(2)}) collective-permute-start(bf16[2,256,256]{2,1,0:T(8,128)(2,1)} %get-tuple-element.38), channel_id=1, source_target_pairs={{0,4},{2,6},{4,8},{6,10},{8,12},{10,14},{12,0},{14,2},{1,5},{3,7},... | collective-permute-start | bytes 786440 | tf_op jit(solution)/shard_map/ppermute | solution.py:176
  12.3 17.2 %collective-permute-start.1 = (bf16[2,256,256]{2,1,0:T(8,128)(2,1)}, bf16[2,256,256]{2,1,0:T(8,128)(2,1)S(1)}, u32[]{:S(2)}, u32[]{:S(2)}) collective-permute-start(bf16[2,256,256]{2,1,0:T(8,128)(2,1)} %get-tuple-element.39), channel_id=1, source_target_pairs={{0,12},{2,14},{4,0},{6,2},{8,4},{10,6},{12,8},{14,10},{1,13},{3,15... | collective-permute-start | bytes 786440 | tf_op jit(solution)/shard_map/ppermute | solution.py:176
  14.2 17.0 %collective-permute-start.12 = (bf16[2,256,256]{2,1,0:T(8,128)(2,1)}, bf16[2,256,256]{2,1,0:T(8,128)(2,1)S(1)}, u32[]{:S(2)}, u32[]{:S(2)}) collective-permute-start(bf16[2,256,256]{2,1,0:T(8,128)(2,1)} %get-tuple-element.51), channel_id=1, source_target_pairs={{0,8},{2,10},{4,12},{6,14},{8,0},{10,2},{12,4},{14,6},{1,9},{3,11}... | collective-permute-start | bytes 786440 | tf_op jit(solution)/shard_map/ppermute | solution.py:176
  30.1 13.9 %copy-start.14 = (bf16[2,256,256]{2,1,0:T(8,128)(2,1)S(1)}, bf16[2,256,256]{2,1,0:T(8,128)(2,1)}, u32[]{:S(2)}) copy-start(bf16[2,256,256]{2,1,0:T(8,128)(2,1)} %get-tuple-element.48) | copy-start | bytes 786436
  30.2 7.0 %collective-permute-start.4 = (bf16[128,640]{1,0:T(8,128)(2,1)S(1)}, bf16[128,640]{1,0:T(8,128)(2,1)S(1)}, u32[]{:S(2)}, u32[]{:S(2)}) collective-permute-start(bf16[128,640]{1,0:T(8,128)(2,1)S(1)} %bitcast_select_fusion), channel_id=1, source_target_pairs={{0,8},{2,10},{4,12},{6,14},{8,0},{10,2},{12,4},{14,6},{1,9},{3,11}... | collective-permute-start | bytes 491528 | tf_op jit(solution)/shard_map/ppermute | solution.py:176
  30.3 8.7 %collective-permute-start.3 = (bf16[128,640]{1,0:T(8,128)(2,1)S(1)}, bf16[128,640]{1,0:T(8,128)(2,1)S(1)}, u32[]{:S(2)}, u32[]{:S(2)}) collective-permute-start(bf16[128,640]{1,0:T(8,128)(2,1)S(1)} %bitcast_select_fusion), channel_id=1, source_target_pairs={{0,12},{2,14},{4,0},{6,2},{8,4},{10,6},{12,8},{14,10},{1,13},{3,15... | collective-permute-start | bytes 491528 | tf_op jit(solution)/shard_map/ppermute | solution.py:176
  31.3 11.6 %collective-permute-start.5 = (bf16[128,640]{1,0:T(8,128)(2,1)S(1)}, bf16[128,640]{1,0:T(8,128)(2,1)S(1)}, u32[]{:S(2)}, u32[]{:S(2)}) collective-permute-start(bf16[128,640]{1,0:T(8,128)(2,1)S(1)} %bitcast_select_fusion), channel_id=1, source_target_pairs={{0,1},{1,0},{2,3},{3,2},{4,5},{5,4},{6,7},{7,6},{8,9},{9,8},{10,11... | collective-permute-start | bytes 491528 | tf_op jit(solution)/shard_map/ppermute | solution.py:176
  33.5 7.1 %collective-permute-start.2 = (bf16[128,640]{1,0:T(8,128)(2,1)S(1)}, bf16[128,640]{1,0:T(8,128)(2,1)S(1)}, u32[]{:S(2)}, u32[]{:S(2)}) collective-permute-start(bf16[128,640]{1,0:T(8,128)(2,1)S(1)} %bitcast_select_fusion), channel_id=1, source_target_pairs={{0,4},{2,6},{4,8},{6,10},{8,12},{10,14},{12,0},{14,2},{1,5},{3,7},... | collective-permute-start | bytes 491528 | tf_op jit(solution)/shard_map/ppermute | solution.py:176
  37.2 6.8 %collective-permute-start.8 = (bf16[128,640]{1,0:T(8,128)(2,1)S(1)}, bf16[128,640]{1,0:T(8,128)(2,1)S(1)}, u32[]{:S(2)}, u32[]{:S(2)}) collective-permute-start(bf16[128,640]{1,0:T(8,128)(2,1)S(1)} %collective-permute-done.4), channel_id=1, source_target_pairs={{0,1},{1,0},{2,3},{3,2},{4,5},{5,4},{6,7},{7,6},{8,9},{9,8},{10,11... | collective-permute-start | bytes 491528 | tf_op jit(solution)/shard_map/ppermute | solution.py:176
  39.0 5.3 %collective-permute-start.7 = (bf16[128,640]{1,0:T(8,128)(2,1)S(1)}, bf16[128,640]{1,0:T(8,128)(2,1)S(1)}, u32[]{:S(2)}, u32[]{:S(2)}) collective-permute-start(bf16[128,640]{1,0:T(8,128)(2,1)S(1)} %collective-permute-done.3), channel_id=1, source_target_pairs={{0,1},{1,0},{2,3},{3,2},{4,5},{5,4},{6,7},{7,6},{8,9},{9,8},{10,11... | collective-permute-start | bytes 491528 | tf_op jit(solution)/shard_map/ppermute | solution.py:176
  40.5 16.7 %collective-permute-start.13 = (bf16[4,256,256]{2,1,0:T(8,128)(2,1)S(1)}, bf16[4,256,256]{2,1,0:T(8,128)(2,1)S(1)}, u32[]{:S(2)}, u32[]{:S(2)}) collective-permute-start(bf16[4,256,256]{2,1,0:T(8,128)(2,1)S(1)} %pad_maximum_fusion.2), channel_id=1, source_target_pairs={{0,2},{2,0},{4,6},{6,4},{8,10},{10,8},{12,14},{14,12},{1,3},{3,1},... | collective-permute-start | bytes 1572872 | tf_op jit(solution)/shard_map/ppermute | solution.py:176
  40.6 9.4 %collective-permute-start.9 = (bf16[2,256,256]{2,1,0:T(8,128)(2,1)}, bf16[2,256,256]{2,1,0:T(8,128)(2,1)S(1)}, u32[]{:S(2)}, u32[]{:S(2)}) collective-permute-start(bf16[2,256,256]{2,1,0:T(8,128)(2,1)} %get-tuple-element.46), channel_id=1, source_target_pairs={{0,4},{2,6},{4,8},{6,10},{8,12},{10,14},{12,0},{14,2},{1,5},{3,7},... | collective-permute-start | bytes 786440 | tf_op jit(solution)/shard_map/ppermute | solution.py:176
  42.9 11.0 %collective-permute-start.10 = (bf16[2,256,256]{2,1,0:T(8,128)(2,1)}, bf16[2,256,256]{2,1,0:T(8,128)(2,1)S(1)}, u32[]{:S(2)}, u32[]{:S(2)}) collective-permute-start(bf16[2,256,256]{2,1,0:T(8,128)(2,1)} %get-tuple-element.47), channel_id=1, source_target_pairs={{0,8},{2,10},{4,12},{6,14},{8,0},{10,2},{12,4},{14,6},{1,9},{3,11}... | collective-permute-start | bytes 786440 | tf_op jit(solution)/shard_map/ppermute | solution.py:176
  44.0 13.2 %collective-permute-start.11 = (bf16[2,256,256]{2,1,0:T(8,128)(2,1)S(1)}, bf16[2,256,256]{2,1,0:T(8,128)(2,1)S(1)}, u32[]{:S(2)}, u32[]{:S(2)}) collective-permute-start(bf16[2,256,256]{2,1,0:T(8,128)(2,1)S(1)} %copy-done.14), channel_id=1, source_target_pairs={{0,12},{2,14},{4,0},{6,2},{8,4},{10,6},{12,8},{14,10},{1,13},{3,15... | collective-permute-start | bytes 786440 | tf_op jit(solution)/shard_map/ppermute | solution.py:176
  44.3 5.3 %collective-permute-start.6 = (bf16[128,640]{1,0:T(8,128)(2,1)S(1)}, bf16[128,640]{1,0:T(8,128)(2,1)S(1)}, u32[]{:S(2)}, u32[]{:S(2)}) collective-permute-start(bf16[128,640]{1,0:T(8,128)(2,1)S(1)} %collective-permute-done.2), channel_id=1, source_target_pairs={{0,1},{1,0},{2,3},{3,2},{4,5},{5,4},{6,7},{7,6},{8,9},{9,8},{10,11... | collective-permute-start | bytes 491528 | tf_op jit(solution)/shard_map/ppermute | solution.py:176
  46.3 12.0 %copy-start.1 = (bf16[2,256,256]{2,1,0:T(8,128)(2,1)S(1)}, bf16[2,256,256]{2,1,0:T(8,128)(2,1)}, u32[]{:S(2)}) copy-start(bf16[2,256,256]{2,1,0:T(8,128)(2,1)} %get-tuple-element.58.refs_9_) | copy-start | bytes 786436
  49.6 10.1 %collective-permute-start.14 = (bf16[4,128,640]{2,1,0:T(8,128)(2,1)S(1)}, bf16[4,128,640]{2,1,0:T(8,128)(2,1)}, u32[]{:S(2)}, u32[]{:S(2)}) collective-permute-start(bf16[4,128,640]{2,1,0:T(8,128)(2,1)S(1)} %pad_maximum_fusion.refs_0_), channel_id=1, source_target_pairs={{0,2},{2,0},{4,6},{6,4},{8,10},{10,8},{12,14},{14,12},{1,3},{3,1},... | collective-permute-start | bytes 1966088 | tf_op jit(solution)/shard_map/ppermute | solution.py:176
  53.9 5.3 %copy-start.2 = (bf16[2,256,256]{2,1,0:T(8,128)(2,1)}, bf16[2,256,256]{2,1,0:T(8,128)(2,1)S(1)}, u32[]{:S(2)}) copy-start(bf16[2,256,256]{2,1,0:T(8,128)(2,1)S(1)} %collective-permute-done.10.refs_11_) | copy-start | bytes 786436
  57.2 2.0 %copy-start.4 = (bf16[2,256,256]{2,1,0:T(8,128)(2,1)}, bf16[2,256,256]{2,1,0:T(8,128)(2,1)S(1)}, u32[]{:S(2)}) copy-start(bf16[2,256,256]{2,1,0:T(8,128)(2,1)S(1)} %collective-permute-done.11.refs_12_) | copy-start | bytes 786436
  57.2 0.8 copy-start.11
  58.1 1.6 %copy-start.16 = (f32[16]{0:T(128)S(1)}, f32[16]{0:T(128)}, u32[]{:S(2)}) copy-start(f32[16]{0:T(128)} %param.14) | copy-start | bytes 196
  58.1 3.5 %copy-start = (bf16[2,256,256]{2,1,0:T(8,128)(2,1)S(1)}, bf16[2,256,256]{2,1,0:T(8,128)(2,1)}, u32[]{:S(2)}) copy-start(bf16[2,256,256]{2,1,0:T(8,128)(2,1)} %get-tuple-element.49.refs_4_) | copy-start | bytes 786436
  58.1 3.5 %copy-start.6 = (s32[3]{0:T(128)S(1)}, s32[3]{0:T(128)}, u32[]{:S(2)}) copy-start(s32[3]{0:T(128)} %pad_add_fusion.info) | copy-start | bytes 40
  58.1 3.5 %copy-start.13 = (s32[1,64]{1,0:T(1,128)S(1)}, s32[1,64]{1,0:T(1,128)}, u32[]{:S(2)}) copy-start(s32[1,64]{1,0:T(1,128)} %param.11) | copy-start | bytes 772
  58.1 3.4 %collective-permute-start.15 = (bf16[4,128,640]{2,1,0:T(8,128)(2,1)S(1)}, bf16[4,128,640]{2,1,0:T(8,128)(2,1)}, u32[]{:S(2)}, u32[]{:S(2)}) collective-permute-start(bf16[4,128,640]{2,1,0:T(8,128)(2,1)S(1)} %pad_maximum_fusion.1.refs_1_), channel_id=1, source_target_pairs={{0,2},{2,0},{4,6},{6,4},{8,10},{10,8},{12,14},{14,12},{1,3},{3,1},... | collective-permute-start | bytes 1966088 | tf_op jit(solution)/shard_map/ppermute | solution.py:176
  59.2 2.4 %collective-permute-start.16 = (bf16[4,256,256]{2,1,0:T(8,128)(2,1)}, bf16[4,256,256]{2,1,0:T(8,128)(2,1)}, u32[]{:S(2)}, u32[]{:S(2)}) collective-permute-start(bf16[4,256,256]{2,1,0:T(8,128)(2,1)} %pad_maximum_fusion.3), channel_id=1, source_target_pairs={{0,2},{2,0},{4,6},{6,4},{8,10},{10,8},{12,14},{14,12},{1,3},{3,1},... | collective-permute-start | bytes 1572872 | tf_op jit(solution)/shard_map/ppermute | solution.py:176
  61.6 1.0 copy-start.3
  62.6 0.9 copy-start.5
  63.5 1.1 copy-start.7
  64.6 1.1 copy-start.8
  65.7 1.0 copy-start.12
  79.4 0.8 copy-start.9
  80.3 5.1 %copy-start.10 = (bf16[4,160,512]{2,1,0:T(8,128)(2,1)S(1)}, bf16[4,160,512]{2,1,0:T(8,128)(2,1)}, u32[]{:S(2)}) copy-start(bf16[4,160,512]{2,1,0:T(8,128)(2,1)} %copy-done.9) | copy-start | bytes 1966084
  80.3 35.9 %all-to-all-start.1 = ((bf16[8,512,256]{2,1,0:T(8,128)(2,1)}), bf16[8,512,256]{2,1,0:T(8,128)(2,1)}, u32[]{:S(2)}, u32[]{:S(2)}) async-start(bf16[8,512,256]{2,1,0:T(8,128)(2,1)} %get-tuple-element.62), calls=%async_computation.1 | async-start | bytes 4194304 | tf_op jit(solution)/shard_map/all_to_all | solution.py:180
  85.4 10.6 %collective-permute-start.17 = (bf16[4,160,512]{2,1,0:T(8,128)(2,1)S(1)}, bf16[4,160,512]{2,1,0:T(8,128)(2,1)S(1)}, u32[]{:S(2)}, u32[]{:S(2)}) collective-permute-start(bf16[4,160,512]{2,1,0:T(8,128)(2,1)S(1)} %copy-done.10), channel_id=1, source_target_pairs={{0,32},{2,226},{4,36},{6,230},{8,40},{10,234},{12,44},{14,238},{16... | collective-permute-start | bytes 1966088 | tf_op jit(solution)/shard_map/ppermute | solution.py:176
  96.2 10.8 %collective-permute-start.18 = (bf16[4,80,512]{2,1,0:T(8,128)(2,1)S(1)}, bf16[4,80,512]{2,1,0:T(8,128)(2,1)S(1)}, u32[]{:S(2)}, u32[]{:S(2)}) collective-permute-start(bf16[4,80,512]{2,1,0:T(8,128)(2,1)S(1)} %dynamic-slice_bitcast_fusion), channel_id=1, source_target_pairs={{0,16},{16,0},{32,48},{48,32},{64,80},{80,64},{96,112},{112,96},{1... | collective-permute-start | bytes 983048 | tf_op jit(solution)/shard_map/ppermute | solution.py:176
  107.1 12.9 %collective-permute-start.21 = (bf16[80,512]{1,0:T(8,128)(2,1)S(1)}, bf16[80,512]{1,0:T(8,128)(2,1)S(1)}, u32[]{:S(2)}, u32[]{:S(2)}) collective-permute-start(bf16[80,512]{1,0:T(8,128)(2,1)S(1)} %get-tuple-element.72), channel_id=1, source_target_pairs={{0,192},{16,208},{32,224},{48,240},{64,0},{80,16},{96,32},{112,48}... | collective-permute-start | bytes 245768 | tf_op jit(solution)/shard_map/ppermute | solution.py:176
  113.6 10.0 %collective-permute-start.20 = (bf16[80,512]{1,0:T(8,128)(2,1)S(1)}, bf16[80,512]{1,0:T(8,128)(2,1)S(1)}, u32[]{:S(2)}, u32[]{:S(2)}) collective-permute-start(bf16[80,512]{1,0:T(8,128)(2,1)S(1)} %get-tuple-element.73), channel_id=1, source_target_pairs={{0,128},{16,144},{32,160},{48,176},{64,192},{80,208},{96,224},{112... | collective-permute-start | bytes 245768 | tf_op jit(solution)/shard_map/ppermute | solution.py:176
  115.2 8.6 %collective-permute-start.19 = (bf16[80,512]{1,0:T(8,128)(2,1)S(1)}, bf16[80,512]{1,0:T(8,128)(2,1)S(1)}, u32[]{:S(2)}, u32[]{:S(2)}) collective-permute-start(bf16[80,512]{1,0:T(8,128)(2,1)S(1)} %get-tuple-element.74), channel_id=1, source_target_pairs={{0,64},{16,80},{32,96},{48,112},{64,128},{80,144},{96,160},{112,17... | collective-permute-start | bytes 245768 | tf_op jit(solution)/shard_map/ppermute | solution.py:176
where the time goes:
time: 126 us; the launch traced here: 125 us
  waiting for transfers between devices  49.3 us (39%)
  starting transfers between devices  41 us (33%)
  Pallas kernels  19.7 us (16%)
  local copies, waits for them, and re-layouts  12.1 us (10%)
  other arithmetic  2.24 us (2%)
    ppermute x22, waiting for transfers between devices, swap(): return lax.ppermute(x, axes, pairs)  49.3 us
    ppermute x22, starting transfers between devices, swap(): return lax.ppermute(x, axes, pairs)  30.1 us
    pallas_call x1, Pallas kernels, body(): pl.pallas_call(fused_kernel, out_shape=(shape((n_seq, 2 * tokens, cols),...  12.7 us
    all_to_all x2, starting transfers between devices, exchange(): lax.all_to_all(x, axes, split_axis=0, concat_axis=0, tiled=True, **kw)  10.9 us
    unnamed x34, local copies, waits for them, and re-layouts  6.8 us
    pallas_call x1, Pallas kernels, body(): pl.pallas_call(spread_kernel, grid=(tokens // 64,), out_shape=(flat_out,...  3.81 us
    pallas_call x1, Pallas kernels, body(): pl.pallas_call(rotate_kernel, out_shape=[shape((2, tokens, cols), BF16)]...  3.16 us
  transfers between devices with their start and end apart: 24, of which 13 were waited for; matrix products, arithmetic and copies ran while one was open for 3% of the time, Pallas kernels for 6%

commit v1 on v0

--- a/solution.py
+++ b/solution.py
@@ -209,14 +209,17 @@
         out_specs=[VMEM] * 8,
         name="rotate",
     )(info, query[0], cotangent[0])
-    q_in = [turned[0]] + [along_x(turned[d], d) for d in range(1, 4)]
+    q_in = [turned[0], along_x(turned[1], 1), None, along_x(turned[3], 3)]
     got, q_in[1], q_in[3] = lax.optimization_barrier((got, q_in[1], q_in[3]))
     mine = jnp.take(got.reshape(16 * slots, ROWS, half), image_slot[0], axis=0)
-    mine = mine.reshape(IMAGES * ROWS, half)
-    own = [mine] + [along_x(mine, d) for d in (1, -1, 2)]
-    other = [across_y(x) for x in own]
-    held, c_out = lax.optimization_barrier((own[1:], turned[4:]))
+    mine, q_far = lax.optimization_barrier((mine.reshape(IMAGES * ROWS, half), turned[2]))
+    moved = [along_x(mine, d) for d in (1, -1, 2)]
+    q_in[2] = along_x(q_far, 2)
+    first = across_y(mine)
+    moved, first, c_out = lax.optimization_barrier((moved, first, turned[4:]))
     c_in = [c_out[0]] + [along_x(c_out[d], d) for d in range(1, 4)]
+    own, other = [mine] + moved, [first] + [across_y(x) for x in moved]
+    q_in, c_in[1:], other[1:] = lax.optimization_barrier((q_in, c_in[1:], other[1:]))
     q_sib = sibling(jnp.stack([x[1] for x in q_in]))
     other, c_in, q_sib = lax.optimization_barrier((other, c_in, q_sib))
     c_sib = sibling(jnp.stack([x[1] for x in c_in]))
@@ -240,7 +243,7 @@
         + [pltpu.VMEM((n_seq, tokens, cols), BF16)] * 2
         + [pltpu.VMEM((n_seq, 2 * tokens, cols), BF16), pltpu.SemaphoreType.DMA((28,))]
         + [pltpu.VMEM((n_seq, tokens, 2 * LAT), x) for x in (F32, F32, BF16, BF16)],
-        compiler_params=pltpu.CompilerParams(vmem_limit_bytes=26 * 2**20),
+        compiler_params=pltpu.CompilerParams(vmem_limit_bytes=60 * 2**20),
         cost_estimate=pl.CostEstimate(
             flops=2**33, bytes_accessed=16 * 2**20, transcendentals=2**19
         ),

time: 126 us -> 120 us (0.952)
  local copies, waits for them, and re-layouts: 12.1 us -> 8.67 us
  starting transfers between devices: 41 us -> 38.7 us
    unnamed x34 -> x32, local copies, waits for them, and re-layouts: 6.8 us -> 2.6 us
    ppermute x22, starting transfers between devices: 30.1 us -> 27.1 us  [swap(): return lax.ppermute(x, axes, pairs)]
  transfers between devices with their start and end apart: 24 -> 24, of which waited for: 13 -> 15; matrix products, arithmetic and copies ran while one was open for 3% -> 2% of each run, Pallas kernels for 6% -> 6%
where the time goes in v1:
time: 120 us; the launch traced here: 119 us
  waiting for transfers between devices  48.2 us (40%)
  starting transfers between devices  38.7 us (32%)
  Pallas kernels  20.3 us (17%)
  local copies, waits for them, and re-layouts  8.67 us (7%)
  other arithmetic  2.43 us (2%)
    ppermute x22, waiting for transfers between devices, swap(): return lax.ppermute(x, axes, pairs)  48.2 us
    ppermute x22, starting transfers between devices, swap(): return lax.ppermute(x, axes, pairs)  27.1 us
    pallas_call x1, Pallas kernels, body(): pl.pallas_call(fused_kernel, out_shape=(shape((n_seq, 2 * tokens, cols),...  13.3 us
    all_to_all x2, starting transfers between devices, exchange(): lax.all_to_all(x, axes, split_axis=0, concat_axis=0, tiled=True, **kw)  11.6 us
    pallas_call x1, Pallas kernels, body(): pl.pallas_call(spread_kernel, grid=(tokens // 64,), out_shape=(flat_out,...  3.81 us
    pallas_call x1, Pallas kernels, body(): pl.pallas_call(rotate_kernel, out_shape=[shape((2, tokens, cols), BF16)]...  3.17 us
    unnamed x32, local copies, waits for them, and re-layouts  2.6 us
  transfers between devices with their start and end apart: 24, of which 15 were waited for; matrix products, arithmetic and copies ran while one was open for 2% of the time, Pallas kernels for 6%

profile of v1, /device:TPU:38, one launch (start us, length us, event | category | flops | bytes accessed | tf_op | source)
XLA Modules:
  0.0 119.3 jit_solution(8278466241040025280)
XLA Ops:
  0.6 1.1 reshape_squeeze.3
  1.8 0.8 copy.14
  2.6 5.8 %all-to-all-start = ((bf16[16,24,640]{2,1,0:T(8,128)(2,1)}), bf16[16,24,640]{2,1,0:T(8,128)(2,1)S(1)}, u32[]{:S(2)}, u32[]{:S(2)}) async-start(bf16[16,24,640]{2,1,0:T(8,128)(2,1)} %bitcast.9), calls=%async_computation | async-start | bytes 983040 | tf_op jit(solution)/shard_map/all_to_all | solution.py:180
  8.5 0.6 pad_add_fusion.info
  9.0 3.2 %rotate.1 = (bf16[2,256,256]{2,1,0:T(8,128)(2,1)}, bf16[2,256,256]{2,1,0:T(8,128)(2,1)}, bf16[2,256,256]{2,1,0:T(8,128)(2,1)}, bf16[2,256,256]{2,1,0:T(8,128)(2,...) custom-call(s32[3]{0:T(128)} %pad_add_fusion.info, ...), custom_call_target="tpu_custom_call" | custom-call | tf_op jit(solution)/shard_map/rotate/pallas_call | solution.py:205
  12.3 1.9 %collective-permute-start.1 = (bf16[2,256,256]{2,1,0:T(8,128)(2,1)}, bf16[2,256,256]{2,1,0:T(8,128)(2,1)S(1)}, u32[]{:S(2)}, u32[]{:S(2)}) collective-permute-start(bf16[2,256,256]{2,1,0:T(8,128)(2,1)} %get-tuple-element.55), channel_id=1, source_target_pairs={{0,12},{2,14},{4,0},{6,2},{8,4},{10,6},{12,8},{14,10},{1,13},{3,15... | collective-permute-start | bytes 786440 | tf_op jit(solution)/shard_map/ppermute | solution.py:176
  14.4 6.9 %collective-permute-done.refs_5_ = bf16[2,256,256]{2,1,0:T(8,128)(2,1)S(1)} collective-permute-done((bf16[2,256,256]{2,1,0:T(8,128)(2,1)}, bf16[2,256,256]{2,1,0:T(8,128)(2,1)S(1)}, u32[]{:S(2)}, u32[]{:S(2)}) %collective-permute-start) | collective-permute-done | bytes 262176 | tf_op jit(solution)/shard_map/ppermute | solution.py:176
  21.4 0.7 collective-permute-done.1.refs_7_
  22.1 0.6 gather_fusion
  22.8 1.7 %collective-permute-start.5 = (bf16[128,640]{1,0:T(8,128)(2,1)S(1)}, bf16[128,640]{1,0:T(8,128)(2,1)S(1)}, u32[]{:S(2)}, u32[]{:S(2)}) collective-permute-start(bf16[128,640]{1,0:T(8,128)(2,1)S(1)} %bitcast_select_fusion), channel_id=1, source_target_pairs={{0,1},{1,0},{2,3},{3,2},{4,5},{5,4},{6,7},{7,6},{8,9},{9,8},{10,11... | collective-permute-start | bytes 491528 | tf_op jit(solution)/shard_map/ppermute | solution.py:176
  24.5 1.2 collective-permute-start.4
  25.7 1.2 collective-permute-start.3
  26.8 2.1 %collective-permute-start.2 = (bf16[128,640]{1,0:T(8,128)(2,1)S(1)}, bf16[128,640]{1,0:T(8,128)(2,1)S(1)}, u32[]{:S(2)}, u32[]{:S(2)}) collective-permute-start(bf16[128,640]{1,0:T(8,128)(2,1)S(1)} %bitcast_select_fusion), channel_id=1, source_target_pairs={{0,4},{2,6},{4,8},{6,10},{8,12},{10,14},{12,0},{14,2},{1,5},{3,7},... | collective-permute-start | bytes 491528 | tf_op jit(solution)/shard_map/ppermute | solution.py:176
  28.9 1.2 collective-permute-start.6
  30.1 3.1 %collective-permute-done.4 = bf16[128,640]{1,0:T(8,128)(2,1)S(1)} collective-permute-done((bf16[128,640]{1,0:T(8,128)(2,1)S(1)}, bf16[128,640]{1,0:T(8,128)(2,1)S(1)}, u32[]{:S(2)}, u32[]{:S(2)}) %collective-permute-start.4) | collective-permute-done | bytes 163872 | tf_op jit(solution)/shard_map/ppermute | solution.py:176
  33.2 3.5 %collective-permute-done.3 = bf16[128,640]{1,0:T(8,128)(2,1)S(1)} collective-permute-done((bf16[128,640]{1,0:T(8,128)(2,1)S(1)}, bf16[128,640]{1,0:T(8,128)(2,1)S(1)}, u32[]{:S(2)}, u32[]{:S(2)}) %collective-permute-start.3) | collective-permute-done | bytes 163872 | tf_op jit(solution)/shard_map/ppermute | solution.py:176
  36.7 0.4 collective-permute-start.10
  37.1 1.6 %collective-permute-start.7 = (bf16[2,256,256]{2,1,0:T(8,128)(2,1)}, bf16[2,256,256]{2,1,0:T(8,128)(2,1)S(1)}, u32[]{:S(2)}, u32[]{:S(2)}) collective-permute-start(bf16[2,256,256]{2,1,0:T(8,128)(2,1)} %get-tuple-element.71), channel_id=1, source_target_pairs={{0,4},{2,6},{4,8},{6,10},{8,12},{10,14},{12,0},{14,2},{1,5},{3,7},... | collective-permute-start | bytes 786440 | tf_op jit(solution)/shard_map/ppermute | solution.py:176
  38.7 0.9 collective-permute-start.8
  40.0 1.3 %collective-permute-start.11 = (bf16[128,640]{1,0:T(8,128)(2,1)S(1)}, bf16[128,640]{1,0:T(8,128)(2,1)S(1)}, u32[]{:S(2)}, u32[]{:S(2)}) collective-permute-start(bf16[128,640]{1,0:T(8,128)(2,1)S(1)} %collective-permute-done.3), channel_id=1, source_target_pairs={{0,1},{1,0},{2,3},{3,2},{4,5},{5,4},{6,7},{7,6},{8,9},{9,8},{10,11... | collective-permute-start | bytes 491528 | tf_op jit(solution)/shard_map/ppermute | solution.py:176
  41.2 2.4 %collective-permute-done.10 = bf16[128,640]{1,0:T(8,128)(2,1)S(1)} collective-permute-done((bf16[128,640]{1,0:T(8,128)(2,1)S(1)}, bf16[128,640]{1,0:T(8,128)(2,1)S(1)}, u32[]{:S(2)}, u32[]{:S(2)}) %collective-permute-start.10) | collective-permute-done | bytes 163872 | tf_op jit(solution)/shard_map/ppermute | solution.py:176
  43.6 3.5 %collective-permute-done.11 = bf16[128,640]{1,0:T(8,128)(2,1)S(1)} collective-permute-done((bf16[128,640]{1,0:T(8,128)(2,1)S(1)}, bf16[128,640]{1,0:T(8,128)(2,1)S(1)}, u32[]{:S(2)}, u32[]{:S(2)}) %collective-permute-start.11) | collective-permute-done | bytes 163872 | tf_op jit(solution)/shard_map/ppermute | solution.py:176
  47.1 1.9 %collective-permute-done.12 = bf16[128,640]{1,0:T(8,128)(2,1)S(1)} collective-permute-done((bf16[128,640]{1,0:T(8,128)(2,1)S(1)}, bf16[128,640]{1,0:T(8,128)(2,1)S(1)}, u32[]{:S(2)}, u32[]{:S(2)}) %collective-permute-start.12) | collective-permute-done | bytes 163872 | tf_op jit(solution)/shard_map/ppermute | solution.py:176
  49.0 2.4 %collective-permute-done.9.refs_12_ = bf16[2,256,256]{2,1,0:T(8,128)(2,1)S(1)} collective-permute-done((bf16[2,256,256]{2,1,0:T(8,128)(2,1)}, bf16[2,256,256]{2,1,0:T(8,128)(2,1)S(1)}, u32[]{:S(2)}, u32[]{:S(2)}) %collective-permute-start.9) | collective-permute-done | bytes 262176 | tf_op jit(solution)/shard_map/ppermute | solution.py:176
  51.5 1.0 slice.30
  52.9 0.6 collective-permute-start.14
  53.4 1.2 collective-permute-done.13.refs_8_
  54.7 0.2 collective-permute-start.15
  55.2 0.3 copy-done.12
  55.5 0.4 collective-permute-start.16
  55.9 1.8 %collective-permute-done.16.refs_13_ = bf16[4,256,256]{2,1,0:T(8,128)(2,1)S(1)} collective-permute-done((bf16[4,256,256]{2,1,0:T(8,128)(2,1)S(1)}, bf16[4,256,256]{2,1,0:T(8,128)(2,1)S(1)}, u32[]{:S(2)}, u32[]{:S(2)}) %collective-permute-start.16) | collective-permute-done | bytes 524320 | tf_op jit(solution)/shard_map/ppermute | solution.py:176
  57.7 0.7 broadcast_in_dim.23
  58.5 13.3 %fused.1 = (bf16[8,512,256]{2,1,0:T(8,128)(2,1)}, bf16[4,160,512]{2,1,0:T(8,128)(2,1)}, bf16[4,160,512]{2,1,0:T(8,128)(2,1)}) custom-call(s32[3]{0:T(128)} %pad_add_fusion.info, s32[64]{0:T(128)} %bitcast.69, f32[1,256]{1,0:T(1,128)} %bitcast.70, bf16[1280,256]{1,0:T(8,128)(2,1)} %bitcast.67, bf16[1280,256]{1,0:T(8,128)(2,1)} %bitcast.68, ...), custom_call_target="tpu_custom_call" | custom-call | flops 8589934592 | bytes 16777216 | tf_op jit(solution)/shard_map/fused/pallas_call | solution.py:234
  71.8 5.8 %all-to-all-start.1 = ((bf16[8,512,256]{2,1,0:T(8,128)(2,1)}), bf16[8,512,256]{2,1,0:T(8,128)(2,1)S(1)}, u32[]{:S(2)}, u32[]{:S(2)}) async-start(bf16[8,512,256]{2,1,0:T(8,128)(2,1)} %get-tuple-element.94), calls=%async_computation.1 | async-start | bytes 4194304 | tf_op jit(solution)/shard_map/all_to_all | solution.py:180
  77.7 10.7 %collective-permute-done.17 = bf16[4,160,512]{2,1,0:T(8,128)(2,1)S(1)} collective-permute-done((bf16[4,160,512]{2,1,0:T(8,128)(2,1)}, bf16[4,160,512]{2,1,0:T(8,128)(2,1)S(1)}, u32[]{:S(2)}, u32[]{:S(2)}) %collective-permute-start.17) | collective-permute-done | bytes 655392 | tf_op jit(solution)/shard_map/ppermute | solution.py:176
  88.4 0.8 copy-done.4
  89.3 1.3 %add_convert_fusion = bf16[4,160,512]{2,1,0:T(8,128)(2,1)S(1)} fusion(bf16[4,160,512]{2,1,0:T(8,128)(2,1)} %copy-done.4, bf16[4,160,512]{2,1,0:T(8,128)(2,1)S(1)} %copy-done.3), kind=kLoop, calls=%fused_computation.1 | loop fusion | flops 1310720 | bytes 1966080 | tf_op jit(solution)/shard_map/convert_element_type | solution.py:278
  90.6 3.0 %collective-permute-start.18 = (bf16[4,80,512]{2,1,0:T(8,128)(2,1)S(1)}, bf16[4,80,512]{2,1,0:T(8,128)(2,1)S(1)}, u32[]{:S(2)}, u32[]{:S(2)}) collective-permute-start(bf16[4,80,512]{2,1,0:T(8,128)(2,1)S(1)} %dynamic-slice_bitcast_fusion), channel_id=1, source_target_pairs={{0,16},{16,0},{32,48},{48,32},{64,80},{80,64},{96,112},{112,96},{1... | collective-permute-start | bytes 983048 | tf_op jit(solution)/shard_map/ppermute | solution.py:176
  93.6 7.7 %collective-permute-done.18 = bf16[4,80,512]{2,1,0:T(8,128)(2,1)S(1)} collective-permute-done((bf16[4,80,512]{2,1,0:T(8,128)(2,1)S(1)}, bf16[4,80,512]{2,1,0:T(8,128)(2,1)S(1)}, u32[]{:S(2)}, u32[]{:S(2)}) %collective-permute-start.18) | collective-permute-done | bytes 327712 | tf_op jit(solution)/shard_map/ppermute | solution.py:176
  101.4 6.5 %collective-permute-start.21 = (bf16[80,512]{1,0:T(8,128)(2,1)S(1)}, bf16[80,512]{1,0:T(8,128)(2,1)S(1)}, u32[]{:S(2)}, u32[]{:S(2)}) collective-permute-start(bf16[80,512]{1,0:T(8,128)(2,1)S(1)} %get-tuple-element.104), channel_id=1, source_target_pairs={{0,192},{16,208},{32,224},{48,240},{64,0},{80,16},{96,32},{112,48}... | collective-permute-start | bytes 245768 | tf_op jit(solution)/shard_map/ppermute | solution.py:176
  107.9 1.6 %collective-permute-start.20 = (bf16[80,512]{1,0:T(8,128)(2,1)S(1)}, bf16[80,512]{1,0:T(8,128)(2,1)S(1)}, u32[]{:S(2)}, u32[]{:S(2)}) collective-permute-start(bf16[80,512]{1,0:T(8,128)(2,1)S(1)} %get-tuple-element.105), channel_id=1, source_target_pairs={{0,128},{16,144},{32,160},{48,176},{64,192},{80,208},{96,224},{112... | collective-permute-start | bytes 245768 | tf_op jit(solution)/shard_map/ppermute | solution.py:176
  109.5 1.0 collective-permute-start.19
  110.5 1.3 %copy-done = bf16[8,512,256]{2,1,0:T(8,128)(2,1)} copy-done((bf16[8,512,256]{2,1,0:T(8,128)(2,1)}, bf16[8,512,256]{2,1,0:T(8,128)(2,1)S(1)}, u32[]{:S(2)}) %copy-start) | copy-done | bytes 2097176
  111.9 3.8 %spread.1 = (bf16[256,2048]{1,0:T(8,128)(2,1)}, bf16[256,2048]{1,0:T(8,128)(2,1)}) custom-call(bf16[8,2,256,256]{3,2,1,0:T(8,128)(2,1)} %bitcast.50), custom_call_target="tpu_custom_call" | custom-call | tf_op jit(solution)/shard_map/spread/pallas_call | solution.py:254
  115.7 1.9 %collective-permute-done.20 = bf16[80,512]{1,0:T(8,128)(2,1)S(1)} collective-permute-done((bf16[80,512]{1,0:T(8,128)(2,1)S(1)}, bf16[80,512]{1,0:T(8,128)(2,1)S(1)}, u32[]{:S(2)}, u32[]{:S(2)}) %collective-permute-start.20) | collective-permute-done | bytes 81952 | tf_op jit(solution)/shard_map/ppermute | solution.py:176
  117.6 0.3 collective-permute-done.19
  117.9 0.7 reshape.72
  118.6 0.7 reshape.71
  (67 shorter events, 1.8 us)
Async XLA Ops:
  2.6 19.5 %all-to-all-start = ((bf16[16,24,640]{2,1,0:T(8,128)(2,1)}), bf16[16,24,640]{2,1,0:T(8,128)(2,1)S(1)}, u32[]{:S(2)}, u32[]{:S(2)}) async-start(bf16[16,24,640]{2,1,0:T(8,128)(2,1)} %bitcast.9), calls=%async_computation | async-start | bytes 983040 | tf_op jit(solution)/shard_map/all_to_all | solution.py:180
  8.4 5.8 %copy-start.14 = (s32[1,16]{1,0:T(1,128)S(1)}, s32[1,16]{1,0:T(1,128)}, u32[]{:S(2)}) copy-start(s32[1,16]{1,0:T(1,128)} %param.10) | copy-start | bytes 196
  12.2 9.1 %collective-permute-start = (bf16[2,256,256]{2,1,0:T(8,128)(2,1)}, bf16[2,256,256]{2,1,0:T(8,128)(2,1)S(1)}, u32[]{:S(2)}, u32[]{:S(2)}) collective-permute-start(bf16[2,256,256]{2,1,0:T(8,128)(2,1)} %get-tuple-element.54), channel_id=1, source_target_pairs={{0,4},{2,6},{4,8},{6,10},{8,12},{10,14},{12,0},{14,2},{1,5},{3,7},... | collective-permute-start | bytes 786440 | tf_op jit(solution)/shard_map/ppermute | solution.py:176
  12.3 9.8 %collective-permute-start.1 = (bf16[2,256,256]{2,1,0:T(8,128)(2,1)}, bf16[2,256,256]{2,1,0:T(8,128)(2,1)S(1)}, u32[]{:S(2)}, u32[]{:S(2)}) collective-permute-start(bf16[2,256,256]{2,1,0:T(8,128)(2,1)} %get-tuple-element.55), channel_id=1, source_target_pairs={{0,12},{2,14},{4,0},{6,2},{8,4},{10,6},{12,8},{14,10},{1,13},{3,15... | collective-permute-start | bytes 786440 | tf_op jit(solution)/shard_map/ppermute | solution.py:176
  21.4 31.2 %copy-start.6 = (bf16[2,256,256]{2,1,0:T(8,128)(2,1)}, bf16[2,256,256]{2,1,0:T(8,128)(2,1)S(1)}, u32[]{:S(2)}) copy-start(bf16[2,256,256]{2,1,0:T(8,128)(2,1)S(1)} %collective-permute-done.refs_5_) | copy-start | bytes 786436
  22.1 30.5 %copy-start.7 = (bf16[2,256,256]{2,1,0:T(8,128)(2,1)}, bf16[2,256,256]{2,1,0:T(8,128)(2,1)S(1)}, u32[]{:S(2)}) copy-start(bf16[2,256,256]{2,1,0:T(8,128)(2,1)S(1)} %collective-permute-done.1.refs_7_) | copy-start | bytes 786436
  22.8 7.3 %collective-permute-start.5 = (bf16[128,640]{1,0:T(8,128)(2,1)S(1)}, bf16[128,640]{1,0:T(8,128)(2,1)S(1)}, u32[]{:S(2)}, u32[]{:S(2)}) collective-permute-start(bf16[128,640]{1,0:T(8,128)(2,1)S(1)} %bitcast_select_fusion), channel_id=1, source_target_pairs={{0,1},{1,0},{2,3},{3,2},{4,5},{5,4},{6,7},{7,6},{8,9},{9,8},{10,11... | collective-permute-start | bytes 491528 | tf_op jit(solution)/shard_map/ppermute | solution.py:176
  24.5 8.7 %collective-permute-start.4 = (bf16[128,640]{1,0:T(8,128)(2,1)S(1)}, bf16[128,640]{1,0:T(8,128)(2,1)S(1)}, u32[]{:S(2)}, u32[]{:S(2)}) collective-permute-start(bf16[128,640]{1,0:T(8,128)(2,1)S(1)} %bitcast_select_fusion), channel_id=1, source_target_pairs={{0,8},{2,10},{4,12},{6,14},{8,0},{10,2},{12,4},{14,6},{1,9},{3,11}... | collective-permute-start | bytes 491528 | tf_op jit(solution)/shard_map/ppermute | solution.py:176
  25.7 11.0 %collective-permute-start.3 = (bf16[128,640]{1,0:T(8,128)(2,1)S(1)}, bf16[128,640]{1,0:T(8,128)(2,1)S(1)}, u32[]{:S(2)}, u32[]{:S(2)}) collective-permute-start(bf16[128,640]{1,0:T(8,128)(2,1)S(1)} %bitcast_select_fusion), channel_id=1, source_target_pairs={{0,12},{2,14},{4,0},{6,2},{8,4},{10,6},{12,8},{14,10},{1,13},{3,15... | collective-permute-start | bytes 491528 | tf_op jit(solution)/shard_map/ppermute | solution.py:176
  26.8 9.8 %collective-permute-start.2 = (bf16[128,640]{1,0:T(8,128)(2,1)S(1)}, bf16[128,640]{1,0:T(8,128)(2,1)S(1)}, u32[]{:S(2)}, u32[]{:S(2)}) collective-permute-start(bf16[128,640]{1,0:T(8,128)(2,1)S(1)} %bitcast_select_fusion), channel_id=1, source_target_pairs={{0,4},{2,6},{4,8},{6,10},{8,12},{10,14},{12,0},{14,2},{1,5},{3,7},... | collective-permute-start | bytes 491528 | tf_op jit(solution)/shard_map/ppermute | solution.py:176
  28.9 11.1 %collective-permute-start.6 = (bf16[2,256,256]{2,1,0:T(8,128)(2,1)}, bf16[2,256,256]{2,1,0:T(8,128)(2,1)S(1)}, u32[]{:S(2)}, u32[]{:S(2)}) collective-permute-start(bf16[2,256,256]{2,1,0:T(8,128)(2,1)} %get-tuple-element.69), channel_id=1, source_target_pairs={{0,8},{2,10},{4,12},{6,14},{8,0},{10,2},{12,4},{14,6},{1,9},{3,11}... | collective-permute-start | bytes 786440 | tf_op jit(solution)/shard_map/ppermute | solution.py:176
  36.7 6.9 %collective-permute-start.10 = (bf16[128,640]{1,0:T(8,128)(2,1)S(1)}, bf16[128,640]{1,0:T(8,128)(2,1)S(1)}, u32[]{:S(2)}, u32[]{:S(2)}) collective-permute-start(bf16[128,640]{1,0:T(8,128)(2,1)S(1)} %collective-permute-done.2), channel_id=1, source_target_pairs={{0,1},{1,0},{2,3},{3,2},{4,5},{5,4},{6,7},{7,6},{8,9},{9,8},{10,11... | collective-permute-start | bytes 491528 | tf_op jit(solution)/shard_map/ppermute | solution.py:176
  37.1 12.0 %collective-permute-start.7 = (bf16[2,256,256]{2,1,0:T(8,128)(2,1)}, bf16[2,256,256]{2,1,0:T(8,128)(2,1)S(1)}, u32[]{:S(2)}, u32[]{:S(2)}) collective-permute-start(bf16[2,256,256]{2,1,0:T(8,128)(2,1)} %get-tuple-element.71), channel_id=1, source_target_pairs={{0,4},{2,6},{4,8},{6,10},{8,12},{10,14},{12,0},{14,2},{1,5},{3,7},... | collective-permute-start | bytes 786440 | tf_op jit(solution)/shard_map/ppermute | solution.py:176
  38.7 10.3 %collective-permute-start.8 = (bf16[2,256,256]{2,1,0:T(8,128)(2,1)}, bf16[2,256,256]{2,1,0:T(8,128)(2,1)S(1)}, u32[]{:S(2)}, u32[]{:S(2)}) collective-permute-start(bf16[2,256,256]{2,1,0:T(8,128)(2,1)} %get-tuple-element.72), channel_id=1, source_target_pairs={{0,8},{2,10},{4,12},{6,14},{8,0},{10,2},{12,4},{14,6},{1,9},{3,11}... | collective-permute-start | bytes 786440 | tf_op jit(solution)/shard_map/ppermute | solution.py:176
  39.6 11.8 %collective-permute-start.9 = (bf16[2,256,256]{2,1,0:T(8,128)(2,1)}, bf16[2,256,256]{2,1,0:T(8,128)(2,1)S(1)}, u32[]{:S(2)}, u32[]{:S(2)}) collective-permute-start(bf16[2,256,256]{2,1,0:T(8,128)(2,1)} %get-tuple-element.73), channel_id=1, source_target_pairs={{0,12},{2,14},{4,0},{6,2},{8,4},{10,6},{12,8},{14,10},{1,13},{3,15... | collective-permute-start | bytes 786440 | tf_op jit(solution)/shard_map/ppermute | solution.py:176
  40.0 12.8 %copy-start.8 = (bf16[2,256,256]{2,1,0:T(8,128)(2,1)}, bf16[2,256,256]{2,1,0:T(8,128)(2,1)S(1)}, u32[]{:S(2)}) copy-start(bf16[2,256,256]{2,1,0:T(8,128)(2,1)S(1)} %collective-permute-done.6.refs_6_) | copy-start | bytes 786436
  40.0 7.1 %collective-permute-start.11 = (bf16[128,640]{1,0:T(8,128)(2,1)S(1)}, bf16[128,640]{1,0:T(8,128)(2,1)S(1)}, u32[]{:S(2)}, u32[]{:S(2)}) collective-permute-start(bf16[128,640]{1,0:T(8,128)(2,1)S(1)} %collective-permute-done.3), channel_id=1, source_target_pairs={{0,1},{1,0},{2,3},{3,2},{4,5},{5,4},{6,7},{7,6},{8,9},{9,8},{10,11... | collective-permute-start | bytes 491528 | tf_op jit(solution)/shard_map/ppermute | solution.py:176
  43.6 5.4 %collective-permute-start.12 = (bf16[128,640]{1,0:T(8,128)(2,1)S(1)}, bf16[128,640]{1,0:T(8,128)(2,1)S(1)}, u32[]{:S(2)}, u32[]{:S(2)}) collective-permute-start(bf16[128,640]{1,0:T(8,128)(2,1)S(1)} %collective-permute-done.4), channel_id=1, source_target_pairs={{0,1},{1,0},{2,3},{3,2},{4,5},{5,4},{6,7},{7,6},{8,9},{9,8},{10,11... | collective-permute-start | bytes 491528 | tf_op jit(solution)/shard_map/ppermute | solution.py:176
  49.0 6.0 %copy-start.9 = (bf16[2,256,256]{2,1,0:T(8,128)(2,1)}, bf16[2,256,256]{2,1,0:T(8,128)(2,1)S(1)}, u32[]{:S(2)}) copy-start(bf16[2,256,256]{2,1,0:T(8,128)(2,1)S(1)} %collective-permute-done.7.refs_10_) | copy-start | bytes 786436
  49.0 6.0 %copy-start.10 = (bf16[2,256,256]{2,1,0:T(8,128)(2,1)}, bf16[2,256,256]{2,1,0:T(8,128)(2,1)S(1)}, u32[]{:S(2)}) copy-start(bf16[2,256,256]{2,1,0:T(8,128)(2,1)S(1)} %collective-permute-done.8.refs_11_) | copy-start | bytes 786436
  51.5 3.6 %copy-start.11 = (bf16[2,256,256]{2,1,0:T(8,128)(2,1)}, bf16[2,256,256]{2,1,0:T(8,128)(2,1)S(1)}, u32[]{:S(2)}) copy-start(bf16[2,256,256]{2,1,0:T(8,128)(2,1)S(1)} %collective-permute-done.9.refs_12_) | copy-start | bytes 786436
  52.6 2.0 %collective-permute-start.13 = (bf16[4,256,256]{2,1,0:T(8,128)(2,1)S(1)}, bf16[4,256,256]{2,1,0:T(8,128)(2,1)S(1)}, u32[]{:S(2)}, u32[]{:S(2)}) collective-permute-start(bf16[4,256,256]{2,1,0:T(8,128)(2,1)S(1)} %pad_maximum_fusion.2), channel_id=1, source_target_pairs={{0,2},{2,0},{4,6},{6,4},{8,10},{10,8},{12,14},{14,12},{1,3},{3,1},... | collective-permute-start | bytes 1572872 | tf_op jit(solution)/shard_map/ppermute | solution.py:176
  52.7 2.2 %copy-start.5 = (bf16[2,256,256]{2,1,0:T(8,128)(2,1)S(1)}, bf16[2,256,256]{2,1,0:T(8,128)(2,1)}, u32[]{:S(2)}) copy-start(bf16[2,256,256]{2,1,0:T(8,128)(2,1)} %get-tuple-element.90.refs_9_) | copy-start | bytes 786436
  52.8 2.3 %copy-start.1 = (bf16[4,128,640]{2,1,0:T(8,128)(2,1)}, bf16[4,128,640]{2,1,0:T(8,128)(2,1)S(1)}, u32[]{:S(2)}) copy-start(bf16[4,128,640]{2,1,0:T(8,128)(2,1)S(1)} %pad_maximum_fusion.refs_0_) | copy-start | bytes 1966084
  52.9 3.0 %collective-permute-start.14 = (bf16[4,128,640]{2,1,0:T(8,128)(2,1)S(1)}, bf16[4,128,640]{2,1,0:T(8,128)(2,1)}, u32[]{:S(2)}, u32[]{:S(2)}) collective-permute-start(bf16[4,128,640]{2,1,0:T(8,128)(2,1)S(1)} %pad_maximum_fusion.refs_0_), channel_id=1, source_target_pairs={{0,2},{2,0},{4,6},{6,4},{8,10},{10,8},{12,14},{14,12},{1,3},{3,1},... | collective-permute-start | bytes 1966088 | tf_op jit(solution)/shard_map/ppermute | solution.py:176
  54.6 0.8 copy-start.12
  54.7 3.7 %copy-start.2 = (bf16[4,128,640]{2,1,0:T(8,128)(2,1)}, bf16[4,128,640]{2,1,0:T(8,128)(2,1)S(1)}, u32[]{:S(2)}) copy-start(bf16[4,128,640]{2,1,0:T(8,128)(2,1)S(1)} %pad_maximum_fusion.1.refs_1_) | copy-start | bytes 1966084
  54.7 1.1 copy-start.15
  54.7 2.9 %collective-permute-start.15 = (bf16[4,128,640]{2,1,0:T(8,128)(2,1)S(1)}, bf16[4,128,640]{2,1,0:T(8,128)(2,1)}, u32[]{:S(2)}, u32[]{:S(2)}) collective-permute-start(bf16[4,128,640]{2,1,0:T(8,128)(2,1)S(1)} %pad_maximum_fusion.1.refs_1_), channel_id=1, source_target_pairs={{0,2},{2,0},{4,6},{6,4},{8,10},{10,8},{12,14},{14,12},{1,3},{3,1},... | collective-permute-start | bytes 1966088 | tf_op jit(solution)/shard_map/ppermute | solution.py:176
  55.5 2.2 %collective-permute-start.16 = (bf16[4,256,256]{2,1,0:T(8,128)(2,1)S(1)}, bf16[4,256,256]{2,1,0:T(8,128)(2,1)S(1)}, u32[]{:S(2)}, u32[]{:S(2)}) collective-permute-start(bf16[4,256,256]{2,1,0:T(8,128)(2,1)S(1)} %pad_maximum_fusion.3), channel_id=1, source_target_pairs={{0,2},{2,0},{4,6},{6,4},{8,10},{10,8},{12,14},{14,12},{1,3},{3,1},... | collective-permute-start | bytes 1572872 | tf_op jit(solution)/shard_map/ppermute | solution.py:176
  57.7 0.8 copy-start.13
  71.8 17.4 %copy-start.3 = (bf16[4,160,512]{2,1,0:T(8,128)(2,1)S(1)}, bf16[4,160,512]{2,1,0:T(8,128)(2,1)}, u32[]{:S(2)}) copy-start(bf16[4,160,512]{2,1,0:T(8,128)(2,1)} %get-tuple-element.97) | copy-start | bytes 1966084
  71.8 38.7 %all-to-all-start.1 = ((bf16[8,512,256]{2,1,0:T(8,128)(2,1)}), bf16[8,512,256]{2,1,0:T(8,128)(2,1)S(1)}, u32[]{:S(2)}, u32[]{:S(2)}) async-start(bf16[8,512,256]{2,1,0:T(8,128)(2,1)} %get-tuple-element.94), calls=%async_computation.1 | async-start | bytes 4194304 | tf_op jit(solution)/shard_map/all_to_all | solution.py:180
  77.6 10.8 %collective-permute-start.17 = (bf16[4,160,512]{2,1,0:T(8,128)(2,1)}, bf16[4,160,512]{2,1,0:T(8,128)(2,1)S(1)}, u32[]{:S(2)}, u32[]{:S(2)}) collective-permute-start(bf16[4,160,512]{2,1,0:T(8,128)(2,1)} %get-tuple-element.98), channel_id=1, source_target_pairs={{0,32},{2,226},{4,36},{6,230},{8,40},{10,234},{12,44},{14,238},{16... | collective-permute-start | bytes 1966088 | tf_op jit(solution)/shard_map/ppermute | solution.py:176
  88.4 0.8 copy-start.4
  90.6 10.7 %collective-permute-start.18 = (bf16[4,80,512]{2,1,0:T(8,128)(2,1)S(1)}, bf16[4,80,512]{2,1,0:T(8,128)(2,1)S(1)}, u32[]{:S(2)}, u32[]{:S(2)}) collective-permute-start(bf16[4,80,512]{2,1,0:T(8,128)(2,1)S(1)} %dynamic-slice_bitcast_fusion), channel_id=1, source_target_pairs={{0,16},{16,0},{32,48},{48,32},{64,80},{80,64},{96,112},{112,96},{1... | collective-permute-start | bytes 983048 | tf_op jit(solution)/shard_map/ppermute | solution.py:176
  101.4 14.3 %collective-permute-start.21 = (bf16[80,512]{1,0:T(8,128)(2,1)S(1)}, bf16[80,512]{1,0:T(8,128)(2,1)S(1)}, u32[]{:S(2)}, u32[]{:S(2)}) collective-permute-start(bf16[80,512]{1,0:T(8,128)(2,1)S(1)} %get-tuple-element.104), channel_id=1, source_target_pairs={{0,192},{16,208},{32,224},{48,240},{64,0},{80,16},{96,32},{112,48}... | collective-permute-start | bytes 245768 | tf_op jit(solution)/shard_map/ppermute | solution.py:176
  107.9 9.7 %collective-permute-start.20 = (bf16[80,512]{1,0:T(8,128)(2,1)S(1)}, bf16[80,512]{1,0:T(8,128)(2,1)S(1)}, u32[]{:S(2)}, u32[]{:S(2)}) collective-permute-start(bf16[80,512]{1,0:T(8,128)(2,1)S(1)} %get-tuple-element.105), channel_id=1, source_target_pairs={{0,128},{16,144},{32,160},{48,176},{64,192},{80,208},{96,224},{112... | collective-permute-start | bytes 245768 | tf_op jit(solution)/shard_map/ppermute | solution.py:176
  109.5 8.4 %collective-permute-start.19 = (bf16[80,512]{1,0:T(8,128)(2,1)S(1)}, bf16[80,512]{1,0:T(8,128)(2,1)S(1)}, u32[]{:S(2)}, u32[]{:S(2)}) collective-permute-start(bf16[80,512]{1,0:T(8,128)(2,1)S(1)} %get-tuple-element.106), channel_id=1, source_target_pairs={{0,64},{16,80},{32,96},{48,112},{64,128},{80,144},{96,160},{112,17... | collective-permute-start | bytes 245768 | tf_op jit(solution)/shard_map/ppermute | solution.py:176
  110.5 1.3 %copy-start = (bf16[8,512,256]{2,1,0:T(8,128)(2,1)}, bf16[8,512,256]{2,1,0:T(8,128)(2,1)S(1)}, u32[]{:S(2)}) copy-start(bf16[8,512,256]{2,1,0:T(8,128)(2,1)S(1)} %all-to-all-done.1) | copy-start | bytes 6291460

commit v2 on v1

--- a/solution.py
+++ b/solution.py
@@ -27,15 +27,14 @@
 def fused_kernel(
     info, blk, gain, wk, wv, *refs
 ):
-    far_parts, far_tok, (oc, send, keep) = refs[:4], refs[4:14], refs[14:17]
+    far_parts, far_tok, (oc, lead, rest, keep) = refs[:4], refs[4:13], refs[13:17]
     (kz, vz, kzt, vzt, acck, accv, ki, gs), parts, toks, made, sems = refs[17:25], refs[25:29], refs[29:31], *refs[31:33]
     ss, pgs, lows, sgs = refs[33:]
     a0, b0, a1, b1 = parts
     moves = list(zip(far_parts, parts))
     for r in range(8):
-        for j in range(2):
-            src = far_tok[5 * j + r].at[0] if r < 4 else far_tok[5 * j + 4].at[r - 4]
-            moves.append((src, toks[j].at[r]))
+        moves.append((far_tok[r].at[0] if r < 4 else far_tok[4].at[r - 4], toks[0].at[r]))
+        moves.append((far_tok[5 + r % 4].at[r // 4], toks[1].at[r]))
     loads = [pltpu.make_async_copy(x, y, sems.at[n]) for n, (x, y) in enumerate(moves)]
     for x in loads:
         x.start()
@@ -146,9 +145,13 @@
         n = 4 * span
         total = dot_t(near[...].reshape(n, half), ki[:n, :]) + dot_t(away[...].reshape(n, half), ki[n:, :])
         gs[rows, :] = total.astype(BF16)
-    n = send.shape[1]
+    n = keep.shape[1]
     for k in range(4):
-        send[k] = gs[pl.ds(pl.multiple_of((2 * k + 1 - odd) * n, n), n), :]
+        give = gs[pl.ds(pl.multiple_of((2 * k + 1 - odd) * n, n), n), :]
+        if k == 0:
+            lead[0] = give
+        else:
+            rest[k - 1] = give
         keep[k] = gs[pl.ds(pl.multiple_of((2 * k + odd) * n, n), n), :]
     for x in stores:
         x.wait()
@@ -162,14 +165,15 @@
             to = lax.rem(me // 2 + d, 4) * 2 + lax.rem(me + j, 2)
             off = pl.multiple_of(to * cols, cols)
             outs[d][j] = q[:, pl.ds(off, cols)]
-            outs[4 + d][j] = c[:, pl.ds(off, cols)]
+            outs[4 + j][d] = c[:, pl.ds(off, cols)]
 
 
 def spread_kernel(y, a, b):
-    cols = y.shape[3]
+    cols, t = y.shape[3], pl.program_id(0)
+    rows = pl.ds(pl.multiple_of(t * a.shape[0], a.shape[0]), a.shape[0])
     for r in range(8):
-        a[:, r * cols : (r + 1) * cols] = y[r, 0]
-        b[:, r * cols : (r + 1) * cols] = y[r, 1]
+        a[:, r * cols : (r + 1) * cols] = y[r, 0, rows, :]
+        b[:, r * cols : (r + 1) * cols] = y[r, 1, rows, :]
 
 
 def swap(x, axes, pairs):
@@ -204,38 +208,39 @@
 
     turned = pl.pallas_call(
         rotate_kernel,
-        out_shape=[shape((2, tokens, cols), BF16)] * 8,
+        out_shape=[shape((2, tokens, cols), BF16)] * 4 + [shape((4, tokens, cols), BF16)] * 2,
         in_specs=[SMEM, VMEM, VMEM],
-        out_specs=[VMEM] * 8,
+        out_specs=[VMEM] * 6,
         name="rotate",
     )(info, query[0], cotangent[0])
     q_in = [turned[0], along_x(turned[1], 1), None, along_x(turned[3], 3)]
-    got, q_in[1], q_in[3] = lax.optimization_barrier((got, q_in[1], q_in[3]))
+    from_sib = sibling(turned[5])
+    c_out = [jnp.stack([turned[4][d], from_sib[d]]) for d in range(4)]
+    got, q_in[1], q_in[3], c_out = lax.optimization_barrier((got, q_in[1], q_in[3], c_out))
     mine = jnp.take(got.reshape(16 * slots, ROWS, half), image_slot[0], axis=0)
     mine, q_far = lax.optimization_barrier((mine.reshape(IMAGES * ROWS, half), turned[2]))
     moved = [along_x(mine, d) for d in (1, -1, 2)]
     q_in[2] = along_x(q_far, 2)
     first = across_y(mine)
-    moved, first, c_out = lax.optimization_barrier((moved, first, turned[4:]))
+    moved, first, c_out = lax.optimization_barrier((moved, first, c_out))
     c_in = [c_out[0]] + [along_x(c_out[d], d) for d in range(1, 4)]
     own, other = [mine] + moved, [first] + [across_y(x) for x in moved]
-    q_in, c_in[1:], other[1:] = lax.optimization_barrier((q_in, c_in[1:], other[1:]))
-    q_sib = sibling(jnp.stack([x[1] for x in q_in]))
-    other, c_in, q_sib = lax.optimization_barrier((other, c_in, q_sib))
-    c_sib = sibling(jnp.stack([x[1] for x in c_in]))
+    q_give = jnp.stack([x[1] for x in q_in])
+    q_give, c_in[1:], other[1:] = lax.optimization_barrier((q_give, c_in[1:], other[1:]))
+    q_sib = sibling(q_give)
     a0, b0 = jnp.stack(own), jnp.stack(other)
     a1, b1 = sibling(a0), sibling(b0)
     wk, wv = key_weight[:, 0, :], value_weight[:, 0, :]
     n_rows = IMAGES * LAT
     gain = jnp.repeat(jnp.tanh(lax.dynamic_slice_in_dim(gate, seq_i * 2, 2)), HD)[None, :]
     rows = kv // 16
-    halves = shape((4, 2 * rows, 4 * HD), BF16)
+    some = [shape((n, 2 * rows, 4 * HD), BF16) for n in (1, 3, 4)]
     zs, zt = (IMAGES, 2 * LAT, 2 * HD), (IMAGES, 2 * HD, 2 * LAT)
-    oc, send, keep = pl.pallas_call(
+    oc, lead, rest, keep = pl.pallas_call(
         fused_kernel,
-        out_shape=(shape((n_seq, 2 * tokens, cols), BF16), halves, halves),
-        in_specs=[SMEM, SMEM] + [VMEM] * 3 + [ANY] * 14,
-        out_specs=(ANY, VMEM, VMEM),
+        out_shape=(shape((n_seq, 2 * tokens, cols), BF16), *some),
+        in_specs=[SMEM, SMEM] + [VMEM] * 3 + [ANY] * 13,
+        out_specs=(ANY, VMEM, VMEM, VMEM),
         scratch_shapes=[pltpu.VMEM(x, BF16) for x in (zs, zs, zt, zt)]
         + [pltpu.VMEM((n_rows, 2 * HD), F32)] * 2
         + [pltpu.VMEM((n_rows, 4 * HD), BF16), pltpu.VMEM((kv, 4 * HD), BF16)]
@@ -248,17 +253,7 @@
             flops=2**33, bytes_accessed=16 * 2**20, transcendentals=2**19
         ),
         name="fused",
-    )(info, block_image[0], gain, wk, wv, a0, b0, a1, b1, *q_in, q_sib, *c_in, c_sib)
-
-    flat_out = shape((tokens, width), BF16)
-    attended, query_grad = pl.pallas_call(
-        spread_kernel,
-        grid=(tokens // 64,),
-        out_shape=(flat_out, flat_out),
-        in_specs=[pl.BlockSpec((n_seq, 2, 64, cols), lambda t: (0, 0, t, 0))],
-        out_specs=[pl.BlockSpec((64, width), lambda t: (t, 0))] * 2,
-        name="spread",
-    )(exchange(oc, "seq").reshape(n_seq, 2, tokens, cols))
+    )(info, block_image[0], gain, wk, wv, a0, b0, a1, b1, *q_in, q_sib, *c_in)
 
     z_i, h_i = dp_i // 2, dp_i % 2
     pairs = []
@@ -277,7 +272,20 @@
     def join(x, y):
         return (x.astype(F32) + y.astype(F32)).astype(BF16)
 
-    part = join(keep, swap(send, ("dp", "seq"), pairs)).reshape(4, 2, rows, 4 * HD)
+    lead = swap(lead, ("dp", "seq"), pairs)
+    rest = swap(rest, ("dp", "seq"), pairs)
+    lead, oc = lax.optimization_barrier((lead, oc))
+    flat_out = shape((tokens, width), BF16)
+    attended, query_grad = pl.pallas_call(
+        spread_kernel,
+        grid=(tokens // 64,),
+        out_shape=(flat_out, flat_out),
+        in_specs=[VMEM],
+        out_specs=[pl.BlockSpec((64, width), lambda t: (t, 0))] * 2,
+        name="spread",
+    )(exchange(oc, "seq").reshape(n_seq, 2, tokens, cols))
+
+    part = join(keep, jnp.concatenate([lead, rest], axis=0)).reshape(4, 2, rows, 4 * HD)
     part = join(pick(part, h_i, 1), swap(pick(part, 1 - h_i, 1), "dp", [(j, j ^ 1) for j in range(16)]))
     k_i = z_i // 2
     more = []

time: 120 us -> 121 us (level)
    ppermute x22 -> x23, waiting for transfers between devices: 48.2 us -> 47.1 us  [swap(): return lax.ppermute(x, axes, pairs)]
    ppermute x22 -> x23, starting transfers between devices: 27.1 us -> 28 us  [swap(): return lax.ppermute(x, axes, pairs)]
    unnamed x32 -> x36, local copies, waits for them, and re-layouts: 2.6 us -> 3.35 us
  transfers between devices with their start and end apart: 24 -> 25, of which waited for: 15 -> 16; matrix products, arithmetic and copies ran while one was open for 2% -> 4% of each run, Pallas kernels for 6% -> 5%
where the time goes in v2:
time: 121 us
  waiting for transfers between devices  47.1 us (39%)
  starting transfers between devices  39.8 us (33%)
  Pallas kernels  19.9 us (16%)
  local copies, waits for them, and re-layouts  9.55 us (8%)
  other arithmetic  3.14 us (3%)
    ppermute x23, waiting for transfers between devices, swap(): return lax.ppermute(x, axes, pairs)  47.1 us
    ppermute x23, starting transfers between devices, swap(): return lax.ppermute(x, axes, pairs)  28 us
    pallas_call x1, Pallas kernels, body(): pl.pallas_call(fused_kernel, out_shape=(shape((n_seq, 2 * tokens, cols),...  13.3 us
    all_to_all x2, starting transfers between devices, exchange(): lax.all_to_all(x, axes, split_axis=0, concat_axis=0, tiled=True, **kw)  11.8 us
    pallas_call x1, Pallas kernels, body(): pl.pallas_call(spread_kernel, grid=(tokens // 64,), out_shape=(flat_out,...  3.45 us
    unnamed x36, local copies, waits for them, and re-layouts  3.35 us
    pallas_call x1, Pallas kernels, body(): pl.pallas_call(rotate_kernel, out_shape=[shape((2, tokens, cols), BF16)]...  3.16 us
  transfers between devices with their start and end apart: 25, of which 16 were waited for; matrix products, arithmetic and copies ran while one was open for 4% of the time, Pallas kernels for 5%

profile of v2, /device:TPU:38, one launch (start us, length us, event | category | flops | bytes accessed | tf_op | source)
XLA Modules:
  0.0 120.5 jit_solution(2394556206562037448)
XLA Ops:
  0.6 1.1 reshape_squeeze.3
  1.8 0.8 copy.14
  2.6 5.8 %all-to-all-start = ((bf16[16,24,640]{2,1,0:T(8,128)(2,1)}), bf16[16,24,640]{2,1,0:T(8,128)(2,1)S(1)}, u32[]{:S(2)}, u32[]{:S(2)}) async-start(bf16[16,24,640]{2,1,0:T(8,128)(2,1)} %bitcast.9), calls=%async_computation | async-start | bytes 983040 | tf_op jit(solution)/shard_map/all_to_all | solution.py:184
  8.5 0.6 pad_add_fusion.info
  9.1 3.2 %rotate.1 = (bf16[2,256,256]{2,1,0:T(8,128)(2,1)}, bf16[2,256,256]{2,1,0:T(8,128)(2,1)}, bf16[2,256,256]{2,1,0:T(8,128)(2,1)}, bf16[2,256,256]{2,1,0:T(8,128)(2,...) custom-call(s32[3]{0:T(128)} %pad_add_fusion.info, bf16[256,2048]{1,0:T(8,128)(2,1)} %bitcast.54, ...), custom_call_target="tpu_custom_call" | custom-call | tf_op jit(solution)/shard_map/rotate/pallas_call | solution.py:209
  12.3 1.9 %collective-permute-start.1 = (bf16[2,256,256]{2,1,0:T(8,128)(2,1)}, bf16[2,256,256]{2,1,0:T(8,128)(2,1)S(1)}, u32[]{:S(2)}, u32[]{:S(2)}) collective-permute-start(bf16[2,256,256]{2,1,0:T(8,128)(2,1)} %get-tuple-element.48), channel_id=1, source_target_pairs={{0,12},{2,14},{4,0},{6,2},{8,4},{10,6},{12,8},{14,10},{1,13},{3,15... | collective-permute-start | bytes 786440 | tf_op jit(solution)/shard_map/ppermute | solution.py:180
  14.5 1.1 fusion.4
  15.6 0.8 collective-permute-done.2
  16.5 0.7 pad_maximum_fusion.3
  17.2 4.1 %collective-permute-done.refs_5_ = bf16[2,256,256]{2,1,0:T(8,128)(2,1)S(1)} collective-permute-done((bf16[2,256,256]{2,1,0:T(8,128)(2,1)}, bf16[2,256,256]{2,1,0:T(8,128)(2,1)S(1)}, u32[]{:S(2)}, u32[]{:S(2)}) %collective-permute-start) | collective-permute-done | bytes 262176 | tf_op jit(solution)/shard_map/ppermute | solution.py:180
  21.4 0.7 collective-permute-done.1.refs_7_
  22.1 0.6 gather_fusion
  22.8 1.7 %collective-permute-start.6 = (bf16[128,640]{1,0:T(8,128)(2,1)S(1)}, bf16[128,640]{1,0:T(8,128)(2,1)S(1)}, u32[]{:S(2)}, u32[]{:S(2)}) collective-permute-start(bf16[128,640]{1,0:T(8,128)(2,1)S(1)} %bitcast_select_fusion), channel_id=1, source_target_pairs={{0,1},{1,0},{2,3},{3,2},{4,5},{5,4},{6,7},{7,6},{8,9},{9,8},{10,11... | collective-permute-start | bytes 491528 | tf_op jit(solution)/shard_map/ppermute | solution.py:180
  24.5 1.2 collective-permute-start.5
  25.7 1.2 collective-permute-start.4
  26.9 2.1 %collective-permute-start.3 = (bf16[128,640]{1,0:T(8,128)(2,1)S(1)}, bf16[128,640]{1,0:T(8,128)(2,1)S(1)}, u32[]{:S(2)}, u32[]{:S(2)}) collective-permute-start(bf16[128,640]{1,0:T(8,128)(2,1)S(1)} %bitcast_select_fusion), channel_id=1, source_target_pairs={{0,4},{2,6},{4,8},{6,10},{8,12},{10,14},{12,0},{14,2},{1,5},{3,7},... | collective-permute-start | bytes 491528 | tf_op jit(solution)/shard_map/ppermute | solution.py:180
  28.9 1.2 collective-permute-start.7
  30.1 3.1 %collective-permute-done.5 = bf16[128,640]{1,0:T(8,128)(2,1)S(1)} collective-permute-done((bf16[128,640]{1,0:T(8,128)(2,1)S(1)}, bf16[128,640]{1,0:T(8,128)(2,1)S(1)}, u32[]{:S(2)}, u32[]{:S(2)}) %collective-permute-start.5) | collective-permute-done | bytes 163872 | tf_op jit(solution)/shard_map/ppermute | solution.py:180
  33.2 3.5 %collective-permute-done.4 = bf16[128,640]{1,0:T(8,128)(2,1)S(1)} collective-permute-done((bf16[128,640]{1,0:T(8,128)(2,1)S(1)}, bf16[128,640]{1,0:T(8,128)(2,1)S(1)}, u32[]{:S(2)}, u32[]{:S(2)}) %collective-permute-start.4) | collective-permute-done | bytes 163872 | tf_op jit(solution)/shard_map/ppermute | solution.py:180
  37.1 1.7 %collective-permute-start.8 = (bf16[2,256,256]{2,1,0:T(8,128)(2,1)S(1)}, bf16[2,256,256]{2,1,0:T(8,128)(2,1)S(1)}, u32[]{:S(2)}, u32[]{:S(2)}) collective-permute-start(bf16[2,256,256]{2,1,0:T(8,128)(2,1)S(1)} %get-tuple-element.66), channel_id=1, source_target_pairs={{0,4},{2,6},{4,8},{6,10},{8,12},{10,14},{12,0},{14,2},{1,5},{3,7},... | collective-permute-start | bytes 786440 | tf_op jit(solution)/shard_map/ppermute | solution.py:180
  38.7 0.9 collective-permute-start.9
  40.0 1.4 %collective-permute-start.12 = (bf16[128,640]{1,0:T(8,128)(2,1)S(1)}, bf16[128,640]{1,0:T(8,128)(2,1)S(1)}, u32[]{:S(2)}, u32[]{:S(2)}) collective-permute-start(bf16[128,640]{1,0:T(8,128)(2,1)S(1)} %collective-permute-done.4), channel_id=1, source_target_pairs={{0,1},{1,0},{2,3},{3,2},{4,5},{5,4},{6,7},{7,6},{8,9},{9,8},{10,11... | collective-permute-start | bytes 491528 | tf_op jit(solution)/shard_map/ppermute | solution.py:180
  41.4 2.2 %collective-permute-done.11 = bf16[128,640]{1,0:T(8,128)(2,1)S(1)} collective-permute-done((bf16[128,640]{1,0:T(8,128)(2,1)S(1)}, bf16[128,640]{1,0:T(8,128)(2,1)S(1)}, u32[]{:S(2)}, u32[]{:S(2)}) %collective-permute-start.11) | collective-permute-done | bytes 163872 | tf_op jit(solution)/shard_map/ppermute | solution.py:180
  43.9 3.3 %collective-permute-done.12 = bf16[128,640]{1,0:T(8,128)(2,1)S(1)} collective-permute-done((bf16[128,640]{1,0:T(8,128)(2,1)S(1)}, bf16[128,640]{1,0:T(8,128)(2,1)S(1)}, u32[]{:S(2)}, u32[]{:S(2)}) %collective-permute-start.12) | collective-permute-done | bytes 163872 | tf_op jit(solution)/shard_map/ppermute | solution.py:180
  47.1 1.9 %collective-permute-done.13 = bf16[128,640]{1,0:T(8,128)(2,1)S(1)} collective-permute-done((bf16[128,640]{1,0:T(8,128)(2,1)S(1)}, bf16[128,640]{1,0:T(8,128)(2,1)S(1)}, u32[]{:S(2)}, u32[]{:S(2)}) %collective-permute-start.13) | collective-permute-done | bytes 163872 | tf_op jit(solution)/shard_map/ppermute | solution.py:180
  49.0 2.2 %collective-permute-done.10.refs_12_ = bf16[2,256,256]{2,1,0:T(8,128)(2,1)S(1)} collective-permute-done((bf16[2,256,256]{2,1,0:T(8,128)(2,1)S(1)}, bf16[2,256,256]{2,1,0:T(8,128)(2,1)S(1)}, u32[]{:S(2)}, u32[]{:S(2)}) %collective-permute-start.10) | collective-permute-done | bytes 262176 | tf_op jit(solution)/shard_map/ppermute | solution.py:180
  51.5 0.5 copy-done.15
  52.3 2.0 %collective-permute-done.16.refs_8_ = bf16[4,256,256]{2,1,0:T(8,128)(2,1)S(1)} collective-permute-done((bf16[4,256,256]{2,1,0:T(8,128)(2,1)S(1)}, bf16[4,256,256]{2,1,0:T(8,128)(2,1)S(1)}, u32[]{:S(2)}, u32[]{:S(2)}) %collective-permute-start.16) | collective-permute-done | bytes 524320 | tf_op jit(solution)/shard_map/ppermute | solution.py:180
  54.3 0.7 broadcast_in_dim.23
  55.1 13.3 %fused.1 = (bf16[8,512,256]{2,1,0:T(8,128)(2,1)}, bf16[1,160,512]{2,1,0:T(8,128)(2,1)}, bf16[3,160,512]{2,1,0:T(8,128)(2,1)}, bf16[4,160,512]{2,1,0:T(8,128)(2,1)}) custom-call(s32[3]{0:T(128)} %pad_add_fusion.info, s32[64]{0:T(128)} %bitcast.69, f32[1,256]{1,0:T(1,128)} %bitcast.70, bf16[1280,256]{1,0:T(8,128)(2,1)} %bitcast.67, ...), custom_call_target="tpu_custom_call" | custom-call | flops 8589934592 | bytes 16777216 | tf_op jit(solution)/shard_map/fused/pallas_call | solution.py:239
  68.7 5.4 %collective-permute-done.17 = bf16[1,160,512]{2,1,0:T(8,128)(2,1)S(1)} collective-permute-done((bf16[1,160,512]{2,1,0:T(8,128)(2,1)}, bf16[1,160,512]{2,1,0:T(8,128)(2,1)S(1)}, u32[]{:S(2)}, u32[]{:S(2)}) %collective-permute-start.17) | collective-permute-done | bytes 163872 | tf_op jit(solution)/shard_map/ppermute | solution.py:180
  74.1 0.7 copy-done.5
  74.7 5.9 %all-to-all-start.1 = ((bf16[8,512,256]{2,1,0:T(8,128)(2,1)}), bf16[8,512,256]{2,1,0:T(8,128)(2,1)S(1)}, u32[]{:S(2)}, u32[]{:S(2)}) async-start(bf16[8,512,256]{2,1,0:T(8,128)(2,1)} %get-tuple-element.79), calls=%async_computation.1 | async-start | bytes 4194304 | tf_op jit(solution)/shard_map/all_to_all | solution.py:184
  80.7 1.5 %collective-permute-start.18 = (bf16[3,160,512]{2,1,0:T(8,128)(2,1)}, bf16[3,160,512]{2,1,0:T(8,128)(2,1)S(1)}, u32[]{:S(2)}, u32[]{:S(2)}) collective-permute-start(bf16[3,160,512]{2,1,0:T(8,128)(2,1)} %get-tuple-element.84), channel_id=1, source_target_pairs={{0,32},{2,226},{4,36},{6,230},{8,40},{10,234},{12,44},{14,238},{16... | collective-permute-start | bytes 1474568 | tf_op jit(solution)/shard_map/ppermute | solution.py:180
  82.2 7.5 %collective-permute-done.18 = bf16[3,160,512]{2,1,0:T(8,128)(2,1)S(1)} collective-permute-done((bf16[3,160,512]{2,1,0:T(8,128)(2,1)}, bf16[3,160,512]{2,1,0:T(8,128)(2,1)S(1)}, u32[]{:S(2)}, u32[]{:S(2)}) %collective-permute-start.18) | collective-permute-done | bytes 491552 | tf_op jit(solution)/shard_map/ppermute | solution.py:180
  89.7 0.8 copy-done.4
  90.5 1.2 %add_convert_fusion = bf16[4,160,512]{2,1,0:T(8,128)(2,1)S(1)} fusion(bf16[4,160,512]{2,1,0:T(8,128)(2,1)S(1)} %copy-done.3, bf16[3,160,512]{2,1,0:T(8,128)(2,1)} %copy-done.4, bf16[1,160,512]{2,1,0:T(8,128)(2,1)} %copy-done.5), kind=kLoop, calls=%fused_computation.1 | loop fusion | flops 1638400 | bytes 1966080 | tf_op jit(solution)/shard_map/convert_element_type | solution.py:273
  91.8 3.0 %collective-permute-start.19 = (bf16[4,80,512]{2,1,0:T(8,128)(2,1)S(1)}, bf16[4,80,512]{2,1,0:T(8,128)(2,1)S(1)}, u32[]{:S(2)}, u32[]{:S(2)}) collective-permute-start(bf16[4,80,512]{2,1,0:T(8,128)(2,1)S(1)} %dynamic-slice_bitcast_fusion), channel_id=1, source_target_pairs={{0,16},{16,0},{32,48},{48,32},{64,80},{80,64},{96,112},{112,96},{1... | collective-permute-start | bytes 983048 | tf_op jit(solution)/shard_map/ppermute | solution.py:180
  94.8 7.7 %collective-permute-done.19 = bf16[4,80,512]{2,1,0:T(8,128)(2,1)S(1)} collective-permute-done((bf16[4,80,512]{2,1,0:T(8,128)(2,1)S(1)}, bf16[4,80,512]{2,1,0:T(8,128)(2,1)S(1)}, u32[]{:S(2)}, u32[]{:S(2)}) %collective-permute-start.19) | collective-permute-done | bytes 327712 | tf_op jit(solution)/shard_map/ppermute | solution.py:180
  102.6 6.2 %collective-permute-start.22 = (bf16[80,512]{1,0:T(8,128)(2,1)S(1)}, bf16[80,512]{1,0:T(8,128)(2,1)S(1)}, u32[]{:S(2)}, u32[]{:S(2)}) collective-permute-start(bf16[80,512]{1,0:T(8,128)(2,1)S(1)} %get-tuple-element.98), channel_id=1, source_target_pairs={{0,192},{16,208},{32,224},{48,240},{64,0},{80,16},{96,32},{112,48}... | collective-permute-start | bytes 245768 | tf_op jit(solution)/shard_map/ppermute | solution.py:180
  108.8 1.7 %collective-permute-start.21 = (bf16[80,512]{1,0:T(8,128)(2,1)S(1)}, bf16[80,512]{1,0:T(8,128)(2,1)S(1)}, u32[]{:S(2)}, u32[]{:S(2)}) collective-permute-start(bf16[80,512]{1,0:T(8,128)(2,1)S(1)} %get-tuple-element.99), channel_id=1, source_target_pairs={{0,128},{16,144},{32,160},{48,176},{64,192},{80,208},{96,224},{112... | collective-permute-start | bytes 245768 | tf_op jit(solution)/shard_map/ppermute | solution.py:180
  110.5 1.2 %collective-permute-start.20 = (bf16[80,512]{1,0:T(8,128)(2,1)S(1)}, bf16[80,512]{1,0:T(8,128)(2,1)S(1)}, u32[]{:S(2)}, u32[]{:S(2)}) collective-permute-start(bf16[80,512]{1,0:T(8,128)(2,1)S(1)} %get-tuple-element.100), channel_id=1, source_target_pairs={{0,64},{16,80},{32,96},{48,112},{64,128},{80,144},{96,160},{112,17... | collective-permute-start | bytes 245768 | tf_op jit(solution)/shard_map/ppermute | solution.py:180
  111.7 1.3 %copy-done = bf16[8,512,256]{2,1,0:T(8,128)(2,1)} copy-done((bf16[8,512,256]{2,1,0:T(8,128)(2,1)}, bf16[8,512,256]{2,1,0:T(8,128)(2,1)S(1)}, u32[]{:S(2)}) %copy-start) | copy-done | bytes 2097176
  113.1 3.4 %spread.1 = (bf16[256,2048]{1,0:T(8,128)(2,1)}, bf16[256,2048]{1,0:T(8,128)(2,1)}) custom-call(bf16[8,2,256,256]{3,2,1,0:T(8,128)(2,1)} %bitcast.50), custom_call_target="tpu_custom_call" | custom-call | tf_op jit(solution)/shard_map/spread/pallas_call | solution.py:279
  116.5 1.4 %collective-permute-done.21 = bf16[80,512]{1,0:T(8,128)(2,1)S(1)} collective-permute-done((bf16[80,512]{1,0:T(8,128)(2,1)S(1)}, bf16[80,512]{1,0:T(8,128)(2,1)S(1)}, u32[]{:S(2)}, u32[]{:S(2)}) %collective-permute-start.21) | collective-permute-done | bytes 81952 | tf_op jit(solution)/shard_map/ppermute | solution.py:180
  117.9 1.2 collective-permute-done.20
  119.1 0.7 reshape.72
  119.8 0.7 reshape.71
  (72 shorter events, 2.5 us)
Async XLA Ops:
  2.6 19.5 %all-to-all-start = ((bf16[16,24,640]{2,1,0:T(8,128)(2,1)}), bf16[16,24,640]{2,1,0:T(8,128)(2,1)S(1)}, u32[]{:S(2)}, u32[]{:S(2)}) async-start(bf16[16,24,640]{2,1,0:T(8,128)(2,1)} %bitcast.9), calls=%async_computation | async-start | bytes 983040 | tf_op jit(solution)/shard_map/all_to_all | solution.py:184
  8.4 5.8 %copy-start.16 = (s32[1,16]{1,0:T(1,128)S(1)}, s32[1,16]{1,0:T(1,128)}, u32[]{:S(2)}) copy-start(s32[1,16]{1,0:T(1,128)} %param.10) | copy-start | bytes 196
  12.2 9.1 %collective-permute-start = (bf16[2,256,256]{2,1,0:T(8,128)(2,1)}, bf16[2,256,256]{2,1,0:T(8,128)(2,1)S(1)}, u32[]{:S(2)}, u32[]{:S(2)}) collective-permute-start(bf16[2,256,256]{2,1,0:T(8,128)(2,1)} %get-tuple-element.47), channel_id=1, source_target_pairs={{0,4},{2,6},{4,8},{6,10},{8,12},{10,14},{12,0},{14,2},{1,5},{3,7},... | collective-permute-start | bytes 786440 | tf_op jit(solution)/shard_map/ppermute | solution.py:180
  12.3 9.8 %collective-permute-start.1 = (bf16[2,256,256]{2,1,0:T(8,128)(2,1)}, bf16[2,256,256]{2,1,0:T(8,128)(2,1)S(1)}, u32[]{:S(2)}, u32[]{:S(2)}) collective-permute-start(bf16[2,256,256]{2,1,0:T(8,128)(2,1)} %get-tuple-element.48), channel_id=1, source_target_pairs={{0,12},{2,14},{4,0},{6,2},{8,4},{10,6},{12,8},{14,10},{1,13},{3,15... | collective-permute-start | bytes 786440 | tf_op jit(solution)/shard_map/ppermute | solution.py:180
  14.2 2.1 %collective-permute-start.2 = (bf16[4,256,256]{2,1,0:T(8,128)(2,1)}, bf16[4,256,256]{2,1,0:T(8,128)(2,1)S(1)}, u32[]{:S(2)}, u32[]{:S(2)}) collective-permute-start(bf16[4,256,256]{2,1,0:T(8,128)(2,1)} %get-tuple-element.50), channel_id=1, source_target_pairs={{0,2},{2,0},{4,6},{6,4},{8,10},{10,8},{12,14},{14,12},{1,3},{3,1},... | collective-permute-start | bytes 1572872 | tf_op jit(solution)/shard_map/ppermute | solution.py:180
  16.4 12.5 %copy-start.12 = (bf16[2,256,256]{2,1,0:T(8,128)(2,1)S(1)}, bf16[2,256,256]{2,1,0:T(8,128)(2,1)}, u32[]{:S(2)}) copy-start(bf16[2,256,256]{2,1,0:T(8,128)(2,1)} %get-tuple-element.64) | copy-start | bytes 786436
  16.4 23.4 %copy-start.6 = (bf16[2,256,256]{2,1,0:T(8,128)(2,1)S(1)}, bf16[2,256,256]{2,1,0:T(8,128)(2,1)}, u32[]{:S(2)}) copy-start(bf16[2,256,256]{2,1,0:T(8,128)(2,1)} %get-tuple-element.62.refs_4_) | copy-start | bytes 786436
  21.4 22.4 %copy-start.7 = (bf16[2,256,256]{2,1,0:T(8,128)(2,1)}, bf16[2,256,256]{2,1,0:T(8,128)(2,1)S(1)}, u32[]{:S(2)}) copy-start(bf16[2,256,256]{2,1,0:T(8,128)(2,1)S(1)} %collective-permute-done.refs_5_) | copy-start | bytes 786436
  22.1 21.6 %copy-start.8 = (bf16[2,256,256]{2,1,0:T(8,128)(2,1)}, bf16[2,256,256]{2,1,0:T(8,128)(2,1)S(1)}, u32[]{:S(2)}) copy-start(bf16[2,256,256]{2,1,0:T(8,128)(2,1)S(1)} %collective-permute-done.1.refs_7_) | copy-start | bytes 786436
  22.8 7.3 %collective-permute-start.6 = (bf16[128,640]{1,0:T(8,128)(2,1)S(1)}, bf16[128,640]{1,0:T(8,128)(2,1)S(1)}, u32[]{:S(2)}, u32[]{:S(2)}) collective-permute-start(bf16[128,640]{1,0:T(8,128)(2,1)S(1)} %bitcast_select_fusion), channel_id=1, source_target_pairs={{0,1},{1,0},{2,3},{3,2},{4,5},{5,4},{6,7},{7,6},{8,9},{9,8},{10,11... | collective-permute-start | bytes 491528 | tf_op jit(solution)/shard_map/ppermute | solution.py:180
  24.5 8.7 %collective-permute-start.5 = (bf16[128,640]{1,0:T(8,128)(2,1)S(1)}, bf16[128,640]{1,0:T(8,128)(2,1)S(1)}, u32[]{:S(2)}, u32[]{:S(2)}) collective-permute-start(bf16[128,640]{1,0:T(8,128)(2,1)S(1)} %bitcast_select_fusion), channel_id=1, source_target_pairs={{0,8},{2,10},{4,12},{6,14},{8,0},{10,2},{12,4},{14,6},{1,9},{3,11}... | collective-permute-start | bytes 491528 | tf_op jit(solution)/shard_map/ppermute | solution.py:180
  25.7 11.0 %collective-permute-start.4 = (bf16[128,640]{1,0:T(8,128)(2,1)S(1)}, bf16[128,640]{1,0:T(8,128)(2,1)S(1)}, u32[]{:S(2)}, u32[]{:S(2)}) collective-permute-start(bf16[128,640]{1,0:T(8,128)(2,1)S(1)} %bitcast_select_fusion), channel_id=1, source_target_pairs={{0,12},{2,14},{4,0},{6,2},{8,4},{10,6},{12,8},{14,10},{1,13},{3,15... | collective-permute-start | bytes 491528 | tf_op jit(solution)/shard_map/ppermute | solution.py:180
  26.9 9.8 %collective-permute-start.3 = (bf16[128,640]{1,0:T(8,128)(2,1)S(1)}, bf16[128,640]{1,0:T(8,128)(2,1)S(1)}, u32[]{:S(2)}, u32[]{:S(2)}) collective-permute-start(bf16[128,640]{1,0:T(8,128)(2,1)S(1)} %bitcast_select_fusion), channel_id=1, source_target_pairs={{0,4},{2,6},{4,8},{6,10},{8,12},{10,14},{12,0},{14,2},{1,5},{3,7},... | collective-permute-start | bytes 491528 | tf_op jit(solution)/shard_map/ppermute | solution.py:180
  28.9 11.1 %collective-permute-start.7 = (bf16[2,256,256]{2,1,0:T(8,128)(2,1)S(1)}, bf16[2,256,256]{2,1,0:T(8,128)(2,1)S(1)}, u32[]{:S(2)}, u32[]{:S(2)}) collective-permute-start(bf16[2,256,256]{2,1,0:T(8,128)(2,1)S(1)} %copy-done.12), channel_id=1, source_target_pairs={{0,8},{2,10},{4,12},{6,14},{8,0},{10,2},{12,4},{14,6},{1,9},{3,11}... | collective-permute-start | bytes 786440 | tf_op jit(solution)/shard_map/ppermute | solution.py:180
  36.7 6.9 %collective-permute-start.11 = (bf16[128,640]{1,0:T(8,128)(2,1)S(1)}, bf16[128,640]{1,0:T(8,128)(2,1)S(1)}, u32[]{:S(2)}, u32[]{:S(2)}) collective-permute-start(bf16[128,640]{1,0:T(8,128)(2,1)S(1)} %collective-permute-done.3), channel_id=1, source_target_pairs={{0,1},{1,0},{2,3},{3,2},{4,5},{5,4},{6,7},{7,6},{8,9},{9,8},{10,11... | collective-permute-start | bytes 491528 | tf_op jit(solution)/shard_map/ppermute | solution.py:180
  37.1 12.0 %collective-permute-start.8 = (bf16[2,256,256]{2,1,0:T(8,128)(2,1)S(1)}, bf16[2,256,256]{2,1,0:T(8,128)(2,1)S(1)}, u32[]{:S(2)}, u32[]{:S(2)}) collective-permute-start(bf16[2,256,256]{2,1,0:T(8,128)(2,1)S(1)} %get-tuple-element.66), channel_id=1, source_target_pairs={{0,4},{2,6},{4,8},{6,10},{8,12},{10,14},{12,0},{14,2},{1,5},{3,7},... | collective-permute-start | bytes 786440 | tf_op jit(solution)/shard_map/ppermute | solution.py:180
  38.7 10.3 %collective-permute-start.9 = (bf16[2,256,256]{2,1,0:T(8,128)(2,1)S(1)}, bf16[2,256,256]{2,1,0:T(8,128)(2,1)S(1)}, u32[]{:S(2)}, u32[]{:S(2)}) collective-permute-start(bf16[2,256,256]{2,1,0:T(8,128)(2,1)S(1)} %get-tuple-element.67), channel_id=1, source_target_pairs={{0,8},{2,10},{4,12},{6,14},{8,0},{10,2},{12,4},{14,6},{1,9},{3,11}... | collective-permute-start | bytes 786440 | tf_op jit(solution)/shard_map/ppermute | solution.py:180
  39.7 11.6 %collective-permute-start.10 = (bf16[2,256,256]{2,1,0:T(8,128)(2,1)S(1)}, bf16[2,256,256]{2,1,0:T(8,128)(2,1)S(1)}, u32[]{:S(2)}, u32[]{:S(2)}) collective-permute-start(bf16[2,256,256]{2,1,0:T(8,128)(2,1)S(1)} %get-tuple-element.68), channel_id=1, source_target_pairs={{0,12},{2,14},{4,0},{6,2},{8,4},{10,6},{12,8},{14,10},{1,13},{3,15... | collective-permute-start | bytes 786440 | tf_op jit(solution)/shard_map/ppermute | solution.py:180
  40.0 3.9 %copy-start.9 = (bf16[2,256,256]{2,1,0:T(8,128)(2,1)}, bf16[2,256,256]{2,1,0:T(8,128)(2,1)S(1)}, u32[]{:S(2)}) copy-start(bf16[2,256,256]{2,1,0:T(8,128)(2,1)S(1)} %collective-permute-done.7.refs_6_) | copy-start | bytes 786436
  40.0 7.1 %collective-permute-start.12 = (bf16[128,640]{1,0:T(8,128)(2,1)S(1)}, bf16[128,640]{1,0:T(8,128)(2,1)S(1)}, u32[]{:S(2)}, u32[]{:S(2)}) collective-permute-start(bf16[128,640]{1,0:T(8,128)(2,1)S(1)} %collective-permute-done.4), channel_id=1, source_target_pairs={{0,1},{1,0},{2,3},{3,2},{4,5},{5,4},{6,7},{7,6},{8,9},{9,8},{10,11... | collective-permute-start | bytes 491528 | tf_op jit(solution)/shard_map/ppermute | solution.py:180
  43.6 5.4 %collective-permute-start.13 = (bf16[128,640]{1,0:T(8,128)(2,1)S(1)}, bf16[128,640]{1,0:T(8,128)(2,1)S(1)}, u32[]{:S(2)}, u32[]{:S(2)}) collective-permute-start(bf16[128,640]{1,0:T(8,128)(2,1)S(1)} %collective-permute-done.5), channel_id=1, source_target_pairs={{0,1},{1,0},{2,3},{3,2},{4,5},{5,4},{6,7},{7,6},{8,9},{9,8},{10,11... | collective-permute-start | bytes 491528 | tf_op jit(solution)/shard_map/ppermute | solution.py:180
  43.7 7.6 %copy-start.1 = (bf16[4,128,640]{2,1,0:T(8,128)(2,1)}, bf16[4,128,640]{2,1,0:T(8,128)(2,1)S(1)}, u32[]{:S(2)}) copy-start(bf16[4,128,640]{2,1,0:T(8,128)(2,1)S(1)} %pad_maximum_fusion.refs_0_) | copy-start | bytes 1966084
  43.7 8.5 %copy-start.17 = (f32[16]{0:T(128)S(1)}, f32[16]{0:T(128)}, u32[]{:S(2)}) copy-start(f32[16]{0:T(128)} %param.14) | copy-start | bytes 196
  47.1 5.2 %collective-permute-start.14 = (bf16[4,128,640]{2,1,0:T(8,128)(2,1)S(1)}, bf16[4,128,640]{2,1,0:T(8,128)(2,1)S(1)}, u32[]{:S(2)}, u32[]{:S(2)}) collective-permute-start(bf16[4,128,640]{2,1,0:T(8,128)(2,1)S(1)} %pad_maximum_fusion.refs_0_), channel_id=1, source_target_pairs={{0,2},{2,0},{4,6},{6,4},{8,10},{10,8},{12,14},{14,12},{1,3},{3,1},... | collective-permute-start | bytes 1966088 | tf_op jit(solution)/shard_map/ppermute | solution.py:180
  49.0 2.5 %copy-start.13 = (bf16[2,256,256]{2,1,0:T(8,128)(2,1)}, bf16[2,256,256]{2,1,0:T(8,128)(2,1)S(1)}, u32[]{:S(2)}) copy-start(bf16[2,256,256]{2,1,0:T(8,128)(2,1)S(1)} %collective-permute-done.8.refs_10_) | copy-start | bytes 786436
  49.0 2.5 %copy-start.14 = (bf16[2,256,256]{2,1,0:T(8,128)(2,1)}, bf16[2,256,256]{2,1,0:T(8,128)(2,1)S(1)}, u32[]{:S(2)}) copy-start(bf16[2,256,256]{2,1,0:T(8,128)(2,1)S(1)} %collective-permute-done.9.refs_11_) | copy-start | bytes 786436
  51.3 0.7 copy-start.15
  51.4 3.7 %copy-start.2 = (bf16[4,128,640]{2,1,0:T(8,128)(2,1)}, bf16[4,128,640]{2,1,0:T(8,128)(2,1)S(1)}, u32[]{:S(2)}) copy-start(bf16[4,128,640]{2,1,0:T(8,128)(2,1)S(1)} %pad_maximum_fusion.1.refs_1_) | copy-start | bytes 1966084
  51.4 2.9 %collective-permute-start.15 = (bf16[4,128,640]{2,1,0:T(8,128)(2,1)S(1)}, bf16[4,128,640]{2,1,0:T(8,128)(2,1)}, u32[]{:S(2)}, u32[]{:S(2)}) collective-permute-start(bf16[4,128,640]{2,1,0:T(8,128)(2,1)S(1)} %pad_maximum_fusion.1.refs_1_), channel_id=1, source_target_pairs={{0,2},{2,0},{4,6},{6,4},{8,10},{10,8},{12,14},{14,12},{1,3},{3,1},... | collective-permute-start | bytes 1966088 | tf_op jit(solution)/shard_map/ppermute | solution.py:180
  52.0 2.4 %collective-permute-start.16 = (bf16[4,256,256]{2,1,0:T(8,128)(2,1)S(1)}, bf16[4,256,256]{2,1,0:T(8,128)(2,1)S(1)}, u32[]{:S(2)}, u32[]{:S(2)}) collective-permute-start(bf16[4,256,256]{2,1,0:T(8,128)(2,1)S(1)} %pad_maximum_fusion.2), channel_id=1, source_target_pairs={{0,2},{2,0},{4,6},{6,4},{8,10},{10,8},{12,14},{14,12},{1,3},{3,1},... | collective-permute-start | bytes 1572872 | tf_op jit(solution)/shard_map/ppermute | solution.py:180
  52.3 2.7 %copy-start.10 = (bf16[4,128,640]{2,1,0:T(8,128)(2,1)}, bf16[4,128,640]{2,1,0:T(8,128)(2,1)S(1)}, u32[]{:S(2)}) copy-start(bf16[4,128,640]{2,1,0:T(8,128)(2,1)S(1)} %collective-permute-done.14.refs_2_) | copy-start | bytes 1966084
  54.3 0.8 copy-start.11
  68.5 5.6 %collective-permute-start.17 = (bf16[1,160,512]{2,1,0:T(8,128)(2,1)}, bf16[1,160,512]{2,1,0:T(8,128)(2,1)S(1)}, u32[]{:S(2)}, u32[]{:S(2)}) collective-permute-start(bf16[1,160,512]{2,1,0:T(8,128)(2,1)} %get-tuple-element.77), channel_id=1, source_target_pairs={{0,32},{2,226},{4,36},{6,230},{8,40},{10,234},{12,44},{14,238},{16... | collective-permute-start | bytes 491528 | tf_op jit(solution)/shard_map/ppermute | solution.py:180
  74.1 0.7 copy-start.5
  74.7 15.8 %copy-start.3 = (bf16[4,160,512]{2,1,0:T(8,128)(2,1)S(1)}, bf16[4,160,512]{2,1,0:T(8,128)(2,1)}, u32[]{:S(2)}) copy-start(bf16[4,160,512]{2,1,0:T(8,128)(2,1)} %get-tuple-element.82) | copy-start | bytes 1966084
  74.7 37.0 %all-to-all-start.1 = ((bf16[8,512,256]{2,1,0:T(8,128)(2,1)}), bf16[8,512,256]{2,1,0:T(8,128)(2,1)S(1)}, u32[]{:S(2)}, u32[]{:S(2)}) async-start(bf16[8,512,256]{2,1,0:T(8,128)(2,1)} %get-tuple-element.79), calls=%async_computation.1 | async-start | bytes 4194304 | tf_op jit(solution)/shard_map/all_to_all | solution.py:184
  80.7 9.0 %collective-permute-start.18 = (bf16[3,160,512]{2,1,0:T(8,128)(2,1)}, bf16[3,160,512]{2,1,0:T(8,128)(2,1)S(1)}, u32[]{:S(2)}, u32[]{:S(2)}) collective-permute-start(bf16[3,160,512]{2,1,0:T(8,128)(2,1)} %get-tuple-element.84), channel_id=1, source_target_pairs={{0,32},{2,226},{4,36},{6,230},{8,40},{10,234},{12,44},{14,238},{16... | collective-permute-start | bytes 1474568 | tf_op jit(solution)/shard_map/ppermute | solution.py:180
  89.7 0.8 copy-start.4
  91.8 10.7 %collective-permute-start.19 = (bf16[4,80,512]{2,1,0:T(8,128)(2,1)S(1)}, bf16[4,80,512]{2,1,0:T(8,128)(2,1)S(1)}, u32[]{:S(2)}, u32[]{:S(2)}) collective-permute-start(bf16[4,80,512]{2,1,0:T(8,128)(2,1)S(1)} %dynamic-slice_bitcast_fusion), channel_id=1, source_target_pairs={{0,16},{16,0},{32,48},{48,32},{64,80},{80,64},{96,112},{112,96},{1... | collective-permute-start | bytes 983048 | tf_op jit(solution)/shard_map/ppermute | solution.py:180
  102.6 13.9 %collective-permute-start.22 = (bf16[80,512]{1,0:T(8,128)(2,1)S(1)}, bf16[80,512]{1,0:T(8,128)(2,1)S(1)}, u32[]{:S(2)}, u32[]{:S(2)}) collective-permute-start(bf16[80,512]{1,0:T(8,128)(2,1)S(1)} %get-tuple-element.98), channel_id=1, source_target_pairs={{0,192},{16,208},{32,224},{48,240},{64,0},{80,16},{96,32},{112,48}... | collective-permute-start | bytes 245768 | tf_op jit(solution)/shard_map/ppermute | solution.py:180
  108.8 9.1 %collective-permute-start.21 = (bf16[80,512]{1,0:T(8,128)(2,1)S(1)}, bf16[80,512]{1,0:T(8,128)(2,1)S(1)}, u32[]{:S(2)}, u32[]{:S(2)}) collective-permute-start(bf16[80,512]{1,0:T(8,128)(2,1)S(1)} %get-tuple-element.99), channel_id=1, source_target_pairs={{0,128},{16,144},{32,160},{48,176},{64,192},{80,208},{96,224},{112... | collective-permute-start | bytes 245768 | tf_op jit(solution)/shard_map/ppermute | solution.py:180
  110.5 8.6 %collective-permute-start.20 = (bf16[80,512]{1,0:T(8,128)(2,1)S(1)}, bf16[80,512]{1,0:T(8,128)(2,1)S(1)}, u32[]{:S(2)}, u32[]{:S(2)}) collective-permute-start(bf16[80,512]{1,0:T(8,128)(2,1)S(1)} %get-tuple-element.100), channel_id=1, source_target_pairs={{0,64},{16,80},{32,96},{48,112},{64,128},{80,144},{96,160},{112,17... | collective-permute-start | bytes 245768 | tf_op jit(solution)/shard_map/ppermute | solution.py:180
  111.7 1.3 %copy-start = (bf16[8,512,256]{2,1,0:T(8,128)(2,1)}, bf16[8,512,256]{2,1,0:T(8,128)(2,1)S(1)}, u32[]{:S(2)}) copy-start(bf16[8,512,256]{2,1,0:T(8,128)(2,1)S(1)} %all-to-all-done.1) | copy-start | bytes 6291460

commit v3 on v2

--- a/solution.py
+++ b/solution.py
@@ -27,9 +27,9 @@
 def fused_kernel(
     info, blk, gain, wk, wv, *refs
 ):
-    far_parts, far_tok, (oc, lead, rest, keep) = refs[:4], refs[4:13], refs[13:17]
-    (kz, vz, kzt, vzt, acck, accv, ki, gs), parts, toks, made, sems = refs[17:25], refs[25:29], refs[29:31], *refs[31:33]
-    ss, pgs, lows, sgs = refs[33:]
+    far_parts, far_tok, (oc, send, keep) = refs[:4], refs[4:13], refs[13:16]
+    (kz, vz, kzt, vzt, acck, accv, ki, gs), parts, toks, made, sems = refs[16:24], refs[24:28], refs[28:30], *refs[30:32]
+    ss, pgs, lows, sgs = refs[32:]
     a0, b0, a1, b1 = parts
     moves = list(zip(far_parts, parts))
     for r in range(8):
@@ -147,11 +147,7 @@
         gs[rows, :] = total.astype(BF16)
     n = keep.shape[1]
     for k in range(4):
-        give = gs[pl.ds(pl.multiple_of((2 * k + 1 - odd) * n, n), n), :]
-        if k == 0:
-            lead[0] = give
-        else:
-            rest[k - 1] = give
+        send[k] = gs[pl.ds(pl.multiple_of((2 * k + 1 - odd) * n, n), n), :]
         keep[k] = gs[pl.ds(pl.multiple_of((2 * k + odd) * n, n), n), :]
     for x in stores:
         x.wait()
@@ -174,6 +170,13 @@
     for r in range(8):
         a[:, r * cols : (r + 1) * cols] = y[r, 0, rows, :]
         b[:, r * cols : (r + 1) * cols] = y[r, 1, rows, :]
+
+
+def total_kernel(a, b, c, d, k, v):
+    total = a[...].astype(F32) + b[...].astype(F32) + c[...].astype(F32) + d[...].astype(F32)
+    n = total.shape[1] // 2
+    k[...] = total[:, None, :n]
+    v[...] = total[:, None, n:]
 
 
 def swap(x, axes, pairs):
@@ -234,13 +237,13 @@
     n_rows = IMAGES * LAT
     gain = jnp.repeat(jnp.tanh(lax.dynamic_slice_in_dim(gate, seq_i * 2, 2)), HD)[None, :]
     rows = kv // 16
-    some = [shape((n, 2 * rows, 4 * HD), BF16) for n in (1, 3, 4)]
+    some = [shape((4, 2 * rows, 4 * HD), BF16)] * 2
     zs, zt = (IMAGES, 2 * LAT, 2 * HD), (IMAGES, 2 * HD, 2 * LAT)
-    oc, lead, rest, keep = pl.pallas_call(
+    oc, send, keep = pl.pallas_call(
         fused_kernel,
         out_shape=(shape((n_seq, 2 * tokens, cols), BF16), *some),
         in_specs=[SMEM, SMEM] + [VMEM] * 3 + [ANY] * 13,
-        out_specs=(ANY, VMEM, VMEM, VMEM),
+        out_specs=(ANY, VMEM, VMEM),
         scratch_shapes=[pltpu.VMEM(x, BF16) for x in (zs, zs, zt, zt)]
         + [pltpu.VMEM((n_rows, 2 * HD), F32)] * 2
         + [pltpu.VMEM((n_rows, 4 * HD), BF16), pltpu.VMEM((kv, 4 * HD), BF16)]
@@ -272,9 +275,8 @@
     def join(x, y):
         return (x.astype(F32) + y.astype(F32)).astype(BF16)
 
-    lead = swap(lead, ("dp", "seq"), pairs)
-    rest = swap(rest, ("dp", "seq"), pairs)
-    lead, oc = lax.optimization_barrier((lead, oc))
+    came = swap(send, ("dp", "seq"), pairs).reshape(4, 2, rows, 4 * HD)
+    keep = keep.reshape(4, 2, rows, 4 * HD)
     flat_out = shape((tokens, width), BF16)
     attended, query_grad = pl.pallas_call(
         spread_kernel,
@@ -285,19 +287,23 @@
         name="spread",
     )(exchange(oc, "seq").reshape(n_seq, 2, tokens, cols))
 
-    part = join(keep, jnp.concatenate([lead, rest], axis=0)).reshape(4, 2, rows, 4 * HD)
-    part = join(pick(part, h_i, 1), swap(pick(part, 1 - h_i, 1), "dp", [(j, j ^ 1) for j in range(16)]))
+    give = join(pick(keep, 1 - h_i, 1), pick(came, 1 - h_i, 1))
+    back = swap(give, "dp", [(j, j ^ 1) for j in range(16)])
+    part = join(join(pick(keep, h_i, 1), pick(came, h_i, 1)), back)
     k_i = z_i // 2
     more = []
     for r in range(1, 4):
         perm = [(z * 2 + h, (z + 2 * r) % 8 * 2 + h) for z in range(8) for h in range(2)]
         more.append(swap(pick(part, (k_i + r) % 4, 0), "dp", perm))
     (attended, query_grad), more = lax.optimization_barrier(((attended, query_grad), more))
-    total = pick(part, k_i, 0).astype(F32)
-    for x in more:
-        total = total + x.astype(F32)
-    key_grad = total[:, : 2 * HD].reshape(rows, 1, 2 * HD)
-    value_grad = total[:, 2 * HD :].reshape(rows, 1, 2 * HD)
+    one = shape((rows, 1, 2 * HD), F32)
+    key_grad, value_grad = pl.pallas_call(
+        total_kernel,
+        out_shape=(one, one),
+        in_specs=[VMEM] * 4,
+        out_specs=(VMEM, VMEM),
+        name="total",
+    )(pick(part, k_i, 0), *more)
     return attended[None], query_grad[None], key_grad, value_grad
 
 

time: 121 us -> 118 us (0.975)
  waiting for transfers between devices: 47.1 us -> 45 us
  Pallas kernels: 19.9 us -> 21.6 us
  starting transfers between devices: 39.8 us -> 38.3 us
  local copies, waits for them, and re-layouts: 9.55 us -> 8.17 us
    ppermute x23 -> x22, waiting for transfers between devices: 47.1 us -> 45 us  [swap(): return lax.ppermute(x, axes, pairs)]
    pallas_call x0 -> x1, Pallas kernels: none -> 1.72 us  [body(): pl.pallas_call(total_kernel, out_shape=(one, one), in_specs=[VMEM] * 4, o...]
    ppermute x23 -> x22, starting transfers between devices: 28 us -> 26.5 us  [swap(): return lax.ppermute(x, axes, pairs)]
    reshape x2 -> x0, local copies, waits for them, and re-layouts: 1.38 us -> none  [the longest x1 0.69 us: body(): value_grad = total[:, 2 * HD:].reshape(rows, 1, 2 * HD)]
    unnamed x36 -> x38, local copies, waits for them, and re-layouts: 3.35 us -> 2.77 us
  transfers between devices with their start and end apart: 25 -> 24, of which waited for: 16 -> 15; matrix products, arithmetic and copies ran while one was open for 4% -> 5% of each run, Pallas kernels for 5% -> 6%
where the time goes in v3:
time: 118 us
  waiting for transfers between devices  45 us (38%)
  starting transfers between devices  38.3 us (32%)
  Pallas kernels  21.6 us (18%)
  local copies, waits for them, and re-layouts  8.17 us (7%)
  other arithmetic  3.66 us (3%)
    ppermute x22, waiting for transfers between devices, swap(): return lax.ppermute(x, axes, pairs)  45 us
    ppermute x22, starting transfers between devices, swap(): return lax.ppermute(x, axes, pairs)  26.5 us
    pallas_call x1, Pallas kernels, body(): pl.pallas_call(fused_kernel, out_shape=(shape((n_seq, 2 * tokens, cols),...  13.3 us
    all_to_all x2, starting transfers between devices, exchange(): lax.all_to_all(x, axes, split_axis=0, concat_axis=0, tiled=True, **kw)  11.8 us
    pallas_call x1, Pallas kernels, body(): pl.pallas_call(spread_kernel, grid=(tokens // 64,), out_shape=(flat_out,...  3.45 us
    pallas_call x1, Pallas kernels, body(): pl.pallas_call(rotate_kernel, out_shape=[shape((2, tokens, cols), BF16)]...  3.16 us
    unnamed x38, local copies, waits for them, and re-layouts  2.77 us
  transfers between devices with their start and end apart: 24, of which 15 were waited for; matrix products, arithmetic and copies ran while one was open for 5% of the time, Pallas kernels for 6%

profile of v3, /device:TPU:38, one launch (start us, length us, event | category | flops | bytes accessed | tf_op | source)
XLA Modules:
  0.0 117.6 jit_solution(14231982530577269928)
XLA Ops:
  0.6 1.1 reshape_squeeze.3
  1.8 0.8 copy.20
  2.6 5.8 %all-to-all-start = ((bf16[16,24,640]{2,1,0:T(8,128)(2,1)}), bf16[16,24,640]{2,1,0:T(8,128)(2,1)S(1)}, u32[]{:S(2)}, u32[]{:S(2)}) async-start(bf16[16,24,640]{2,1,0:T(8,128)(2,1)} %bitcast.9), calls=%async_computation | async-start | bytes 983040 | tf_op jit(solution)/shard_map/all_to_all | solution.py:187
  8.4 0.6 pad_add_fusion.info
  9.0 3.2 %rotate.1 = (bf16[2,256,256]{2,1,0:T(8,128)(2,1)}, bf16[2,256,256]{2,1,0:T(8,128)(2,1)}, bf16[2,256,256]{2,1,0:T(8,128)(2,1)}, bf16[2,256,256]{2,1,0:T(8,128)(2,...) custom-call(s32[3]{0:T(128)} %pad_add_fusion.info, bf16[256,2048]{1,0:T(8,128)(2,1)} %bitcast.60, ...), custom_call_target="tpu_custom_call" | custom-call | tf_op jit(solution)/shard_map/rotate/pallas_call | solution.py:212
  12.3 1.9 %collective-permute-start.1 = (bf16[2,256,256]{2,1,0:T(8,128)(2,1)}, bf16[2,256,256]{2,1,0:T(8,128)(2,1)S(1)}, u32[]{:S(2)}, u32[]{:S(2)}) collective-permute-start(bf16[2,256,256]{2,1,0:T(8,128)(2,1)} %get-tuple-element.47), channel_id=1, source_target_pairs={{0,12},{2,14},{4,0},{6,2},{8,4},{10,6},{12,8},{14,10},{1,13},{3,15... | collective-permute-start | bytes 786440 | tf_op jit(solution)/shard_map/ppermute | solution.py:183
  14.4 1.1 fusion.4
  15.6 0.7 collective-permute-done.2
  16.4 0.7 pad_maximum_fusion.3
  17.2 4.2 %collective-permute-done.refs_5_ = bf16[2,256,256]{2,1,0:T(8,128)(2,1)S(1)} collective-permute-done((bf16[2,256,256]{2,1,0:T(8,128)(2,1)}, bf16[2,256,256]{2,1,0:T(8,128)(2,1)S(1)}, u32[]{:S(2)}, u32[]{:S(2)}) %collective-permute-start) | collective-permute-done | bytes 262176 | tf_op jit(solution)/shard_map/ppermute | solution.py:183
  21.4 0.7 collective-permute-done.1.refs_7_
  22.0 0.6 gather_fusion
  22.7 1.8 %collective-permute-start.6 = (bf16[128,640]{1,0:T(8,128)(2,1)S(1)}, bf16[128,640]{1,0:T(8,128)(2,1)S(1)}, u32[]{:S(2)}, u32[]{:S(2)}) collective-permute-start(bf16[128,640]{1,0:T(8,128)(2,1)S(1)} %bitcast_select_fusion), channel_id=1, source_target_pairs={{0,1},{1,0},{2,3},{3,2},{4,5},{5,4},{6,7},{7,6},{8,9},{9,8},{10,11... | collective-permute-start | bytes 491528 | tf_op jit(solution)/shard_map/ppermute | solution.py:183
  24.5 1.2 %collective-permute-start.5 = (bf16[128,640]{1,0:T(8,128)(2,1)S(1)}, bf16[128,640]{1,0:T(8,128)(2,1)S(1)}, u32[]{:S(2)}, u32[]{:S(2)}) collective-permute-start(bf16[128,640]{1,0:T(8,128)(2,1)S(1)} %bitcast_select_fusion), channel_id=1, source_target_pairs={{0,8},{2,10},{4,12},{6,14},{8,0},{10,2},{12,4},{14,6},{1,9},{3,11}... | collective-permute-start | bytes 491528 | tf_op jit(solution)/shard_map/ppermute | solution.py:183
  25.7 1.2 %collective-permute-start.4 = (bf16[128,640]{1,0:T(8,128)(2,1)S(1)}, bf16[128,640]{1,0:T(8,128)(2,1)S(1)}, u32[]{:S(2)}, u32[]{:S(2)}) collective-permute-start(bf16[128,640]{1,0:T(8,128)(2,1)S(1)} %bitcast_select_fusion), channel_id=1, source_target_pairs={{0,12},{2,14},{4,0},{6,2},{8,4},{10,6},{12,8},{14,10},{1,13},{3,15... | collective-permute-start | bytes 491528 | tf_op jit(solution)/shard_map/ppermute | solution.py:183
  26.9 2.1 %collective-permute-start.3 = (bf16[128,640]{1,0:T(8,128)(2,1)S(1)}, bf16[128,640]{1,0:T(8,128)(2,1)S(1)}, u32[]{:S(2)}, u32[]{:S(2)}) collective-permute-start(bf16[128,640]{1,0:T(8,128)(2,1)S(1)} %bitcast_select_fusion), channel_id=1, source_target_pairs={{0,4},{2,6},{4,8},{6,10},{8,12},{10,14},{12,0},{14,2},{1,5},{3,7},... | collective-permute-start | bytes 491528 | tf_op jit(solution)/shard_map/ppermute | solution.py:183
  28.9 1.1 collective-permute-start.7
  30.0 3.1 %collective-permute-done.5 = bf16[128,640]{1,0:T(8,128)(2,1)S(1)} collective-permute-done((bf16[128,640]{1,0:T(8,128)(2,1)S(1)}, bf16[128,640]{1,0:T(8,128)(2,1)S(1)}, u32[]{:S(2)}, u32[]{:S(2)}) %collective-permute-start.5) | collective-permute-done | bytes 163872 | tf_op jit(solution)/shard_map/ppermute | solution.py:183
  33.2 3.5 %collective-permute-done.4 = bf16[128,640]{1,0:T(8,128)(2,1)S(1)} collective-permute-done((bf16[128,640]{1,0:T(8,128)(2,1)S(1)}, bf16[128,640]{1,0:T(8,128)(2,1)S(1)}, u32[]{:S(2)}, u32[]{:S(2)}) %collective-permute-start.4) | collective-permute-done | bytes 163872 | tf_op jit(solution)/shard_map/ppermute | solution.py:183
  36.6 0.4 collective-permute-start.11
  37.0 1.7 %collective-permute-start.8 = (bf16[2,256,256]{2,1,0:T(8,128)(2,1)S(1)}, bf16[2,256,256]{2,1,0:T(8,128)(2,1)S(1)}, u32[]{:S(2)}, u32[]{:S(2)}) collective-permute-start(bf16[2,256,256]{2,1,0:T(8,128)(2,1)S(1)} %get-tuple-element.65), channel_id=1, source_target_pairs={{0,4},{2,6},{4,8},{6,10},{8,12},{10,14},{12,0},{14,2},{1,5},{3,7},... | collective-permute-start | bytes 786440 | tf_op jit(solution)/shard_map/ppermute | solution.py:183
  38.7 0.9 collective-permute-start.9
  39.9 1.5 %collective-permute-start.12 = (bf16[128,640]{1,0:T(8,128)(2,1)S(1)}, bf16[128,640]{1,0:T(8,128)(2,1)S(1)}, u32[]{:S(2)}, u32[]{:S(2)}) collective-permute-start(bf16[128,640]{1,0:T(8,128)(2,1)S(1)} %collective-permute-done.4), channel_id=1, source_target_pairs={{0,1},{1,0},{2,3},{3,2},{4,5},{5,4},{6,7},{7,6},{8,9},{9,8},{10,11... | collective-permute-start | bytes 491528 | tf_op jit(solution)/shard_map/ppermute | solution.py:183
  41.5 2.1 %collective-permute-done.11 = bf16[128,640]{1,0:T(8,128)(2,1)S(1)} collective-permute-done((bf16[128,640]{1,0:T(8,128)(2,1)S(1)}, bf16[128,640]{1,0:T(8,128)(2,1)S(1)}, u32[]{:S(2)}, u32[]{:S(2)}) %collective-permute-start.11) | collective-permute-done | bytes 163872 | tf_op jit(solution)/shard_map/ppermute | solution.py:183
  43.8 3.3 %collective-permute-done.12 = bf16[128,640]{1,0:T(8,128)(2,1)S(1)} collective-permute-done((bf16[128,640]{1,0:T(8,128)(2,1)S(1)}, bf16[128,640]{1,0:T(8,128)(2,1)S(1)}, u32[]{:S(2)}, u32[]{:S(2)}) %collective-permute-start.12) | collective-permute-done | bytes 163872 | tf_op jit(solution)/shard_map/ppermute | solution.py:183
  47.1 1.9 %collective-permute-done.13 = bf16[128,640]{1,0:T(8,128)(2,1)S(1)} collective-permute-done((bf16[128,640]{1,0:T(8,128)(2,1)S(1)}, bf16[128,640]{1,0:T(8,128)(2,1)S(1)}, u32[]{:S(2)}, u32[]{:S(2)}) %collective-permute-start.13) | collective-permute-done | bytes 163872 | tf_op jit(solution)/shard_map/ppermute | solution.py:183
  49.0 2.2 %collective-permute-done.10.refs_12_ = bf16[2,256,256]{2,1,0:T(8,128)(2,1)S(1)} collective-permute-done((bf16[2,256,256]{2,1,0:T(8,128)(2,1)S(1)}, bf16[2,256,256]{2,1,0:T(8,128)(2,1)S(1)}, u32[]{:S(2)}, u32[]{:S(2)}) %collective-permute-start.10) | collective-permute-done | bytes 262176 | tf_op jit(solution)/shard_map/ppermute | solution.py:183
  51.5 0.4 copy-done.16
  51.9 0.3 collective-permute-start.16
  52.3 2.0 %collective-permute-done.16.refs_8_ = bf16[4,256,256]{2,1,0:T(8,128)(2,1)S(1)} collective-permute-done((bf16[4,256,256]{2,1,0:T(8,128)(2,1)S(1)}, bf16[4,256,256]{2,1,0:T(8,128)(2,1)S(1)}, u32[]{:S(2)}, u32[]{:S(2)}) %collective-permute-start.16) | collective-permute-done | bytes 524320 | tf_op jit(solution)/shard_map/ppermute | solution.py:183
  54.3 0.7 broadcast_in_dim.23
  55.1 0.2 copy-done.11
  55.3 13.3 %fused.1 = (bf16[8,512,256]{2,1,0:T(8,128)(2,1)}, bf16[4,160,512]{2,1,0:T(8,128)(2,1)}, bf16[4,160,512]{2,1,0:T(8,128)(2,1)}) custom-call(s32[3]{0:T(128)} %pad_add_fusion.info, s32[64]{0:T(128)} %bitcast.79, f32[1,256]{1,0:T(1,128)} %bitcast.80, bf16[1280,256]{1,0:T(8,128)(2,1)} %bitcast.77, bf16[1280,256]{1,0:T(8,128)(2,1)} %bitcast.78, ...), custom_call_target="tpu_custom_call" | custom-call | flops 8589934592 | bytes 16777216 | tf_op jit(solution)/shard_map/fused/pallas_call | solution.py:242
  68.6 6.0 %all-to-all-start.1 = ((bf16[8,512,256]{2,1,0:T(8,128)(2,1)}), bf16[8,512,256]{2,1,0:T(8,128)(2,1)S(1)}, u32[]{:S(2)}, u32[]{:S(2)}) async-start(bf16[8,512,256]{2,1,0:T(8,128)(2,1)} %get-tuple-element.76), calls=%async_computation.1 | async-start | bytes 4194304 | tf_op jit(solution)/shard_map/all_to_all | solution.py:187
  74.8 10.7 %collective-permute-done.17 = bf16[4,160,512]{2,1,0:T(8,128)(2,1)S(1)} collective-permute-done((bf16[4,160,512]{2,1,0:T(8,128)(2,1)}, bf16[4,160,512]{2,1,0:T(8,128)(2,1)S(1)}, u32[]{:S(2)}, u32[]{:S(2)}) %collective-permute-start.17) | collective-permute-done | bytes 655392 | tf_op jit(solution)/shard_map/ppermute | solution.py:183
  85.4 0.8 fusion.2
  86.3 2.9 %collective-permute-start.18 = (bf16[4,80,512]{2,1,0:T(8,128)(2,1)}, bf16[4,80,512]{2,1,0:T(8,128)(2,1)}, u32[]{:S(2)}, u32[]{:S(2)}) collective-permute-start(bf16[4,80,512]{2,1,0:T(8,128)(2,1)} %fusion.2), channel_id=1, source_target_pairs={{0,16},{16,0},{32,48},{48,32},{64,80},{80,64},{96,112},{112,96},{1... | collective-permute-start | bytes 983048 | tf_op jit(solution)/shard_map/ppermute | solution.py:183
  89.1 8.0 %collective-permute-done.18 = bf16[4,80,512]{2,1,0:T(8,128)(2,1)} collective-permute-done((bf16[4,80,512]{2,1,0:T(8,128)(2,1)}, bf16[4,80,512]{2,1,0:T(8,128)(2,1)}, u32[]{:S(2)}, u32[]{:S(2)}) %collective-permute-start.18) | collective-permute-done | bytes 327712 | tf_op jit(solution)/shard_map/ppermute | solution.py:183
  97.2 1.1 fusion
  98.3 0.7 dynamic-slice_bitcast_fusion
  98.9 6.4 %collective-permute-start.21 = (bf16[80,512]{1,0:T(8,128)(2,1)S(1)}, bf16[80,512]{1,0:T(8,128)(2,1)S(1)}, u32[]{:S(2)}, u32[]{:S(2)}) collective-permute-start(bf16[80,512]{1,0:T(8,128)(2,1)S(1)} %get-tuple-element.97), channel_id=1, source_target_pairs={{0,192},{16,208},{32,224},{48,240},{64,0},{80,16},{96,32},{112,48}... | collective-permute-start | bytes 245768 | tf_op jit(solution)/shard_map/ppermute | solution.py:183
  105.4 1.6 %collective-permute-start.20 = (bf16[80,512]{1,0:T(8,128)(2,1)S(1)}, bf16[80,512]{1,0:T(8,128)(2,1)S(1)}, u32[]{:S(2)}, u32[]{:S(2)}) collective-permute-start(bf16[80,512]{1,0:T(8,128)(2,1)S(1)} %get-tuple-element.98), channel_id=1, source_target_pairs={{0,128},{16,144},{32,160},{48,176},{64,192},{80,208},{96,224},{112... | collective-permute-start | bytes 245768 | tf_op jit(solution)/shard_map/ppermute | solution.py:183
  107.0 1.0 collective-permute-start.19
  108.0 1.3 %copy-done = bf16[8,512,256]{2,1,0:T(8,128)(2,1)} copy-done((bf16[8,512,256]{2,1,0:T(8,128)(2,1)}, bf16[8,512,256]{2,1,0:T(8,128)(2,1)S(1)}, u32[]{:S(2)}) %copy-start) | copy-done | bytes 2097176
  109.3 3.4 %spread.1 = (bf16[256,2048]{1,0:T(8,128)(2,1)}, bf16[256,2048]{1,0:T(8,128)(2,1)}) custom-call(bf16[8,2,256,256]{3,2,1,0:T(8,128)(2,1)} %bitcast.58), custom_call_target="tpu_custom_call" | custom-call | tf_op jit(solution)/shard_map/spread/pallas_call | solution.py:281
  112.7 2.3 %collective-permute-done.20.c = bf16[80,512]{1,0:T(8,128)(2,1)S(1)} collective-permute-done((bf16[80,512]{1,0:T(8,128)(2,1)S(1)}, bf16[80,512]{1,0:T(8,128)(2,1)S(1)}, u32[]{:S(2)}, u32[]{:S(2)}) %collective-permute-start.20) | collective-permute-done | bytes 81952 | tf_op jit(solution)/shard_map/ppermute | solution.py:183
  115.2 0.5 copy-done.5
  115.9 1.7 %total.1 = (f32[80,1,256]{2,1,0:T(1,128)}, f32[80,1,256]{2,1,0:T(1,128)}) custom-call(bf16[80,512]{1,0:T(8,128)(2,1)} %get-tuple-element.96.a, bf16[80,512]{1,0:T(8,128)(2,1)} %copy-done.6, bf16[80,512]{1,0:T(8,128)(2,1)} %copy-done.5, bf16[80,512]{1,0:T(8,128)(2,1)} %copy-done.4), custom_call_target="tpu_custom_call" | custom-call | tf_op jit(solution)/shard_map/total/pallas_call | solution.py:300
  (68 shorter events, 1.8 us)
Async XLA Ops:
  1.8 12.4 %copy-start.17 = (s32[1,16]{1,0:T(1,128)S(1)}, s32[1,16]{1,0:T(1,128)}, u32[]{:S(2)}) copy-start(s32[1,16]{1,0:T(1,128)} %param.10) | copy-start | bytes 196
  2.6 19.4 %all-to-all-start = ((bf16[16,24,640]{2,1,0:T(8,128)(2,1)}), bf16[16,24,640]{2,1,0:T(8,128)(2,1)S(1)}, u32[]{:S(2)}, u32[]{:S(2)}) async-start(bf16[16,24,640]{2,1,0:T(8,128)(2,1)} %bitcast.9), calls=%async_computation | async-start | bytes 983040 | tf_op jit(solution)/shard_map/all_to_all | solution.py:187
  12.2 9.2 %collective-permute-start = (bf16[2,256,256]{2,1,0:T(8,128)(2,1)}, bf16[2,256,256]{2,1,0:T(8,128)(2,1)S(1)}, u32[]{:S(2)}, u32[]{:S(2)}) collective-permute-start(bf16[2,256,256]{2,1,0:T(8,128)(2,1)} %get-tuple-element.46), channel_id=1, source_target_pairs={{0,4},{2,6},{4,8},{6,10},{8,12},{10,14},{12,0},{14,2},{1,5},{3,7},... | collective-permute-start | bytes 786440 | tf_op jit(solution)/shard_map/ppermute | solution.py:183
  12.3 9.7 %collective-permute-start.1 = (bf16[2,256,256]{2,1,0:T(8,128)(2,1)}, bf16[2,256,256]{2,1,0:T(8,128)(2,1)S(1)}, u32[]{:S(2)}, u32[]{:S(2)}) collective-permute-start(bf16[2,256,256]{2,1,0:T(8,128)(2,1)} %get-tuple-element.47), channel_id=1, source_target_pairs={{0,12},{2,14},{4,0},{6,2},{8,4},{10,6},{12,8},{14,10},{1,13},{3,15... | collective-permute-start | bytes 786440 | tf_op jit(solution)/shard_map/ppermute | solution.py:183
  14.2 2.1 %collective-permute-start.2 = (bf16[4,256,256]{2,1,0:T(8,128)(2,1)}, bf16[4,256,256]{2,1,0:T(8,128)(2,1)S(1)}, u32[]{:S(2)}, u32[]{:S(2)}) collective-permute-start(bf16[4,256,256]{2,1,0:T(8,128)(2,1)} %get-tuple-element.49), channel_id=1, source_target_pairs={{0,2},{2,0},{4,6},{6,4},{8,10},{10,8},{12,14},{14,12},{1,3},{3,1},... | collective-permute-start | bytes 1572872 | tf_op jit(solution)/shard_map/ppermute | solution.py:183
  15.6 13.4 %copy-start.13 = (bf16[2,256,256]{2,1,0:T(8,128)(2,1)S(1)}, bf16[2,256,256]{2,1,0:T(8,128)(2,1)}, u32[]{:S(2)}) copy-start(bf16[2,256,256]{2,1,0:T(8,128)(2,1)} %get-tuple-element.63) | copy-start | bytes 786436
  15.6 24.3 %copy-start.7 = (bf16[2,256,256]{2,1,0:T(8,128)(2,1)S(1)}, bf16[2,256,256]{2,1,0:T(8,128)(2,1)}, u32[]{:S(2)}) copy-start(bf16[2,256,256]{2,1,0:T(8,128)(2,1)} %get-tuple-element.61.refs_4_) | copy-start | bytes 786436
  21.4 29.9 %copy-start.8 = (bf16[2,256,256]{2,1,0:T(8,128)(2,1)}, bf16[2,256,256]{2,1,0:T(8,128)(2,1)S(1)}, u32[]{:S(2)}) copy-start(bf16[2,256,256]{2,1,0:T(8,128)(2,1)S(1)} %collective-permute-done.refs_5_) | copy-start | bytes 786436
  22.0 29.3 %copy-start.9 = (bf16[2,256,256]{2,1,0:T(8,128)(2,1)}, bf16[2,256,256]{2,1,0:T(8,128)(2,1)S(1)}, u32[]{:S(2)}) copy-start(bf16[2,256,256]{2,1,0:T(8,128)(2,1)S(1)} %collective-permute-done.1.refs_7_) | copy-start | bytes 786436
  22.7 7.3 %collective-permute-start.6 = (bf16[128,640]{1,0:T(8,128)(2,1)S(1)}, bf16[128,640]{1,0:T(8,128)(2,1)S(1)}, u32[]{:S(2)}, u32[]{:S(2)}) collective-permute-start(bf16[128,640]{1,0:T(8,128)(2,1)S(1)} %bitcast_select_fusion), channel_id=1, source_target_pairs={{0,1},{1,0},{2,3},{3,2},{4,5},{5,4},{6,7},{7,6},{8,9},{9,8},{10,11... | collective-permute-start | bytes 491528 | tf_op jit(solution)/shard_map/ppermute | solution.py:183
  24.5 8.7 %collective-permute-start.5 = (bf16[128,640]{1,0:T(8,128)(2,1)S(1)}, bf16[128,640]{1,0:T(8,128)(2,1)S(1)}, u32[]{:S(2)}, u32[]{:S(2)}) collective-permute-start(bf16[128,640]{1,0:T(8,128)(2,1)S(1)} %bitcast_select_fusion), channel_id=1, source_target_pairs={{0,8},{2,10},{4,12},{6,14},{8,0},{10,2},{12,4},{14,6},{1,9},{3,11}... | collective-permute-start | bytes 491528 | tf_op jit(solution)/shard_map/ppermute | solution.py:183
  25.7 10.9 %collective-permute-start.4 = (bf16[128,640]{1,0:T(8,128)(2,1)S(1)}, bf16[128,640]{1,0:T(8,128)(2,1)S(1)}, u32[]{:S(2)}, u32[]{:S(2)}) collective-permute-start(bf16[128,640]{1,0:T(8,128)(2,1)S(1)} %bitcast_select_fusion), channel_id=1, source_target_pairs={{0,12},{2,14},{4,0},{6,2},{8,4},{10,6},{12,8},{14,10},{1,13},{3,15... | collective-permute-start | bytes 491528 | tf_op jit(solution)/shard_map/ppermute | solution.py:183
  26.9 9.8 %collective-permute-start.3 = (bf16[128,640]{1,0:T(8,128)(2,1)S(1)}, bf16[128,640]{1,0:T(8,128)(2,1)S(1)}, u32[]{:S(2)}, u32[]{:S(2)}) collective-permute-start(bf16[128,640]{1,0:T(8,128)(2,1)S(1)} %bitcast_select_fusion), channel_id=1, source_target_pairs={{0,4},{2,6},{4,8},{6,10},{8,12},{10,14},{12,0},{14,2},{1,5},{3,7},... | collective-permute-start | bytes 491528 | tf_op jit(solution)/shard_map/ppermute | solution.py:183
  28.9 11.0 %collective-permute-start.7 = (bf16[2,256,256]{2,1,0:T(8,128)(2,1)S(1)}, bf16[2,256,256]{2,1,0:T(8,128)(2,1)S(1)}, u32[]{:S(2)}, u32[]{:S(2)}) collective-permute-start(bf16[2,256,256]{2,1,0:T(8,128)(2,1)S(1)} %copy-done.13), channel_id=1, source_target_pairs={{0,8},{2,10},{4,12},{6,14},{8,0},{10,2},{12,4},{14,6},{1,9},{3,11}... | collective-permute-start | bytes 786440 | tf_op jit(solution)/shard_map/ppermute | solution.py:183
  36.6 6.9 %collective-permute-start.11 = (bf16[128,640]{1,0:T(8,128)(2,1)S(1)}, bf16[128,640]{1,0:T(8,128)(2,1)S(1)}, u32[]{:S(2)}, u32[]{:S(2)}) collective-permute-start(bf16[128,640]{1,0:T(8,128)(2,1)S(1)} %collective-permute-done.3), channel_id=1, source_target_pairs={{0,1},{1,0},{2,3},{3,2},{4,5},{5,4},{6,7},{7,6},{8,9},{9,8},{10,11... | collective-permute-start | bytes 491528 | tf_op jit(solution)/shard_map/ppermute | solution.py:183
  37.0 12.0 %collective-permute-start.8 = (bf16[2,256,256]{2,1,0:T(8,128)(2,1)S(1)}, bf16[2,256,256]{2,1,0:T(8,128)(2,1)S(1)}, u32[]{:S(2)}, u32[]{:S(2)}) collective-permute-start(bf16[2,256,256]{2,1,0:T(8,128)(2,1)S(1)} %get-tuple-element.65), channel_id=1, source_target_pairs={{0,4},{2,6},{4,8},{6,10},{8,12},{10,14},{12,0},{14,2},{1,5},{3,7},... | collective-permute-start | bytes 786440 | tf_op jit(solution)/shard_map/ppermute | solution.py:183
  38.7 10.3 %collective-permute-start.9 = (bf16[2,256,256]{2,1,0:T(8,128)(2,1)S(1)}, bf16[2,256,256]{2,1,0:T(8,128)(2,1)S(1)}, u32[]{:S(2)}, u32[]{:S(2)}) collective-permute-start(bf16[2,256,256]{2,1,0:T(8,128)(2,1)S(1)} %get-tuple-element.66), channel_id=1, source_target_pairs={{0,8},{2,10},{4,12},{6,14},{8,0},{10,2},{12,4},{14,6},{1,9},{3,11}... | collective-permute-start | bytes 786440 | tf_op jit(solution)/shard_map/ppermute | solution.py:183
  39.7 11.5 %collective-permute-start.10 = (bf16[2,256,256]{2,1,0:T(8,128)(2,1)S(1)}, bf16[2,256,256]{2,1,0:T(8,128)(2,1)S(1)}, u32[]{:S(2)}, u32[]{:S(2)}) collective-permute-start(bf16[2,256,256]{2,1,0:T(8,128)(2,1)S(1)} %get-tuple-element.67), channel_id=1, source_target_pairs={{0,12},{2,14},{4,0},{6,2},{8,4},{10,6},{12,8},{14,10},{1,13},{3,15... | collective-permute-start | bytes 786440 | tf_op jit(solution)/shard_map/ppermute | solution.py:183
  39.9 12.3 %copy-start.18 = (f32[16]{0:T(128)S(1)}, f32[16]{0:T(128)}, u32[]{:S(2)}) copy-start(f32[16]{0:T(128)} %param.14) | copy-start | bytes 196
  39.9 3.7 %copy-start.10 = (bf16[2,256,256]{2,1,0:T(8,128)(2,1)}, bf16[2,256,256]{2,1,0:T(8,128)(2,1)S(1)}, u32[]{:S(2)}) copy-start(bf16[2,256,256]{2,1,0:T(8,128)(2,1)S(1)} %collective-permute-done.7.refs_6_) | copy-start | bytes 786436
  39.9 7.1 %collective-permute-start.12 = (bf16[128,640]{1,0:T(8,128)(2,1)S(1)}, bf16[128,640]{1,0:T(8,128)(2,1)S(1)}, u32[]{:S(2)}, u32[]{:S(2)}) collective-permute-start(bf16[128,640]{1,0:T(8,128)(2,1)S(1)} %collective-permute-done.4), channel_id=1, source_target_pairs={{0,1},{1,0},{2,3},{3,2},{4,5},{5,4},{6,7},{7,6},{8,9},{9,8},{10,11... | collective-permute-start | bytes 491528 | tf_op jit(solution)/shard_map/ppermute | solution.py:183
  43.6 5.4 %collective-permute-start.13 = (bf16[128,640]{1,0:T(8,128)(2,1)S(1)}, bf16[128,640]{1,0:T(8,128)(2,1)S(1)}, u32[]{:S(2)}, u32[]{:S(2)}) collective-permute-start(bf16[128,640]{1,0:T(8,128)(2,1)S(1)} %collective-permute-done.5), channel_id=1, source_target_pairs={{0,1},{1,0},{2,3},{3,2},{4,5},{5,4},{6,7},{7,6},{8,9},{9,8},{10,11... | collective-permute-start | bytes 491528 | tf_op jit(solution)/shard_map/ppermute | solution.py:183
  43.7 11.3 %copy-start.2 = (bf16[4,128,640]{2,1,0:T(8,128)(2,1)}, bf16[4,128,640]{2,1,0:T(8,128)(2,1)S(1)}, u32[]{:S(2)}) copy-start(bf16[4,128,640]{2,1,0:T(8,128)(2,1)S(1)} %pad_maximum_fusion.refs_0_) | copy-start | bytes 1966084
  47.1 5.2 %collective-permute-start.14 = (bf16[4,128,640]{2,1,0:T(8,128)(2,1)S(1)}, bf16[4,128,640]{2,1,0:T(8,128)(2,1)}, u32[]{:S(2)}, u32[]{:S(2)}) collective-permute-start(bf16[4,128,640]{2,1,0:T(8,128)(2,1)S(1)} %pad_maximum_fusion.refs_0_), channel_id=1, source_target_pairs={{0,2},{2,0},{4,6},{6,4},{8,10},{10,8},{12,14},{14,12},{1,3},{3,1},... | collective-permute-start | bytes 1966088 | tf_op jit(solution)/shard_map/ppermute | solution.py:183
  49.0 2.5 %copy-start.14 = (bf16[2,256,256]{2,1,0:T(8,128)(2,1)}, bf16[2,256,256]{2,1,0:T(8,128)(2,1)S(1)}, u32[]{:S(2)}) copy-start(bf16[2,256,256]{2,1,0:T(8,128)(2,1)S(1)} %collective-permute-done.8.refs_10_) | copy-start | bytes 786436
  49.0 2.5 %copy-start.15 = (bf16[2,256,256]{2,1,0:T(8,128)(2,1)}, bf16[2,256,256]{2,1,0:T(8,128)(2,1)S(1)}, u32[]{:S(2)}) copy-start(bf16[2,256,256]{2,1,0:T(8,128)(2,1)S(1)} %collective-permute-done.9.refs_11_) | copy-start | bytes 786436
  51.2 0.7 copy-start.16
  51.3 3.7 %copy-start.3 = (bf16[4,128,640]{2,1,0:T(8,128)(2,1)}, bf16[4,128,640]{2,1,0:T(8,128)(2,1)S(1)}, u32[]{:S(2)}) copy-start(bf16[4,128,640]{2,1,0:T(8,128)(2,1)S(1)} %pad_maximum_fusion.1.refs_1_) | copy-start | bytes 1966084
  51.3 2.9 %collective-permute-start.15 = (bf16[4,128,640]{2,1,0:T(8,128)(2,1)S(1)}, bf16[4,128,640]{2,1,0:T(8,128)(2,1)S(1)}, u32[]{:S(2)}, u32[]{:S(2)}) collective-permute-start(bf16[4,128,640]{2,1,0:T(8,128)(2,1)S(1)} %pad_maximum_fusion.1.refs_1_), channel_id=1, source_target_pairs={{0,2},{2,0},{4,6},{6,4},{8,10},{10,8},{12,14},{14,12},{1,3},{3,1},... | collective-permute-start | bytes 1966088 | tf_op jit(solution)/shard_map/ppermute | solution.py:183
  51.9 2.4 %collective-permute-start.16 = (bf16[4,256,256]{2,1,0:T(8,128)(2,1)S(1)}, bf16[4,256,256]{2,1,0:T(8,128)(2,1)S(1)}, u32[]{:S(2)}, u32[]{:S(2)}) collective-permute-start(bf16[4,256,256]{2,1,0:T(8,128)(2,1)S(1)} %pad_maximum_fusion.2), channel_id=1, source_target_pairs={{0,2},{2,0},{4,6},{6,4},{8,10},{10,8},{12,14},{14,12},{1,3},{3,1},... | collective-permute-start | bytes 1572872 | tf_op jit(solution)/shard_map/ppermute | solution.py:183
  54.3 0.8 copy-start.12
  54.3 1.0 copy-start.11
  68.6 16.8 %copy-start.1 = (bf16[4,160,512]{2,1,0:T(8,128)(2,1)S(1)}, bf16[4,160,512]{2,1,0:T(8,128)(2,1)}, u32[]{:S(2)}) copy-start(bf16[4,160,512]{2,1,0:T(8,128)(2,1)} %get-tuple-element.79) | copy-start | bytes 1966084
  68.6 39.3 %all-to-all-start.1 = ((bf16[8,512,256]{2,1,0:T(8,128)(2,1)}), bf16[8,512,256]{2,1,0:T(8,128)(2,1)S(1)}, u32[]{:S(2)}, u32[]{:S(2)}) async-start(bf16[8,512,256]{2,1,0:T(8,128)(2,1)} %get-tuple-element.76), calls=%async_computation.1 | async-start | bytes 4194304 | tf_op jit(solution)/shard_map/all_to_all | solution.py:187
  74.6 10.8 %collective-permute-start.17 = (bf16[4,160,512]{2,1,0:T(8,128)(2,1)}, bf16[4,160,512]{2,1,0:T(8,128)(2,1)S(1)}, u32[]{:S(2)}, u32[]{:S(2)}) collective-permute-start(bf16[4,160,512]{2,1,0:T(8,128)(2,1)} %get-tuple-element.80), channel_id=1, source_target_pairs={{0,32},{2,226},{4,36},{6,230},{8,40},{10,234},{12,44},{14,238},{16... | collective-permute-start | bytes 1966088 | tf_op jit(solution)/shard_map/ppermute | solution.py:183
  86.3 10.9 %collective-permute-start.18 = (bf16[4,80,512]{2,1,0:T(8,128)(2,1)}, bf16[4,80,512]{2,1,0:T(8,128)(2,1)}, u32[]{:S(2)}, u32[]{:S(2)}) collective-permute-start(bf16[4,80,512]{2,1,0:T(8,128)(2,1)} %fusion.2), channel_id=1, source_target_pairs={{0,16},{16,0},{32,48},{48,32},{64,80},{80,64},{96,112},{112,96},{1... | collective-permute-start | bytes 983048 | tf_op jit(solution)/shard_map/ppermute | solution.py:183
  98.9 13.8 %collective-permute-start.21 = (bf16[80,512]{1,0:T(8,128)(2,1)S(1)}, bf16[80,512]{1,0:T(8,128)(2,1)S(1)}, u32[]{:S(2)}, u32[]{:S(2)}) collective-permute-start(bf16[80,512]{1,0:T(8,128)(2,1)S(1)} %get-tuple-element.97), channel_id=1, source_target_pairs={{0,192},{16,208},{32,224},{48,240},{64,0},{80,16},{96,32},{112,48}... | collective-permute-start | bytes 245768 | tf_op jit(solution)/shard_map/ppermute | solution.py:183
  105.4 9.7 %collective-permute-start.20 = (bf16[80,512]{1,0:T(8,128)(2,1)S(1)}, bf16[80,512]{1,0:T(8,128)(2,1)S(1)}, u32[]{:S(2)}, u32[]{:S(2)}) collective-permute-start(bf16[80,512]{1,0:T(8,128)(2,1)S(1)} %get-tuple-element.98), channel_id=1, source_target_pairs={{0,128},{16,144},{32,160},{48,176},{64,192},{80,208},{96,224},{112... | collective-permute-start | bytes 245768 | tf_op jit(solution)/shard_map/ppermute | solution.py:183
  107.0 8.3 %collective-permute-start.19 = (bf16[80,512]{1,0:T(8,128)(2,1)S(1)}, bf16[80,512]{1,0:T(8,128)(2,1)S(1)}, u32[]{:S(2)}, u32[]{:S(2)}) collective-permute-start(bf16[80,512]{1,0:T(8,128)(2,1)S(1)} %get-tuple-element.99), channel_id=1, source_target_pairs={{0,64},{16,80},{32,96},{48,112},{64,128},{80,144},{96,160},{112,17... | collective-permute-start | bytes 245768 | tf_op jit(solution)/shard_map/ppermute | solution.py:183
  108.0 1.3 %copy-start = (bf16[8,512,256]{2,1,0:T(8,128)(2,1)}, bf16[8,512,256]{2,1,0:T(8,128)(2,1)S(1)}, u32[]{:S(2)}) copy-start(bf16[8,512,256]{2,1,0:T(8,128)(2,1)S(1)} %all-to-all-done.1) | copy-start | bytes 6291460
  112.7 2.5 %copy-start.4 = (bf16[80,512]{1,0:T(8,128)(2,1)}, bf16[80,512]{1,0:T(8,128)(2,1)S(1)}, u32[]{:S(2)}) copy-start(bf16[80,512]{1,0:T(8,128)(2,1)S(1)} %collective-permute-done.21.d) | copy-start | bytes 245764
  115.1 0.7 copy-start.5
  115.2 0.6 copy-start.6

commit v4 on v3

--- a/solution.py
+++ b/solution.py
@@ -214,6 +214,7 @@
         out_shape=[shape((2, tokens, cols), BF16)] * 4 + [shape((4, tokens, cols), BF16)] * 2,
         in_specs=[SMEM, VMEM, VMEM],
         out_specs=[VMEM] * 6,
+        compiler_params=pltpu.CompilerParams(vmem_limit_bytes=8 * 2**20),
         name="rotate",
     )(info, query[0], cotangent[0])
     q_in = [turned[0], along_x(turned[1], 1), None, along_x(turned[3], 3)]
@@ -284,6 +285,7 @@
         out_shape=(flat_out, flat_out),
         in_specs=[VMEM],
         out_specs=[pl.BlockSpec((64, width), lambda t: (t, 0))] * 2,
+        compiler_params=pltpu.CompilerParams(vmem_limit_bytes=6 * 2**20),
         name="spread",
     )(exchange(oc, "seq").reshape(n_seq, 2, tokens, cols))
 
@@ -302,6 +304,7 @@
         out_shape=(one, one),
         in_specs=[VMEM] * 4,
         out_specs=(VMEM, VMEM),
+        compiler_params=pltpu.CompilerParams(vmem_limit_bytes=4 * 2**20),
         name="total",
     )(pick(part, k_i, 0), *more)
     return attended[None], query_grad[None], key_grad, value_grad

time: 118 us -> 119 us (level)
  starting transfers between devices: 38.3 us -> 43.4 us
  Pallas kernels: 21.6 us -> 17.5 us
  waiting for transfers between devices: 45 us -> 46.3 us
    ppermute x22, starting transfers between devices: 26.5 us -> 30.9 us  [swap(): return lax.ppermute(x, axes, pairs)]
    pallas_call x1, Pallas kernels: 3.45 us -> 1.86 us  [body(): pl.pallas_call(spread_kernel, grid=(tokens // 64,), out_shape=(flat_out,...]
    pallas_call x1, Pallas kernels: 3.16 us -> 1.62 us  [body(): pl.pallas_call(rotate_kernel, out_shape=[shape((2, tokens, cols), BF16)]...]
    unnamed x38 -> x34, local copies, waits for them, and re-layouts: 2.77 us -> 1.38 us
    ppermute x22, waiting for transfers between devices: 45 us -> 46.3 us  [swap(): return lax.ppermute(x, axes, pairs)]
  transfers between devices with their start and end apart: 24 -> 24, of which waited for: 15 -> 13; matrix products, arithmetic and copies ran while one was open for 5% -> 4% of each run, Pallas kernels for 6% -> 3%
where the time goes in v4:
time: 119 us
  waiting for transfers between devices  46.3 us (39%)
  starting transfers between devices  43.4 us (36%)
  Pallas kernels  17.5 us (15%)
  local copies, waits for them, and re-layouts  7.23 us (6%)
  other arithmetic  3.17 us (3%)
    ppermute x22, waiting for transfers between devices, swap(): return lax.ppermute(x, axes, pairs)  46.3 us
    ppermute x22, starting transfers between devices, swap(): return lax.ppermute(x, axes, pairs)  30.9 us
    pallas_call x1, Pallas kernels, body(): pl.pallas_call(fused_kernel, out_shape=(shape((n_seq, 2 * tokens, cols),...  13.3 us
    all_to_all x2, starting transfers between devices, exchange(): lax.all_to_all(x, axes, split_axis=0, concat_axis=0, tiled=True, **kw)  12.5 us
  transfers between devices with their start and end apart: 24, of which 13 were waited for; matrix products, arithmetic and copies ran while one was open for 4% of the time, Pallas kernels for 3%

profile of v4, /device:TPU:38, one launch (start us, length us, event | category | flops | bytes accessed | tf_op | source)
XLA Modules:
  0.0 118.5 jit_solution(5260504663757432042)
XLA Ops:
  0.7 1.3 %reshape_squeeze.3 = bf16[3,8,8,2,640]{4,3,2,1,0:T(2,128)(2,1)S(1)} reshape(bf16[1,3,64,1280]{3,2,1,0:T(8,128)(2,1)} %param.9) | data formatting | bytes 983040 | tf_op jit(solution)/shard_map/reshape;squeeze | solution.py:200
  2.0 0.8 copy.20
  2.8 5.8 %all-to-all-start = ((bf16[16,24,640]{2,1,0:T(8,128)(2,1)}), bf16[16,24,640]{2,1,0:T(8,128)(2,1)}, u32[]{:S(2)}, u32[]{:S(2)}) async-start(bf16[16,24,640]{2,1,0:T(8,128)(2,1)} %bitcast.9), calls=%async_computation | async-start | bytes 983040 | tf_op jit(solution)/shard_map/all_to_all | solution.py:187
  8.7 1.6 %rotate.1 = (bf16[2,256,256]{2,1,0:T(8,128)(2,1)S(1)}, bf16[2,256,256]{2,1,0:T(8,128)(2,1)}, bf16[2,256,256]{2,1,0:T(8,128)(2,1)S(1)}, bf16[2,256,256]{2,1,0:T(8...) custom-call(s32[3]{0:T(128)S(1)} %pad_add_fusion.info, bf16[256,2048]{1,0:T(8,128)(2,1)S(1)} %bitcast.59, ...), custom_call_target="tpu_custom_call" | custom-call | tf_op jit(solution)/shard_map/rotate/pallas_call | solution.py:212
  10.3 0.7 copy-done.4
  11.0 0.2 collective-permute-start
  11.2 1.9 %collective-permute-start.1 = (bf16[2,256,256]{2,1,0:T(8,128)(2,1)}, bf16[2,256,256]{2,1,0:T(8,128)(2,1)}, u32[]{:S(2)}, u32[]{:S(2)}) collective-permute-start(bf16[2,256,256]{2,1,0:T(8,128)(2,1)} %get-tuple-element.47), channel_id=1, source_target_pairs={{0,12},{2,14},{4,0},{6,2},{8,4},{10,6},{12,8},{14,10},{1,13},{3,15... | collective-permute-start | bytes 786440 | tf_op jit(solution)/shard_map/ppermute | solution.py:183
  13.3 1.6 %collective-permute-done.2 = bf16[4,256,256]{2,1,0:T(8,128)(2,1)S(1)} collective-permute-done((bf16[4,256,256]{2,1,0:T(8,128)(2,1)S(1)}, bf16[4,256,256]{2,1,0:T(8,128)(2,1)S(1)}, u32[]{:S(2)}, u32[]{:S(2)}) %collective-permute-start.2) | collective-permute-done | bytes 524320 | tf_op jit(solution)/shard_map/ppermute | solution.py:183
  15.1 0.8 pad_maximum_fusion.3
  15.8 5.7 %collective-permute-done.refs_5_ = bf16[2,256,256]{2,1,0:T(8,128)(2,1)S(1)} collective-permute-done((bf16[2,256,256]{2,1,0:T(8,128)(2,1)}, bf16[2,256,256]{2,1,0:T(8,128)(2,1)S(1)}, u32[]{:S(2)}, u32[]{:S(2)}) %collective-permute-start) | collective-permute-done | bytes 262176 | tf_op jit(solution)/shard_map/ppermute | solution.py:183
  21.5 1.7 %gather_fusion = bf16[16,8,640]{2,1,0:T(8,128)(2,1)S(1)} fusion(bf16[48,8,640]{2,1,0:T(8,128)(2,1)} %bitcast.12, s32[1024]{0:T(1024)S(1)} %pad_clamp_fusion), kind=kCustom, calls=%fused_computation | custom fusion | bytes 327744 | tf_op jit(solution)/shard_map/jit(_take)/gather | solution.py:224
  23.4 1.6 %collective-permute-start.6 = (bf16[128,640]{1,0:T(8,128)(2,1)S(1)}, bf16[128,640]{1,0:T(8,128)(2,1)S(1)}, u32[]{:S(2)}, u32[]{:S(2)}) collective-permute-start(bf16[128,640]{1,0:T(8,128)(2,1)S(1)} %bitcast_select_fusion), channel_id=1, source_target_pairs={{0,1},{1,0},{2,3},{3,2},{4,5},{5,4},{6,7},{7,6},{8,9},{9,8},{10,11... | collective-permute-start | bytes 491528 | tf_op jit(solution)/shard_map/ppermute | solution.py:183
  24.9 2.1 %collective-permute-start.5 = (bf16[128,640]{1,0:T(8,128)(2,1)S(1)}, bf16[128,640]{1,0:T(8,128)(2,1)S(1)}, u32[]{:S(2)}, u32[]{:S(2)}) collective-permute-start(bf16[128,640]{1,0:T(8,128)(2,1)S(1)} %bitcast_select_fusion), channel_id=1, source_target_pairs={{0,8},{2,10},{4,12},{6,14},{8,0},{10,2},{12,4},{14,6},{1,9},{3,11}... | collective-permute-start | bytes 491528 | tf_op jit(solution)/shard_map/ppermute | solution.py:183
  27.0 1.2 collective-permute-start.4
  28.1 2.1 %collective-permute-start.3 = (bf16[128,640]{1,0:T(8,128)(2,1)S(1)}, bf16[128,640]{1,0:T(8,128)(2,1)S(1)}, u32[]{:S(2)}, u32[]{:S(2)}) collective-permute-start(bf16[128,640]{1,0:T(8,128)(2,1)S(1)} %bitcast_select_fusion), channel_id=1, source_target_pairs={{0,4},{2,6},{4,8},{6,10},{8,12},{10,14},{12,0},{14,2},{1,5},{3,7},... | collective-permute-start | bytes 491528 | tf_op jit(solution)/shard_map/ppermute | solution.py:183
  30.2 0.2 collective-permute-start.7
  30.5 3.1 %collective-permute-done.5 = bf16[128,640]{1,0:T(8,128)(2,1)S(1)} collective-permute-done((bf16[128,640]{1,0:T(8,128)(2,1)S(1)}, bf16[128,640]{1,0:T(8,128)(2,1)S(1)}, u32[]{:S(2)}, u32[]{:S(2)}) %collective-permute-start.5) | collective-permute-done | bytes 163872 | tf_op jit(solution)/shard_map/ppermute | solution.py:183
  33.6 3.5 %collective-permute-done.4 = bf16[128,640]{1,0:T(8,128)(2,1)S(1)} collective-permute-done((bf16[128,640]{1,0:T(8,128)(2,1)S(1)}, bf16[128,640]{1,0:T(8,128)(2,1)S(1)}, u32[]{:S(2)}, u32[]{:S(2)}) %collective-permute-start.4) | collective-permute-done | bytes 163872 | tf_op jit(solution)/shard_map/ppermute | solution.py:183
  37.1 0.6 collective-permute-start.11
  37.6 5.6 %collective-permute-start.8 = (bf16[2,256,256]{2,1,0:T(8,128)(2,1)S(1)}, bf16[2,256,256]{2,1,0:T(8,128)(2,1)S(1)}, u32[]{:S(2)}, u32[]{:S(2)}) collective-permute-start(bf16[2,256,256]{2,1,0:T(8,128)(2,1)S(1)} %get-tuple-element.65), channel_id=1, source_target_pairs={{0,4},{2,6},{4,8},{6,10},{8,12},{10,14},{12,0},{14,2},{1,5},{3,7},... | collective-permute-start | bytes 786440 | tf_op jit(solution)/shard_map/ppermute | solution.py:183
  43.3 0.9 collective-permute-start.10
  44.2 0.9 slice.47
  45.1 0.8 collective-permute-start.12
  45.9 1.3 %collective-permute-start.13 = (bf16[128,640]{1,0:T(8,128)(2,1)S(1)}, bf16[128,640]{1,0:T(8,128)(2,1)S(1)}, u32[]{:S(2)}, u32[]{:S(2)}) collective-permute-start(bf16[128,640]{1,0:T(8,128)(2,1)S(1)} %collective-permute-done.5), channel_id=1, source_target_pairs={{0,1},{1,0},{2,3},{3,2},{4,5},{5,4},{6,7},{7,6},{8,9},{9,8},{10,11... | collective-permute-start | bytes 491528 | tf_op jit(solution)/shard_map/ppermute | solution.py:183
  47.2 0.1 pad_maximum_fusion.refs_0_
  47.4 3.1 %collective-permute-done.12 = bf16[128,640]{1,0:T(8,128)(2,1)S(1)} collective-permute-done((bf16[128,640]{1,0:T(8,128)(2,1)S(1)}, bf16[128,640]{1,0:T(8,128)(2,1)S(1)}, u32[]{:S(2)}, u32[]{:S(2)}) %collective-permute-start.12) | collective-permute-done | bytes 163872 | tf_op jit(solution)/shard_map/ppermute | solution.py:183
  50.5 1.8 %collective-permute-done.13 = bf16[128,640]{1,0:T(8,128)(2,1)S(1)} collective-permute-done((bf16[128,640]{1,0:T(8,128)(2,1)S(1)}, bf16[128,640]{1,0:T(8,128)(2,1)S(1)}, u32[]{:S(2)}, u32[]{:S(2)}) %collective-permute-start.13) | collective-permute-done | bytes 163872 | tf_op jit(solution)/shard_map/ppermute | solution.py:183
  52.3 0.2 collective-permute-done.8.refs_10_
  52.4 1.2 %collective-permute-done.10.refs_12_ = bf16[2,256,256]{2,1,0:T(8,128)(2,1)S(1)} collective-permute-done((bf16[2,256,256]{2,1,0:T(8,128)(2,1)S(1)}, bf16[2,256,256]{2,1,0:T(8,128)(2,1)S(1)}, u32[]{:S(2)}, u32[]{:S(2)}) %collective-permute-start.10) | collective-permute-done | bytes 262176 | tf_op jit(solution)/shard_map/ppermute | solution.py:183
  53.9 0.5 copy-done.14
  54.5 2.4 %collective-permute-done.16.refs_8_ = bf16[4,256,256]{2,1,0:T(8,128)(2,1)} collective-permute-done((bf16[4,256,256]{2,1,0:T(8,128)(2,1)S(1)}, bf16[4,256,256]{2,1,0:T(8,128)(2,1)}, u32[]{:S(2)}, u32[]{:S(2)}) %collective-permute-start.16) | collective-permute-done | bytes 524320 | tf_op jit(solution)/shard_map/ppermute | solution.py:183
  56.8 0.7 broadcast_in_dim.23
  57.6 0.1 copy-done.11
  57.7 13.3 %fused.1 = (bf16[8,512,256]{2,1,0:T(8,128)(2,1)}, bf16[4,160,512]{2,1,0:T(8,128)(2,1)}, bf16[4,160,512]{2,1,0:T(8,128)(2,1)}) custom-call(s32[3]{0:T(128)} %copy-done.3, s32[64]{0:T(128)} %bitcast.78, f32[1,256]{1,0:T(1,128)} %bitcast.79, bf16[1280,256]{1,0:T(8,128)(2,1)} %bitcast.76, bf16[1280,256]{1,0:T(8,128)(2,1)} %bitcast.77, ...), custom_call_target="tpu_custom_call" | custom-call | flops 8589934592 | bytes 16777216 | tf_op jit(solution)/shard_map/fused/pallas_call | solution.py:243
  71.0 6.7 %all-to-all-start.1 = ((bf16[8,512,256]{2,1,0:T(8,128)(2,1)}), bf16[8,512,256]{2,1,0:T(8,128)(2,1)S(1)}, u32[]{:S(2)}, u32[]{:S(2)}) async-start(bf16[8,512,256]{2,1,0:T(8,128)(2,1)} %get-tuple-element.76), calls=%async_computation.1 | async-start | bytes 4194304 | tf_op jit(solution)/shard_map/all_to_all | solution.py:187
  77.7 0.5 collective-permute-start.17
  78.2 10.3 %collective-permute-done.17 = bf16[4,160,512]{2,1,0:T(8,128)(2,1)S(1)} collective-permute-done((bf16[4,160,512]{2,1,0:T(8,128)(2,1)}, bf16[4,160,512]{2,1,0:T(8,128)(2,1)S(1)}, u32[]{:S(2)}, u32[]{:S(2)}) %collective-permute-start.17) | collective-permute-done | bytes 655392 | tf_op jit(solution)/shard_map/ppermute | solution.py:183
  88.5 0.8 fusion.2
  89.3 2.9 %collective-permute-start.18 = (bf16[4,80,512]{2,1,0:T(8,128)(2,1)}, bf16[4,80,512]{2,1,0:T(8,128)(2,1)}, u32[]{:S(2)}, u32[]{:S(2)}) collective-permute-start(bf16[4,80,512]{2,1,0:T(8,128)(2,1)} %fusion.2), channel_id=1, source_target_pairs={{0,16},{16,0},{32,48},{48,32},{64,80},{80,64},{96,112},{112,96},{1... | collective-permute-start | bytes 983048 | tf_op jit(solution)/shard_map/ppermute | solution.py:183
  92.2 8.0 %collective-permute-done.18 = bf16[4,80,512]{2,1,0:T(8,128)(2,1)} collective-permute-done((bf16[4,80,512]{2,1,0:T(8,128)(2,1)}, bf16[4,80,512]{2,1,0:T(8,128)(2,1)}, u32[]{:S(2)}, u32[]{:S(2)}) %collective-permute-start.18) | collective-permute-done | bytes 327712 | tf_op jit(solution)/shard_map/ppermute | solution.py:183
  100.2 1.1 fusion
  101.3 6.5 %collective-permute-start.21 = (bf16[80,512]{1,0:T(8,128)(2,1)S(1)}, bf16[80,512]{1,0:T(8,128)(2,1)S(1)}, u32[]{:S(2)}, u32[]{:S(2)}) collective-permute-start(bf16[80,512]{1,0:T(8,128)(2,1)S(1)} %get-tuple-element.97), channel_id=1, source_target_pairs={{0,192},{16,208},{32,224},{48,240},{64,0},{80,16},{96,32},{112,48}... | collective-permute-start | bytes 245768 | tf_op jit(solution)/shard_map/ppermute | solution.py:183
  107.9 1.6 %collective-permute-start.20 = (bf16[80,512]{1,0:T(8,128)(2,1)S(1)}, bf16[80,512]{1,0:T(8,128)(2,1)S(1)}, u32[]{:S(2)}, u32[]{:S(2)}) collective-permute-start(bf16[80,512]{1,0:T(8,128)(2,1)S(1)} %get-tuple-element.98), channel_id=1, source_target_pairs={{0,128},{16,144},{32,160},{48,176},{64,192},{80,208},{96,224},{112... | collective-permute-start | bytes 245768 | tf_op jit(solution)/shard_map/ppermute | solution.py:183
  109.5 1.0 collective-permute-start.19
  110.5 1.9 %spread.1 = (bf16[256,2048]{1,0:T(8,128)(2,1)}, bf16[256,2048]{1,0:T(8,128)(2,1)}) custom-call(bf16[8,2,256,256]{3,2,1,0:T(8,128)(2,1)S(1)} %bitcast.58), custom_call_target="tpu_custom_call" | custom-call | tf_op jit(solution)/shard_map/spread/pallas_call | solution.py:282
  112.3 5.2 %collective-permute-done.20.c = bf16[80,512]{1,0:T(8,128)(2,1)S(1)} collective-permute-done((bf16[80,512]{1,0:T(8,128)(2,1)S(1)}, bf16[80,512]{1,0:T(8,128)(2,1)S(1)}, u32[]{:S(2)}, u32[]{:S(2)}) %collective-permute-start.20) | collective-permute-done | bytes 81952 | tf_op jit(solution)/shard_map/ppermute | solution.py:183
  117.5 0.3 collective-permute-done.19.b
  117.8 0.7 total.1
  (64 shorter events, 1.0 us)
Async XLA Ops:
  0.6 8.0 %copy-start.1 = (bf16[1,256,2048]{2,1,0:T(8,128)(2,1)S(1)}, bf16[1,256,2048]{2,1,0:T(8,128)(2,1)}, u32[]{:S(2)}) copy-start(bf16[1,256,2048]{2,1,0:T(8,128)(2,1)} %param.15) | copy-start | bytes 3145732
  0.6 8.0 %copy-start = (bf16[1,256,2048]{2,1,0:T(8,128)(2,1)S(1)}, bf16[1,256,2048]{2,1,0:T(8,128)(2,1)}, u32[]{:S(2)}) copy-start(bf16[1,256,2048]{2,1,0:T(8,128)(2,1)} %param.8) | copy-start | bytes 3145732
  1.9 11.1 %copy-start.15 = (s32[1,16]{1,0:T(1,128)S(1)}, s32[1,16]{1,0:T(1,128)}, u32[]{:S(2)}) copy-start(s32[1,16]{1,0:T(1,128)} %param.10) | copy-start | bytes 196
  2.8 18.8 %all-to-all-start = ((bf16[16,24,640]{2,1,0:T(8,128)(2,1)}), bf16[16,24,640]{2,1,0:T(8,128)(2,1)}, u32[]{:S(2)}, u32[]{:S(2)}) async-start(bf16[16,24,640]{2,1,0:T(8,128)(2,1)} %bitcast.9), calls=%async_computation | async-start | bytes 983040 | tf_op jit(solution)/shard_map/all_to_all | solution.py:187
  8.7 6.3 %copy-start.3 = (s32[3]{0:T(128)}, s32[3]{0:T(128)S(1)}, u32[]{:S(2)}) copy-start(s32[3]{0:T(128)S(1)} %pad_add_fusion.info) | copy-start | bytes 40
  10.3 0.7 copy-start.4
  11.0 33.1 %copy-start.2 = (bf16[2,256,256]{2,1,0:T(8,128)(2,1)}, bf16[2,256,256]{2,1,0:T(8,128)(2,1)S(1)}, u32[]{:S(2)}) copy-start(bf16[2,256,256]{2,1,0:T(8,128)(2,1)S(1)} %get-tuple-element.61.refs_4_) | copy-start | bytes 786436
  11.0 10.5 %collective-permute-start = (bf16[2,256,256]{2,1,0:T(8,128)(2,1)}, bf16[2,256,256]{2,1,0:T(8,128)(2,1)S(1)}, u32[]{:S(2)}, u32[]{:S(2)}) collective-permute-start(bf16[2,256,256]{2,1,0:T(8,128)(2,1)} %get-tuple-element.46), channel_id=1, source_target_pairs={{0,4},{2,6},{4,8},{6,10},{8,12},{10,14},{12,0},{14,2},{1,5},{3,7},... | collective-permute-start | bytes 786440 | tf_op jit(solution)/shard_map/ppermute | solution.py:183
  11.2 10.3 %collective-permute-start.1 = (bf16[2,256,256]{2,1,0:T(8,128)(2,1)}, bf16[2,256,256]{2,1,0:T(8,128)(2,1)}, u32[]{:S(2)}, u32[]{:S(2)}) collective-permute-start(bf16[2,256,256]{2,1,0:T(8,128)(2,1)} %get-tuple-element.47), channel_id=1, source_target_pairs={{0,12},{2,14},{4,0},{6,2},{8,4},{10,6},{12,8},{14,10},{1,13},{3,15... | collective-permute-start | bytes 786440 | tf_op jit(solution)/shard_map/ppermute | solution.py:183
  13.1 1.9 %collective-permute-start.2 = (bf16[4,256,256]{2,1,0:T(8,128)(2,1)S(1)}, bf16[4,256,256]{2,1,0:T(8,128)(2,1)S(1)}, u32[]{:S(2)}, u32[]{:S(2)}) collective-permute-start(bf16[4,256,256]{2,1,0:T(8,128)(2,1)S(1)} %get-tuple-element.49), channel_id=1, source_target_pairs={{0,2},{2,0},{4,6},{6,4},{8,10},{10,8},{12,14},{14,12},{1,3},{3,1},... | collective-permute-start | bytes 1572872 | tf_op jit(solution)/shard_map/ppermute | solution.py:183
  13.3 16.9 %copy-start.5 = (bf16[2,256,256]{2,1,0:T(8,128)(2,1)S(1)}, bf16[2,256,256]{2,1,0:T(8,128)(2,1)}, u32[]{:S(2)}) copy-start(bf16[2,256,256]{2,1,0:T(8,128)(2,1)} %copy-done.4) | copy-start | bytes 786436
  21.5 25.8 %copy-start.9 = (bf16[2,256,256]{2,1,0:T(8,128)(2,1)}, bf16[2,256,256]{2,1,0:T(8,128)(2,1)S(1)}, u32[]{:S(2)}) copy-start(bf16[2,256,256]{2,1,0:T(8,128)(2,1)S(1)} %collective-permute-done.refs_5_) | copy-start | bytes 786436
  23.4 7.1 %collective-permute-start.6 = (bf16[128,640]{1,0:T(8,128)(2,1)S(1)}, bf16[128,640]{1,0:T(8,128)(2,1)S(1)}, u32[]{:S(2)}, u32[]{:S(2)}) collective-permute-start(bf16[128,640]{1,0:T(8,128)(2,1)S(1)} %bitcast_select_fusion), channel_id=1, source_target_pairs={{0,1},{1,0},{2,3},{3,2},{4,5},{5,4},{6,7},{7,6},{8,9},{9,8},{10,11... | collective-permute-start | bytes 491528 | tf_op jit(solution)/shard_map/ppermute | solution.py:183
  24.9 8.6 %collective-permute-start.5 = (bf16[128,640]{1,0:T(8,128)(2,1)S(1)}, bf16[128,640]{1,0:T(8,128)(2,1)S(1)}, u32[]{:S(2)}, u32[]{:S(2)}) collective-permute-start(bf16[128,640]{1,0:T(8,128)(2,1)S(1)} %bitcast_select_fusion), channel_id=1, source_target_pairs={{0,8},{2,10},{4,12},{6,14},{8,0},{10,2},{12,4},{14,6},{1,9},{3,11}... | collective-permute-start | bytes 491528 | tf_op jit(solution)/shard_map/ppermute | solution.py:183
  27.0 10.1 %collective-permute-start.4 = (bf16[128,640]{1,0:T(8,128)(2,1)S(1)}, bf16[128,640]{1,0:T(8,128)(2,1)S(1)}, u32[]{:S(2)}, u32[]{:S(2)}) collective-permute-start(bf16[128,640]{1,0:T(8,128)(2,1)S(1)} %bitcast_select_fusion), channel_id=1, source_target_pairs={{0,12},{2,14},{4,0},{6,2},{8,4},{10,6},{12,8},{14,10},{1,13},{3,15... | collective-permute-start | bytes 491528 | tf_op jit(solution)/shard_map/ppermute | solution.py:183
  28.1 8.9 %collective-permute-start.3 = (bf16[128,640]{1,0:T(8,128)(2,1)S(1)}, bf16[128,640]{1,0:T(8,128)(2,1)S(1)}, u32[]{:S(2)}, u32[]{:S(2)}) collective-permute-start(bf16[128,640]{1,0:T(8,128)(2,1)S(1)} %bitcast_select_fusion), channel_id=1, source_target_pairs={{0,4},{2,6},{4,8},{6,10},{8,12},{10,14},{12,0},{14,2},{1,5},{3,7},... | collective-permute-start | bytes 491528 | tf_op jit(solution)/shard_map/ppermute | solution.py:183
  30.2 14.9 %collective-permute-start.7 = (bf16[2,256,256]{2,1,0:T(8,128)(2,1)S(1)}, bf16[2,256,256]{2,1,0:T(8,128)(2,1)S(1)}, u32[]{:S(2)}, u32[]{:S(2)}) collective-permute-start(bf16[2,256,256]{2,1,0:T(8,128)(2,1)S(1)} %copy-done.5), channel_id=1, source_target_pairs={{0,8},{2,10},{4,12},{6,14},{8,0},{10,2},{12,4},{14,6},{1,9},{3,11}... | collective-permute-start | bytes 786440 | tf_op jit(solution)/shard_map/ppermute | solution.py:183
  37.1 8.8 %collective-permute-start.11 = (bf16[128,640]{1,0:T(8,128)(2,1)S(1)}, bf16[128,640]{1,0:T(8,128)(2,1)S(1)}, u32[]{:S(2)}, u32[]{:S(2)}) collective-permute-start(bf16[128,640]{1,0:T(8,128)(2,1)S(1)} %collective-permute-done.3), channel_id=1, source_target_pairs={{0,1},{1,0},{2,3},{3,2},{4,5},{5,4},{6,7},{7,6},{8,9},{9,8},{10,11... | collective-permute-start | bytes 491528 | tf_op jit(solution)/shard_map/ppermute | solution.py:183
  37.6 14.8 %collective-permute-start.8 = (bf16[2,256,256]{2,1,0:T(8,128)(2,1)S(1)}, bf16[2,256,256]{2,1,0:T(8,128)(2,1)S(1)}, u32[]{:S(2)}, u32[]{:S(2)}) collective-permute-start(bf16[2,256,256]{2,1,0:T(8,128)(2,1)S(1)} %get-tuple-element.65), channel_id=1, source_target_pairs={{0,4},{2,6},{4,8},{6,10},{8,12},{10,14},{12,0},{14,2},{1,5},{3,7},... | collective-permute-start | bytes 786440 | tf_op jit(solution)/shard_map/ppermute | solution.py:183
  43.2 9.2 %collective-permute-start.9 = (bf16[2,256,256]{2,1,0:T(8,128)(2,1)S(1)}, bf16[2,256,256]{2,1,0:T(8,128)(2,1)S(1)}, u32[]{:S(2)}, u32[]{:S(2)}) collective-permute-start(bf16[2,256,256]{2,1,0:T(8,128)(2,1)S(1)} %get-tuple-element.66), channel_id=1, source_target_pairs={{0,8},{2,10},{4,12},{6,14},{8,0},{10,2},{12,4},{14,6},{1,9},{3,11}... | collective-permute-start | bytes 786440 | tf_op jit(solution)/shard_map/ppermute | solution.py:183
  43.3 10.4 %collective-permute-start.10 = (bf16[2,256,256]{2,1,0:T(8,128)(2,1)S(1)}, bf16[2,256,256]{2,1,0:T(8,128)(2,1)S(1)}, u32[]{:S(2)}, u32[]{:S(2)}) collective-permute-start(bf16[2,256,256]{2,1,0:T(8,128)(2,1)S(1)} %get-tuple-element.67), channel_id=1, source_target_pairs={{0,12},{2,14},{4,0},{6,2},{8,4},{10,6},{12,8},{14,10},{1,13},{3,15... | collective-permute-start | bytes 786440 | tf_op jit(solution)/shard_map/ppermute | solution.py:183
  44.1 10.2 %copy-start.16 = (f32[16]{0:T(128)S(1)}, f32[16]{0:T(128)}, u32[]{:S(2)}) copy-start(f32[16]{0:T(128)} %param.14) | copy-start | bytes 196
  45.1 12.5 %copy-start.10 = (bf16[2,256,256]{2,1,0:T(8,128)(2,1)}, bf16[2,256,256]{2,1,0:T(8,128)(2,1)S(1)}, u32[]{:S(2)}) copy-start(bf16[2,256,256]{2,1,0:T(8,128)(2,1)S(1)} %collective-permute-done.7.refs_6_) | copy-start | bytes 786436
  45.1 5.4 %collective-permute-start.12 = (bf16[128,640]{1,0:T(8,128)(2,1)S(1)}, bf16[128,640]{1,0:T(8,128)(2,1)S(1)}, u32[]{:S(2)}, u32[]{:S(2)}) collective-permute-start(bf16[128,640]{1,0:T(8,128)(2,1)S(1)} %collective-permute-done.4), channel_id=1, source_target_pairs={{0,1},{1,0},{2,3},{3,2},{4,5},{5,4},{6,7},{7,6},{8,9},{9,8},{10,11... | collective-permute-start | bytes 491528 | tf_op jit(solution)/shard_map/ppermute | solution.py:183
  45.9 6.4 %collective-permute-start.13 = (bf16[128,640]{1,0:T(8,128)(2,1)S(1)}, bf16[128,640]{1,0:T(8,128)(2,1)S(1)}, u32[]{:S(2)}, u32[]{:S(2)}) collective-permute-start(bf16[128,640]{1,0:T(8,128)(2,1)S(1)} %collective-permute-done.5), channel_id=1, source_target_pairs={{0,1},{1,0},{2,3},{3,2},{4,5},{5,4},{6,7},{7,6},{8,9},{9,8},{10,11... | collective-permute-start | bytes 491528 | tf_op jit(solution)/shard_map/ppermute | solution.py:183
  47.3 10.2 %copy-start.7 = (bf16[4,128,640]{2,1,0:T(8,128)(2,1)}, bf16[4,128,640]{2,1,0:T(8,128)(2,1)S(1)}, u32[]{:S(2)}) copy-start(bf16[4,128,640]{2,1,0:T(8,128)(2,1)S(1)} %pad_maximum_fusion.refs_0_) | copy-start | bytes 1966084
  50.5 4.0 %collective-permute-start.14 = (bf16[4,128,640]{2,1,0:T(8,128)(2,1)S(1)}, bf16[4,128,640]{2,1,0:T(8,128)(2,1)}, u32[]{:S(2)}, u32[]{:S(2)}) collective-permute-start(bf16[4,128,640]{2,1,0:T(8,128)(2,1)S(1)} %pad_maximum_fusion.refs_0_), channel_id=1, source_target_pairs={{0,2},{2,0},{4,6},{6,4},{8,10},{10,8},{12,14},{14,12},{1,3},{3,1},... | collective-permute-start | bytes 1966088 | tf_op jit(solution)/shard_map/ppermute | solution.py:183
  52.4 1.3 %copy-start.12 = (bf16[2,256,256]{2,1,0:T(8,128)(2,1)}, bf16[2,256,256]{2,1,0:T(8,128)(2,1)S(1)}, u32[]{:S(2)}) copy-start(bf16[2,256,256]{2,1,0:T(8,128)(2,1)S(1)} %collective-permute-done.8.refs_10_) | copy-start | bytes 786436
  52.4 1.4 %copy-start.13 = (bf16[2,256,256]{2,1,0:T(8,128)(2,1)}, bf16[2,256,256]{2,1,0:T(8,128)(2,1)S(1)}, u32[]{:S(2)}) copy-start(bf16[2,256,256]{2,1,0:T(8,128)(2,1)S(1)} %collective-permute-done.9.refs_11_) | copy-start | bytes 786436
  53.6 0.7 copy-start.14
  53.8 3.8 %copy-start.8 = (bf16[4,128,640]{2,1,0:T(8,128)(2,1)}, bf16[4,128,640]{2,1,0:T(8,128)(2,1)S(1)}, u32[]{:S(2)}) copy-start(bf16[4,128,640]{2,1,0:T(8,128)(2,1)S(1)} %pad_maximum_fusion.1.refs_1_) | copy-start | bytes 1966084
  53.8 3.1 %collective-permute-start.15 = (bf16[4,128,640]{2,1,0:T(8,128)(2,1)S(1)}, bf16[4,128,640]{2,1,0:T(8,128)(2,1)S(1)}, u32[]{:S(2)}, u32[]{:S(2)}) collective-permute-start(bf16[4,128,640]{2,1,0:T(8,128)(2,1)S(1)} %pad_maximum_fusion.1.refs_1_), channel_id=1, source_target_pairs={{0,2},{2,0},{4,6},{6,4},{8,10},{10,8},{12,14},{14,12},{1,3},{3,1},... | collective-permute-start | bytes 1966088 | tf_op jit(solution)/shard_map/ppermute | solution.py:183
  54.4 2.5 %collective-permute-start.16 = (bf16[4,256,256]{2,1,0:T(8,128)(2,1)S(1)}, bf16[4,256,256]{2,1,0:T(8,128)(2,1)}, u32[]{:S(2)}, u32[]{:S(2)}) collective-permute-start(bf16[4,256,256]{2,1,0:T(8,128)(2,1)S(1)} %pad_maximum_fusion.2), channel_id=1, source_target_pairs={{0,2},{2,0},{4,6},{6,4},{8,10},{10,8},{12,14},{14,12},{1,3},{3,1},... | collective-permute-start | bytes 1572872 | tf_op jit(solution)/shard_map/ppermute | solution.py:183
  56.8 0.8 copy-start.11
  71.0 17.5 %copy-start.6 = (bf16[4,160,512]{2,1,0:T(8,128)(2,1)S(1)}, bf16[4,160,512]{2,1,0:T(8,128)(2,1)}, u32[]{:S(2)}) copy-start(bf16[4,160,512]{2,1,0:T(8,128)(2,1)} %get-tuple-element.79) | copy-start | bytes 1966084
  71.0 39.4 %all-to-all-start.1 = ((bf16[8,512,256]{2,1,0:T(8,128)(2,1)}), bf16[8,512,256]{2,1,0:T(8,128)(2,1)S(1)}, u32[]{:S(2)}, u32[]{:S(2)}) async-start(bf16[8,512,256]{2,1,0:T(8,128)(2,1)} %get-tuple-element.76), calls=%async_computation.1 | async-start | bytes 4194304 | tf_op jit(solution)/shard_map/all_to_all | solution.py:187
  77.7 10.8 %collective-permute-start.17 = (bf16[4,160,512]{2,1,0:T(8,128)(2,1)}, bf16[4,160,512]{2,1,0:T(8,128)(2,1)S(1)}, u32[]{:S(2)}, u32[]{:S(2)}) collective-permute-start(bf16[4,160,512]{2,1,0:T(8,128)(2,1)} %get-tuple-element.80), channel_id=1, source_target_pairs={{0,32},{2,226},{4,36},{6,230},{8,40},{10,234},{12,44},{14,238},{16... | collective-permute-start | bytes 1966088 | tf_op jit(solution)/shard_map/ppermute | solution.py:183
  89.3 10.9 %collective-permute-start.18 = (bf16[4,80,512]{2,1,0:T(8,128)(2,1)}, bf16[4,80,512]{2,1,0:T(8,128)(2,1)}, u32[]{:S(2)}, u32[]{:S(2)}) collective-permute-start(bf16[4,80,512]{2,1,0:T(8,128)(2,1)} %fusion.2), channel_id=1, source_target_pairs={{0,16},{16,0},{32,48},{48,32},{64,80},{80,64},{96,112},{112,96},{1... | collective-permute-start | bytes 983048 | tf_op jit(solution)/shard_map/ppermute | solution.py:183
  101.3 11.0 %collective-permute-start.21 = (bf16[80,512]{1,0:T(8,128)(2,1)S(1)}, bf16[80,512]{1,0:T(8,128)(2,1)S(1)}, u32[]{:S(2)}, u32[]{:S(2)}) collective-permute-start(bf16[80,512]{1,0:T(8,128)(2,1)S(1)} %get-tuple-element.97), channel_id=1, source_target_pairs={{0,192},{16,208},{32,224},{48,240},{64,0},{80,16},{96,32},{112,48}... | collective-permute-start | bytes 245768 | tf_op jit(solution)/shard_map/ppermute | solution.py:183
  107.9 9.7 %collective-permute-start.20 = (bf16[80,512]{1,0:T(8,128)(2,1)S(1)}, bf16[80,512]{1,0:T(8,128)(2,1)S(1)}, u32[]{:S(2)}, u32[]{:S(2)}) collective-permute-start(bf16[80,512]{1,0:T(8,128)(2,1)S(1)} %get-tuple-element.98), channel_id=1, source_target_pairs={{0,128},{16,144},{32,160},{48,176},{64,192},{80,208},{96,224},{112... | collective-permute-start | bytes 245768 | tf_op jit(solution)/shard_map/ppermute | solution.py:183
  109.5 8.3 %collective-permute-start.19 = (bf16[80,512]{1,0:T(8,128)(2,1)S(1)}, bf16[80,512]{1,0:T(8,128)(2,1)S(1)}, u32[]{:S(2)}, u32[]{:S(2)}) collective-permute-start(bf16[80,512]{1,0:T(8,128)(2,1)S(1)} %get-tuple-element.99), channel_id=1, source_target_pairs={{0,64},{16,80},{32,96},{48,112},{64,128},{80,144},{96,160},{112,17... | collective-permute-start | bytes 245768 | tf_op jit(solution)/shard_map/ppermute | solution.py:183
